TPU v7x, 32 devices: a whole 2x2x4 slice. The times are simulated.
32 devices in a mesh: dp: 4 (over y, core), row: 2 (over x), col: 4 (over z).
Axes of the slice: x: 2, y: 2, z: 4, core: 2. Of those that a mesh axis runs over, the one named last changes fastest.
Arguments:
- tokens: bfloat16 [8192, 1536], P(('dp', 'row', 'col')), may hold values from -6 to 6
- cotangent: bfloat16 [8192, 1536], P(('dp', 'row', 'col')), may hold values from -6 to 6
- seq_lengths: int32 [8, 4], P('dp'), may hold values from 1 to 682, 1024 in all within a row
- token_order: int32 [8192], replicated, may hold values from 0 to 8191, as said below
- norm_in: bfloat16 [1536], replicated, may hold values from 0.5 to 1.5
- w_gate: bfloat16 [1536, 3072], P('dp', ('row', 'col')), may hold values from -0.15625 to 0.15625
- w_value: bfloat16 [1536, 3072], P('dp', ('row', 'col')), may hold values from -0.15625 to 0.15625
- w_pair: bfloat16 [1536, 256], P('dp', ('row', 'col')), may hold values from -0.15625 to 0.15625
- w_step: bfloat16 [1536, 48], P('dp', ('row', 'col')), may hold values from -0.15625 to 0.15625
- conv_value: float32 [4, 3072], P(None, ('row', 'col')), may hold values from -3 to 3
- bias_value: float32 [3072], P(('row', 'col')), may hold values from -3 to 3
- conv_pair: float32 [4, 256], P(None, ('row', 'col')), may hold values from -3 to 3
- bias_pair: float32 [256], P(('row', 'col')), may hold values from -3 to 3
- step_bias: float32 [48], P(('row', 'col')), may hold values from -4 to -1
- decay_log: float32 [48], P(('row', 'col')), may hold values from 0 to 2.5
- skip_gain: float32 [48], P(('row', 'col')), may hold values from 0.5 to 1.5
- norm_gate: float32 [3072], P(('row', 'col')), may hold values from 0.5 to 1.5
- w_out: bfloat16 [3072, 1536], P(('row', 'col'), 'dp'), may hold values from -0.109375 to 0.109375
Outputs:
- block_out: bfloat16 [8192, 1536], P(('dp', 'row', 'col'))
- grad_tokens: bfloat16 [8192, 1536], P(('dp', 'row', 'col'))
- grad_norm_in: float32 [1536], replicated
- grad_w_gate: float32 [1536, 3072], P('dp', ('row', 'col'))
- grad_w_value: float32 [1536, 3072], P('dp', ('row', 'col'))
- grad_w_pair: float32 [1536, 256], P('dp', ('row', 'col'))
- grad_w_step: float32 [1536, 48], P('dp', ('row', 'col'))
- grad_conv_value: float32 [4, 3072], P(None, ('row', 'col'))
- grad_bias_value: float32 [3072], P(('row', 'col'))
- grad_conv_pair: float32 [4, 256], P(None, ('row', 'col'))
- grad_bias_pair: float32 [256], P(('row', 'col'))
- grad_step_bias: float32 [48], P(('row', 'col'))
- grad_decay_log: float32 [48], P(('row', 'col'))
- grad_skip_gain: float32 [48], P(('row', 'col'))
- grad_norm_gate: float32 [3072], P(('row', 'col'))
- grad_w_out: float32 [3072, 1536], P(('row', 'col'), 'dp')
Inputs may be any that keep to these rules, and one draw needn't show every extreme that they name: token_order is a permutation. Cut the natural positions into 32 blocks of 256 in order, block index g * 2 * 4 + r. Let the dealt set (g, r) be the dealt positions g * 2048 + b * 1024 + r * 128 + u, for b < 2 and u < 128. Every natural block (g, r) sends exactly 64 tokens into each dealt set (g2, r), for every g2. `seq_lengths`: row b holds micro-batch b of token group b // 2; each row sums to 1024, its largest entry is 682, and its last entry counts padding tokens.
All inputs are finite; a program needn't handle non-finite values.
Results may differ from a plain program's by a relative error of at most 0.018.
Values may be sent and summed in bfloat16 or wider, within the bound.
No kernel may reach another device: no remote copies, remote signals or barrier semaphores. Data moves between devices by JAX's collectives and lax.ppermute only.
A program may use at most 192 MiB of HBM per device.

v0:
```python
from functools import partial
from functools import reduce

import jax
import jax.numpy as jnp
from jax import lax
from jax.sharding import PartitionSpec as P

SPAN = 256


EPS = 1e-05
PRECISE = lax.Precision.HIGHEST


def segment_ids(lengths_row, count):
    bounds = jnp.cumsum(lengths_row)
    places = jnp.arange(count, dtype=jnp.int32)
    return jnp.sum((places[:, None] >= bounds[None, :]).astype(jnp.int32), axis=1)


def causal_conv(values, kernel, offset, segment):
    tap_count = kernel.shape[0]
    length = values.shape[0]
    padded = jnp.concatenate(
        [jnp.zeros((tap_count - 1, values.shape[1]), jnp.float32), values], axis=0
    )
    seg_pad = jnp.concatenate([jnp.full((tap_count - 1,), -1, jnp.int32), segment])
    result = jnp.zeros_like(values) + offset[None, :]
    for tap_index in range(tap_count):
        same_seg = (seg_pad[tap_index : tap_index + length] == segment).astype(jnp.float32)
        result = (
            result
            + padded[tap_index : tap_index + length]
            * kernel[tap_index][None, :]
            * same_seg[:, None]
        )
    return result


def conv_silu(values, kernel, offset, segment):
    return jax.nn.silu(causal_conv(values, kernel, offset, segment))


def softplus_shift(step_proj, step_bias):
    return jax.nn.softplus(step_proj + step_bias[None, :])


def silu_slope(values):
    sigmoid_val = jax.nn.sigmoid(values)
    return sigmoid_val * (1.0 + values * (1.0 - sigmoid_val))


def ssd_scan(values, steps_in, decay_rates, keys_in, reads_in, segment, span_len):
    length, head_count, head_width = values.shape
    block_count = length // span_len
    blocks = (
        values.reshape(block_count, span_len, head_count, head_width),
        steps_in.reshape(block_count, span_len, head_count),
        keys_in.reshape(block_count, span_len, keys_in.shape[1]),
        reads_in.reshape(block_count, span_len, reads_in.shape[1]),
        segment.reshape(block_count, span_len),
    )
    places = jnp.arange(span_len, dtype=jnp.int32)
    causal = places[:, None] >= places[None, :]

    def one_block(carry, block):
        carry_state, last_seg = carry
        block_values, block_steps, block_keys, block_reads, block_seg = block
        log_decay = jnp.cumsum(block_steps * decay_rates[None, :], axis=0)
        allowed = (causal & (block_seg[:, None] == block_seg[None, :])).astype(jnp.float32)
        gap_logs = log_decay[:, None, :] - log_decay[None, :, :]
        decay_grid = (
            jnp.exp(jnp.where(allowed[:, :, None] > 0.5, gap_logs, 0.0)) * allowed[:, :, None]
        )
        scores = jnp.dot(block_reads, block_keys.T, precision=PRECISE)
        mix_grid = scores[:, :, None] * decay_grid * block_steps[None, :, :]
        inside = jnp.einsum("tsh,shp->thp", mix_grid, block_values, precision=PRECISE)
        carried = (block_seg == last_seg).astype(jnp.float32)
        reach_now = jnp.exp(log_decay) * carried[:, None]
        outside = (
            jnp.einsum("tn,hpn->thp", block_reads, carry_state, precision=PRECISE)
            * reach_now[:, :, None]
        )
        end_same = (block_seg == block_seg[-1]).astype(jnp.float32)
        tail_weight = jnp.exp(log_decay[-1][None, :] - log_decay) * block_steps * end_same[:, None]
        fresh_state = jnp.einsum(
            "sh,shp,sn->hpn", tail_weight, block_values, block_keys, precision=PRECISE
        )
        kept_state = (
            carry_state * (jnp.exp(log_decay[-1]) * carried[-1])[:, None, None] + fresh_state
        )
        return ((kept_state, block_seg[-1]), inside + outside)

    start_carry = (
        jnp.zeros((head_count, head_width, keys_in.shape[1]), jnp.float32),
        jnp.int32(-1),
    )
    final_carry, outputs = lax.scan(jax.checkpoint(one_block), start_carry, blocks)
    return outputs.reshape(length, head_count, head_width)


def mixer_local(mixed_in, steps_in, decay_log, shared, skip_gain, segment, head_count):
    length = mixed_in.shape[0]
    shaped = mixed_in.reshape(length, head_count, mixed_in.shape[1] // head_count)
    half_width = shared.shape[1] // 2
    scanned = ssd_scan(
        shaped,
        steps_in,
        -jnp.exp(decay_log),
        shared[:, :half_width],
        shared[:, half_width:],
        segment,
        SPAN,
    )
    return (scanned + skip_gain[None, :, None] * shaped).reshape(length, mixed_in.shape[1])


def fetch_weights(w_gate, w_value, w_pair, w_step, w_out):
    return (
        lax.all_gather(w_gate, "dp", axis=0, tiled=True),
        lax.all_gather(w_value, "dp", axis=0, tiled=True),
        lax.all_gather(w_pair, "dp", axis=0, tiled=True),
        lax.all_gather(w_step, "dp", axis=0, tiled=True),
        lax.all_gather(w_out, "dp", axis=1, tiled=True),
    )


def reduce_weights(grad_gate, grad_value, grad_pair, grad_step, grad_out):
    return (
        lax.psum_scatter(
            grad_gate.astype(jnp.bfloat16), "dp", scatter_dimension=0, tiled=True
        ).astype(jnp.float32),
        lax.psum_scatter(
            grad_value.astype(jnp.bfloat16), "dp", scatter_dimension=0, tiled=True
        ).astype(jnp.float32),
        lax.psum_scatter(
            grad_pair.astype(jnp.bfloat16), "dp", scatter_dimension=0, tiled=True
        ).astype(jnp.float32),
        lax.psum_scatter(
            grad_step.astype(jnp.bfloat16), "dp", scatter_dimension=0, tiled=True
        ).astype(jnp.float32),
        lax.psum_scatter(
            grad_out.astype(jnp.bfloat16), "dp", scatter_dimension=1, tiled=True
        ).astype(jnp.float32),
    )


def add_trees(first_tree, second_tree):
    return jax.tree.map(jnp.add, first_tree, second_tree)


def per_device(
    tokens,
    cotangent,
    seq_lengths,
    token_order,
    norm_in,
    w_gate,
    w_value,
    w_pair,
    w_step,
    conv_value,
    bias_value,
    conv_pair,
    bias_pair,
    step_bias,
    decay_log,
    skip_gain,
    norm_gate,
    w_out,
):
    group_count = lax.axis_size("dp")
    team_size = lax.axis_size(("row", "col"))
    share_len = tokens.shape[0]
    quota_len = share_len // group_count
    micro_count = seq_lengths.shape[0]
    piece_len = share_len // micro_count
    block_len = piece_len * team_size
    group_len = share_len * team_size
    width_full = tokens.shape[1]
    inner_full = norm_gate.shape[0] * team_size
    head_count = step_bias.shape[0]
    my_index = lax.axis_index("dp")
    my_team = lax.axis_index(("row", "col"))
    all_count = token_order.shape[0]
    positions = jnp.arange(all_count, dtype=jnp.int32)
    inverse = jnp.zeros((all_count,), jnp.int32).at[token_order].set(positions)
    own_start = (my_index * team_size + my_team) * share_len
    own_inverse = lax.dynamic_slice_in_dim(inverse, own_start, share_len)
    listing = jnp.arange(share_len, dtype=jnp.int32)
    send_key = own_inverse // group_len * share_len + listing
    send_order = jnp.argsort(send_key)
    send_rank = jnp.argsort(send_order)
    dealt_places = (
        my_index * group_len
        + listing // piece_len * block_len
        + my_team * piece_len
        + listing % piece_len
    )
    own_order = token_order[dealt_places]
    recv_order = jnp.argsort(own_order)
    recv_rank = jnp.argsort(recv_order)
    arrived = (
        lax.all_to_all(
            tokens[send_order].reshape(group_count, quota_len, width_full),
            "dp",
            split_axis=0,
            concat_axis=0,
            tiled=True,
        ),
        lax.all_to_all(
            cotangent[send_order].reshape(group_count, quota_len, width_full),
            "dp",
            split_axis=0,
            concat_axis=0,
            tiled=True,
        ),
    )
    dealt_in = arrived[0].reshape(share_len, width_full)[recv_rank]
    dealt_back = arrived[1].reshape(share_len, width_full)[recv_rank]
    norm_in_f = norm_in.astype(jnp.float32)
    g_norm_in = jnp.zeros(norm_in.shape, jnp.float32)
    g_conv_value = jnp.zeros(conv_value.shape, jnp.float32)
    g_bias_value = jnp.zeros(bias_value.shape, jnp.float32)
    g_conv_pair = jnp.zeros(conv_pair.shape, jnp.float32)
    g_bias_pair = jnp.zeros(bias_pair.shape, jnp.float32)
    g_step_bias = jnp.zeros(step_bias.shape, jnp.float32)
    g_decay = jnp.zeros(decay_log.shape, jnp.float32)
    g_skip = jnp.zeros(skip_gain.shape, jnp.float32)
    g_norm_gate = jnp.zeros(norm_gate.shape, jnp.float32)
    out_blocks = []
    back_blocks = []
    local_terms = []
    for micro_index in range(micro_count):
        first_row = micro_index * piece_len
        gate_w, value_w, pair_w, step_w, out_w = fetch_weights(
            w_gate, w_value, w_pair, w_step, w_out
        )
        row_local = dealt_in[first_row : first_row + piece_len]
        back_local = dealt_back[first_row : first_row + piece_len]
        segment = segment_ids(seq_lengths[micro_index], block_len)
        live_mask = (segment < seq_lengths.shape[1] - 1).astype(jnp.float32)
        live_local = lax.dynamic_slice_in_dim(live_mask, my_team * piece_len, piece_len)
        full_rows = lax.all_gather(row_local, ("row", "col"), axis=0, tiled=True)
        rows_f = full_rows.astype(jnp.float32)
        rms_scale = lax.rsqrt(jnp.mean(rows_f * rows_f, axis=1, keepdims=True) + EPS)
        rms_local = lax.dynamic_slice_in_dim(rms_scale, my_team * piece_len, piece_len)
        normed = (rows_f * rms_scale * norm_in_f[None, :]).astype(jnp.bfloat16)
        gate_proj = jnp.dot(normed, gate_w, preferred_element_type=jnp.float32)
        value_proj = jnp.dot(normed, value_w, preferred_element_type=jnp.float32)
        pair_proj = jnp.dot(normed, pair_w, preferred_element_type=jnp.float32)
        step_proj = jnp.dot(normed, step_w, preferred_element_type=jnp.float32)
        mixed_in, value_pull = jax.vjp(
            partial(conv_silu, segment=segment), value_proj, conv_value, bias_value
        )
        shared_local, pair_pull = jax.vjp(
            partial(conv_silu, segment=segment), pair_proj, conv_pair, bias_pair
        )
        shared = lax.all_gather(
            shared_local.astype(jnp.bfloat16), ("row", "col"), axis=1, tiled=True
        ).astype(jnp.float32)
        steps, step_pull = jax.vjp(softplus_shift, step_proj, step_bias)
        scanned, mixer_pull = jax.vjp(
            partial(mixer_local, segment=segment, head_count=head_count),
            mixed_in,
            steps,
            decay_log,
            shared,
            skip_gain,
        )
        gate_act = jax.nn.silu(gate_proj)
        gated = scanned * gate_act
        square_sum = lax.psum(jnp.sum(gated * gated, axis=1), ("row", "col"))
        spread = lax.rsqrt(square_sum / inner_full + EPS)[:, None]
        normed_out = (gated * spread * norm_gate[None, :]).astype(jnp.bfloat16)
        partial_out = jnp.dot(normed_out, out_w, preferred_element_type=jnp.float32)
        branch = lax.psum_scatter(
            partial_out.astype(jnp.bfloat16), ("row", "col"), scatter_dimension=0, tiled=True
        ).astype(jnp.float32)
        out_blocks.append(
            (row_local.astype(jnp.float32) + live_local[:, None] * branch).astype(jnp.bfloat16)
        )
        gate_w, value_w, pair_w, step_w, out_w = fetch_weights(
            w_gate, w_value, w_pair, w_step, w_out
        )
        full_back = lax.all_gather(back_local, ("row", "col"), axis=0, tiled=True)
        grad_branch = full_back * live_mask[:, None].astype(jnp.bfloat16)
        out_term = jnp.einsum(
            "ti,td->id", normed_out, grad_branch, preferred_element_type=jnp.float32
        )
        grad_normed = jnp.einsum(
            "td,id->ti", grad_branch, out_w, preferred_element_type=jnp.float32
        )
        weighted = grad_normed * norm_gate[None, :]
        cross_sum = lax.psum(jnp.sum(weighted * gated, axis=1), ("row", "col"))
        grad_gated = weighted * spread - gated * spread**3 * (cross_sum / inner_full)[:, None]
        g_norm_gate = g_norm_gate + jnp.sum(grad_normed * gated * spread, axis=0)
        grad_scanned = grad_gated * gate_act
        grad_gate_proj = grad_gated * scanned * silu_slope(gate_proj)
        grad_mixed, grad_steps, grad_decay, grad_shared, grad_skip = mixer_pull(grad_scanned)
        g_decay = g_decay + grad_decay
        g_skip = g_skip + grad_skip
        grad_shared_local = lax.psum_scatter(
            grad_shared.astype(jnp.bfloat16), ("row", "col"), scatter_dimension=1, tiled=True
        ).astype(jnp.float32)
        grad_pair_proj, conv_pair_term, bias_pair_term = pair_pull(grad_shared_local)
        grad_value_proj, conv_value_term, bias_value_term = value_pull(grad_mixed)
        grad_step_proj, step_bias_term = step_pull(grad_steps)
        g_conv_pair = g_conv_pair + conv_pair_term
        g_bias_pair = g_bias_pair + bias_pair_term
        g_conv_value = g_conv_value + conv_value_term
        g_bias_value = g_bias_value + bias_value_term
        g_step_bias = g_step_bias + step_bias_term
        low_gate = grad_gate_proj.astype(jnp.bfloat16)
        low_value = grad_value_proj.astype(jnp.bfloat16)
        low_pair = grad_pair_proj.astype(jnp.bfloat16)
        low_step = grad_step_proj.astype(jnp.bfloat16)
        gate_term = jnp.einsum("td,tc->dc", normed, low_gate, preferred_element_type=jnp.float32)
        value_term = jnp.einsum("td,tc->dc", normed, low_value, preferred_element_type=jnp.float32)
        pair_term = jnp.einsum("td,tc->dc", normed, low_pair, preferred_element_type=jnp.float32)
        step_term = jnp.einsum("td,tc->dc", normed, low_step, preferred_element_type=jnp.float32)
        grad_in = jnp.einsum("tc,dc->td", low_gate, gate_w, preferred_element_type=jnp.float32)
        grad_in = grad_in + jnp.einsum(
            "tc,dc->td", low_value, value_w, preferred_element_type=jnp.float32
        )
        grad_in = grad_in + jnp.einsum(
            "tc,dc->td", low_pair, pair_w, preferred_element_type=jnp.float32
        )
        grad_in = grad_in + jnp.einsum(
            "tc,dc->td", low_step, step_w, preferred_element_type=jnp.float32
        )
        grad_in_local = lax.psum_scatter(
            grad_in.astype(jnp.bfloat16), ("row", "col"), scatter_dimension=0, tiled=True
        ).astype(jnp.float32)
        local_rows = row_local.astype(jnp.float32) * rms_local
        weighted_in = grad_in_local * norm_in_f[None, :]
        cross_in = jnp.sum(weighted_in * local_rows, axis=1)
        grad_rows = back_local.astype(jnp.float32) + rms_local * (
            weighted_in - local_rows * (cross_in / width_full)[:, None]
        )
        back_blocks.append(grad_rows.astype(jnp.bfloat16))
        g_norm_in = g_norm_in + jnp.sum(grad_in_local * local_rows, axis=0)
        local_terms.append((gate_term, value_term, pair_term, step_term, out_term))
    local_total = reduce(add_trees, local_terms)
    final_grads = reduce_weights(
        local_total[0], local_total[1], local_total[2], local_total[3], local_total[4]
    )
    team_norm_in = lax.psum(g_norm_in, ("row", "col"))
    small_total = lax.psum(
        (
            team_norm_in,
            g_conv_value,
            g_bias_value,
            g_conv_pair,
            g_bias_pair,
            g_step_bias,
            g_decay,
            g_skip,
            g_norm_gate,
        ),
        "dp",
    )
    out_dealt = jnp.concatenate(out_blocks, axis=0)
    back_dealt = jnp.concatenate(back_blocks, axis=0)
    returned = (
        lax.all_to_all(
            out_dealt[recv_order].reshape(group_count, quota_len, width_full),
            "dp",
            split_axis=0,
            concat_axis=0,
            tiled=True,
        ),
        lax.all_to_all(
            back_dealt[recv_order].reshape(group_count, quota_len, width_full),
            "dp",
            split_axis=0,
            concat_axis=0,
            tiled=True,
        ),
    )
    block_out = returned[0].reshape(share_len, width_full)[send_rank]
    grad_tokens = returned[1].reshape(share_len, width_full)[send_rank]
    return (
        block_out,
        grad_tokens,
        small_total[0],
        final_grads[0],
        final_grads[1],
        final_grads[2],
        final_grads[3],
        small_total[1],
        small_total[2],
        small_total[3],
        small_total[4],
        small_total[5],
        small_total[6],
        small_total[7],
        small_total[8],
        final_grads[4],
    )


def solution(mesh):
    placed = (
        P(("dp", "row", "col"), None),
        P(("dp", "row", "col"), None),
        P("dp", None),
        P(),
        P(),
        P("dp", ("row", "col")),
        P("dp", ("row", "col")),
        P("dp", ("row", "col")),
        P("dp", ("row", "col")),
        P(None, ("row", "col")),
        P(("row", "col")),
        P(None, ("row", "col")),
        P(("row", "col")),
        P(("row", "col")),
        P(("row", "col")),
        P(("row", "col")),
        P(("row", "col")),
        P(("row", "col"), "dp"),
    )
    return jax.shard_map(
        per_device,
        mesh=mesh,
        in_specs=placed,
        out_specs=(
            P(("dp", "row", "col"), None),
            P(("dp", "row", "col"), None),
            P(),
            P("dp", ("row", "col")),
            P("dp", ("row", "col")),
            P("dp", ("row", "col")),
            P("dp", ("row", "col")),
            P(None, ("row", "col")),
            P(("row", "col")),
            P(None, ("row", "col")),
            P(("row", "col")),
            P(("row", "col")),
            P(("row", "col")),
            P(("row", "col")),
            P(("row", "col")),
            P(("row", "col"), "dp"),
        ),
        check_vma=False,
    )
```

profile of v0, /device:TPU:1, one launch (start us, length us, event | category | flops | bytes accessed | tf_op | source)
XLA Modules:
  0.0 1964.8 jit_solution(651409051739620356)
XLA Ops:
  8.1 30.5 %scatter_custom_fusion = s32[8192]{0:T(1024)S(1)} fusion(s32[8192]{0:T(1024)S(1)} %compare_select_fusion.6, s32[8192]{0:T(1024)S(1)} %iota.37, s32[]{:T(128)} %constant.290.clone.1), kind=kCustom, calls=%fused_computation.496 | custom fusion | bytes 32772 | tf_op jit(solution)/shard_map/scatter | solution.py:188
  65.7 14.5 all_to_all.20
  85.8 6.0 all_gather.23
  91.8 5.8 all_gather.25
  100.7 22.2 %all-gather.16.cloned.1.call-done = bf16[1024,1536]{1,0:T(8,128)(2,1)} async-done(((bf16[128,1536]{1,0:T(8,128)(2,1)}), bf16[1024,1536]{1,0:T(8,128)(2,1)}) %all-gather.16.cloned.1.call-update) | async-done | bytes 3145744 | tf_op jit(solution)/shard_map/all_gather | solution.py:245
  126.1 58.6 %all-gather.8.cloned.1.call-done = bf16[1024,1536]{1,0:T(8,128)(2,1)} async-done(((bf16[128,1536]{1,0:T(8,128)(2,1)}), bf16[1024,1536]{1,0:T(8,128)(2,1)}) %all-gather.8.cloned.1.call-update) | async-done | bytes 3145744 | tf_op jit(solution)/shard_map/all_gather | solution.py:245
  197.0 27.2 %all_gather.52 = bf16[1024,256]{0,1:T(8,128)(2,1)S(1)} all-gather(bf16[1024,32]{0,1:T(8,128)(2,1)S(1)} %get-tuple-element.1753), channel_id=1, replica_groups=mesh['dp'=4,'row'=2,'col'=4] {'row','col'}, dimensions={1}, use_global_device_ids=true | all-gather | bytes 589824 | tf_op jit(solution)/shard_map/all_gather | solution.py:260
  235.6 4.6 fusion.227
  251.8 143.3 %while.90 = (s32[]{:T(128)}, f32[6,64,128]{2,1,0:T(8,128)S(1)}, s32[]{:T(128)}, f32[4,256,6,64]{1,0,3,2:T(4,128)}, f32[4,6,64,128]{3,2,1,0:T(8,128)}, /*index=5*...) while((s32[]{:T(128)}, f32[6,64,128]{2,1,0:T(8,128)S(1)}, ...), condition=%wide.region_10.12_spmd.clone, body=%wide.region_7.11_spmd.clone.sunk | while | flops 707682816 | bytes 6378105 | solution.py:99
  272.5 9.6 dynamic_update_slice.144
  308.3 9.6 dynamic_update_slice.144
  344.2 9.6 dynamic_update_slice.144
  380.0 9.6 dynamic_update_slice.144
  395.1 26.9 %all_gather.56 = bf16[1024,256]{0,1:T(8,128)(2,1)S(1)} all-gather(bf16[1024,32]{0,1:T(8,128)(2,1)} %get-tuple-element.1862), channel_id=1, replica_groups=mesh['dp'=4,'row'=2,'col'=4] {'row','col'}, dimensions={1}, use_global_device_ids=true | all-gather | bytes 589824 | tf_op jit(solution)/shard_map/all_gather | solution.py:260
  439.0 114.2 %while.91 = (s32[]{:T(128)}, f32[6,64,128]{2,1,0:T(8,128)S(1)}, s32[]{:T(128)}, f32[4,256,6,64]{1,0,3,2:T(4,128)}, f32[4,6,64,128]{3,2,1,0:T(8,128)}, /*index=5*...) while((s32[]{:T(128)}, f32[6,64,128]{2,1,0:T(8,128)S(1)}, ...), condition=%wide.region_20.22_spmd.clone, body=%wide.region_17.21_spmd.clone.sunk | while | flops 707682816 | bytes 6367685 | solution.py:99
  452.7 9.5 dynamic_update_slice.147
  481.2 9.5 dynamic_update_slice.147
  509.8 9.5 dynamic_update_slice.147
  538.4 9.5 dynamic_update_slice.147
  568.8 6.4 multiply_reduce_fusion.21
  575.2 16.2 all-reduce.47
  591.5 5.2 fusion.206
  596.7 7.4 multiply_reduce_fusion.7
  604.1 14.0 all-reduce.46
  618.2 9.0 multiply_reduce_fusion.8
  637.0 337.4 %while.92 = (s32[]{:T(128)}, f32[6]{0:T(128)}, f32[6,64,128]{2,1,0:T(8,128)}, f32[4,256,6,64]{1,0,3,2:T(4,128)}, f32[4,256,6]{1,2,0:T(8,128)}, /*index=5*/f32[4,...) while((s32[]{:T(128)}, f32[6]{0:T(128)}, ...), condition=%wide.region_40.42_spmd.clone, body=%wide.region_27.41_spmd.clone.sunk | while | flops 1670699520 | bytes 24199096 | solution.py:99
  686.1 8.8 reduce-window.164
  706.2 9.5 dynamic_update_slice.152
  770.1 8.8 reduce-window.164
  790.2 9.5 dynamic_update_slice.152
  854.8 8.8 reduce-window.164
  874.9 9.5 dynamic_update_slice.152
  939.5 8.8 reduce-window.164
  959.5 9.5 dynamic_update_slice.152
  984.1 335.6 %while.93 = (s32[]{:T(128)}, f32[6]{0:T(128)}, f32[6,64,128]{2,1,0:T(8,128)}, f32[4,256,6,64]{1,0,3,2:T(4,128)}, f32[4,256,6]{1,2,0:T(8,128)}, /*index=5*/f32[4,...) while((s32[]{:T(128)}, f32[6]{0:T(128)}, ...), condition=%wide.region_59.61_spmd.clone, body=%wide.region_46.60_spmd.clone.sunk | while | flops 1670699520 | bytes 24199096 | solution.py:99
  1032.7 8.7 reduce-window.168
  1052.5 9.5 dynamic_update_slice.156
  1116.2 8.7 reduce-window.168
  1136.1 9.5 dynamic_update_slice.156
  1200.5 8.7 reduce-window.168
  1220.3 9.5 dynamic_update_slice.156
  1284.7 8.7 reduce-window.168
  1304.5 9.5 dynamic_update_slice.156
  1331.8 7.1 multiply_reduce_fusion.17
  1351.1 7.1 multiply_reduce_fusion.13
  1373.9 30.7 %reduce-scatter.22.cloned.1.call-done = bf16[1024,32]{0,1:T(8,128)(2,1)} async-done(((bf16[1024,256]{0,1:T(8,128)(2,1)}), bf16[1024,32]{0,1:T(8,128)(2,1)}) %reduce-scatter.22.cloned.1.call-update) | async-done | bytes 65552 | tf_op jit(solution)/shard_map/reduce_scatter | solution.py:304
  1407.1 62.8 %reduce-scatter.26.cloned.1.call-done = bf16[1024,32]{0,1:T(8,128)(2,1)} async-done(((bf16[1024,256]{0,1:T(8,128)(2,1)}), bf16[1024,32]{0,1:T(8,128)(2,1)}) %reduce-scatter.26.cloned.1.call-update) | async-done | bytes 65552 | tf_op jit(solution)/shard_map/reduce_scatter | solution.py:304
  1475.4 6.0 add_convert_fusion
  1491.9 5.3 convolution_convert_fusion.1
  1497.8 5.3 convolution_convert_fusion
  1507.3 5.5 fusion.208
  1515.1 5.8 fusion.204
  1540.6 15.4 reduce-scatter.28.cloned.1.call-done
  1556.0 76.9 %reduce-scatter.24.cloned.1.call-done = bf16[128,1536]{1,0:T(8,128)(2,1)} async-done(((bf16[1024,1536]{1,0:T(8,128)(2,1)}), bf16[128,1536]{1,0:T(8,128)(2,1)}) %reduce-scatter.24.cloned.1.call-update) | async-done | bytes 393232 | tf_op jit(solution)/shard_map/reduce_scatter | solution.py:333
  1634.6 75.2 %reduce-scatter.18.cloned.1.call-done = bf16[128,1536]{1,0:T(8,128)(2,1)} async-done(((bf16[1024,1536]{1,0:T(8,128)(2,1)}), bf16[128,1536]{1,0:T(8,128)(2,1)}) %reduce-scatter.18.cloned.1.call-update) | async-done | bytes 393232 | tf_op jit(solution)/shard_map/reduce_scatter | solution.py:278
  1709.9 77.1 %reduce-scatter.20.cloned.1.call-done = bf16[128,1536]{1,0:T(8,128)(2,1)} async-done(((bf16[1024,1536]{1,0:T(8,128)(2,1)}), bf16[128,1536]{1,0:T(8,128)(2,1)}) %reduce-scatter.20.cloned.1.call-update) | async-done | bytes 393232 | tf_op jit(solution)/shard_map/reduce_scatter | solution.py:278
  1791.0 5.0 all-to-all-start.3
  1801.6 5.2 all-to-all-done.3
  1813.6 20.9 %reduce-scatter.34.cloned.1.call-done = bf16[384,32]{1,0:T(8,128)(2,1)} async-done(((bf16[1536,32]{1,0:T(8,128)(2,1)}), bf16[384,32]{1,0:T(8,128)(2,1)}) %reduce-scatter.34.cloned.1.call-update) | async-done | bytes 24592
  1836.1 26.6 %reduce-scatter.38.cloned.1.call-done = bf16[384,384]{1,0:T(8,128)(2,1)} async-done(((bf16[1536,384]{1,0:T(8,128)(2,1)}), bf16[384,384]{1,0:T(8,128)(2,1)}) %reduce-scatter.38.cloned.1.call-update) | async-done | bytes 294928
  1864.7 26.3 %reduce-scatter.32.cloned.1.call-done = bf16[384,384]{1,0:T(8,128)(2,1)} async-done(((bf16[1536,384]{1,0:T(8,128)(2,1)}), bf16[384,384]{1,0:T(8,128)(2,1)}) %reduce-scatter.32.cloned.1.call-update) | async-done | bytes 294928 | tf_op jit(solution)/shard_map/reduce_scatter | solution.py:134
  1892.8 26.4 %reduce-scatter.30.cloned.1.call-done = bf16[384,384]{1,0:T(8,128)(2,1)} async-done(((bf16[1536,384]{1,0:T(8,128)(2,1)}), bf16[384,384]{1,0:T(8,128)(2,1)}) %reduce-scatter.30.cloned.1.call-update) | async-done | bytes 294928 | tf_op jit(solution)/shard_map/reduce_scatter | solution.py:131
  1921.0 18.0 psum.102
  1939.0 14.5 all-reduce.48
  (1516 shorter events, 939.5 us)
Async XLA Ops:
  7.2 35.2 %copy-start = (bf16[256,1536]{1,0:T(8,128)(2,1)S(1)}, bf16[256,1536]{1,0:T(8,128)(2,1)}, u32[]{:S(2)}) copy-start(bf16[256,1536]{1,0:T(8,128)(2,1)} %param.27) | copy-start | bytes 2359300
  44.5 15.0 all-to-all-start
  48.9 74.0 %all-gather.16.cloned.1.call-start = ((), (), s32[]{:S(2)}) async-start(), calls=%async_computation.20 | async-start | bytes 3538944 | tf_op jit(solution)/shard_map/all_gather | solution.py:245
  61.7 122.9 %all-gather.8.cloned.1.call-start = ((), (), s32[]{:S(2)}) async-start(), calls=%async_computation.15 | async-start | bytes 3538944 | tf_op jit(solution)/shard_map/all_gather | solution.py:245
  62.5 166.8 %all-gather.10.cloned.1.call-start = ((), (), s32[]{:S(2)}) async-start(), calls=%async_computation.16 | async-start | bytes 1474560 | tf_op jit(solution)/shard_map/all_gather | solution.py:122
  63.2 501.9 %all-gather.12.cloned.1.call-start = ((), (), s32[]{:S(2)}) async-start(), calls=%async_computation.17 | async-start | bytes 1474560 | tf_op jit(solution)/shard_map/all_gather | solution.py:121
  63.8 527.7 %all-gather.14.cloned.1.call-start = ((), (), s32[]{:S(2)}) async-start(), calls=%async_computation.18 | async-start | bytes 1474560 | tf_op jit(solution)/shard_map/all_gather | solution.py:125
  64.4 527.1 %all-gather.20.cloned.1.call-start = ((), (), s32[]{:S(2)}) async-start(), calls=%async_computation.25 | async-start | bytes 3538944 | tf_op jit(solution)/shard_map/all_gather | solution.py:287
  81.5 44.0 %copy-start.27 = (bf16[256,1536]{1,0:T(8,128)(2,1)}, bf16[256,1536]{1,0:T(8,128)(2,1)S(1)}, u32[]{:S(2)}) copy-start(bf16[256,1536]{1,0:T(8,128)(2,1)S(1)} %gather_fusion.6) | copy-start | bytes 2359300
  81.6 16.1 copy-start.148
  81.6 16.7 copy-start.175
  81.6 17.3 copy-start.165
  82.6 514.2 %all-gather.18.cloned.1.call-start = ((), (), s32[]{:S(2)}) async-start(), calls=%async_computation.22 | async-start | bytes 3538944 | tf_op jit(solution)/shard_map/all_gather | solution.py:287
  100.0 135.5 %copy-start.88 = (f32[1024]{0:T(1024)}, f32[1024]{0:T(1024)S(1)}, u32[]{:S(2)}) copy-start(f32[1024]{0:T(1024)S(1)} %get-tuple-element.1853) | copy-start | bytes 12292
  100.0 135.5 %copy-start.90 = (f32[1024]{0:T(1024)}, f32[1024]{0:T(1024)S(1)}, u32[]{:S(2)}) copy-start(f32[1024]{0:T(1024)S(1)} %get-tuple-element.1854) | copy-start | bytes 12292
  100.0 135.5 %copy-start.92 = (f32[1024]{0:T(1024)}, f32[1024]{0:T(1024)S(1)}, u32[]{:S(2)}) copy-start(f32[1024]{0:T(1024)S(1)} %get-tuple-element.1855) | copy-start | bytes 12292
  100.7 134.8 %copy-start.94 = (f32[1024]{0:T(1024)}, f32[1024]{0:T(1024)S(1)}, u32[]{:S(2)}) copy-start(f32[1024]{0:T(1024)S(1)} %get-tuple-element.1858) | copy-start | bytes 12292
  100.7 1304.0 %reduce-scatter.22.cloned.1.call-start = ((), (), s32[]{:S(2)}) async-start(), calls=%async_computation.23 | async-start | bytes 589824 | tf_op jit(solution)/shard_map/reduce_scatter | solution.py:304
  269.8 12.9 copy-start.115
  269.8 12.3 copy-start.114
  305.6 12.9 copy-start.115
  305.6 12.3 copy-start.114
  341.6 12.8 copy-start.115
  341.6 12.2 copy-start.114
  377.3 12.8 copy-start.115
  377.3 12.3 copy-start.114
  568.8 22.7 %copy-start.166 = (bf16[1024]{0:T(1024)(128)(2,1)S(1)}, bf16[1024]{0:T(1024)(128)(2,1)}, u32[]{:S(2)}) copy-start(bf16[1024]{0:T(1024)(128)(2,1)} %get-tuple-element.1857) | copy-start | bytes 6148
  591.4 26.8 %copy-start.107 = (f32[1024]{0:T(1024)}, f32[1024]{0:T(1024)S(1)}, u32[]{:S(2)}) copy-start(f32[1024]{0:T(1024)S(1)} %get-tuple-element.1849) | copy-start | bytes 12292
  591.4 26.8 %copy-start.131 = (f32[1024]{0:T(1024)}, f32[1024]{0:T(1024)S(1)}, u32[]{:S(2)}) copy-start(f32[1024]{0:T(1024)S(1)} %get-tuple-element.1851) | copy-start | bytes 12292
  702.3 14.7 copy-start.50
  786.3 14.7 copy-start.50
  871.0 14.7 copy-start.50
  955.6 14.7 copy-start.50
  1048.6 14.6 copy-start.52
  1132.2 14.6 copy-start.52
  1216.4 14.6 copy-start.52
  1300.6 14.6 copy-start.52
  1325.8 144.1 %reduce-scatter.26.cloned.1.call-start = ((), (), s32[]{:S(2)}) async-start(), calls=%async_computation.26 | async-start | bytes 589824 | tf_op jit(solution)/shard_map/reduce_scatter | solution.py:304
  1358.3 197.7 %reduce-scatter.28.cloned.1.call-start = ((), (), s32[]{:S(2)}) async-start(), calls=%async_computation.27 | async-start | bytes 3538944 | tf_op jit(solution)/shard_map/reduce_scatter | solution.py:333
  1369.4 35.2 %copy-start.58 = (f32[1024,32]{0,1:T(8,128)S(1)}, f32[1024,32]{0,1:T(8,128)}, u32[]{:S(2)}) copy-start(f32[1024,32]{0,1:T(8,128)} %copy-done.57) | copy-start | bytes 393220
  1369.4 100.5 %copy-start.56 = (f32[1024,32]{0,1:T(8,128)S(1)}, f32[1024,32]{0,1:T(8,128)}, u32[]{:S(2)}) copy-start(f32[1024,32]{0,1:T(8,128)} %copy-done.55) | copy-start | bytes 393220
  1407.1 65.5 %copy-start.48 = (bf16[1536,32]{0,1:T(8,128)(2,1)S(1)}, bf16[1536,32]{0,1:T(8,128)(2,1)}, u32[]{:S(2)}) copy-start(bf16[1536,32]{0,1:T(8,128)(2,1)} %all_gather.25) | copy-start | bytes 294916
  1481.4 151.4 %reduce-scatter.24.cloned.1.call-start = ((), (), s32[]{:S(2)}) async-start(), calls=%async_computation.24 | async-start | bytes 3538944 | tf_op jit(solution)/shard_map/reduce_scatter | solution.py:333
  1491.2 218.7 %reduce-scatter.18.cloned.1.call-start = ((), (), s32[]{:S(2)}) async-start(), calls=%async_computation.19 | async-start | bytes 3538944 | tf_op jit(solution)/shard_map/reduce_scatter | solution.py:278
  1497.2 289.8 %reduce-scatter.20.cloned.1.call-start = ((), (), s32[]{:S(2)}) async-start(), calls=%async_computation.21 | async-start | bytes 3538944 | tf_op jit(solution)/shard_map/reduce_scatter | solution.py:278
  1503.2 308.7 %reduce-scatter.36.cloned.1.call-start = ((), (), s32[]{:S(2)}) async-start(), calls=%async_computation.31 | async-start | bytes 491520
  1507.2 327.2 %reduce-scatter.34.cloned.1.call-start = ((), (), s32[]{:S(2)}) async-start(), calls=%async_computation.30 | async-start | bytes 491520
  1515.1 347.6 %reduce-scatter.38.cloned.1.call-start = ((), (), s32[]{:S(2)}) async-start(), calls=%async_computation.32 | async-start | bytes 1474560
  1523.4 367.6 %reduce-scatter.32.cloned.1.call-start = ((), (), s32[]{:S(2)}) async-start(), calls=%async_computation.29 | async-start | bytes 1474560 | tf_op jit(solution)/shard_map/reduce_scatter | solution.py:134
  1530.6 388.6 %reduce-scatter.30.cloned.1.call-start = ((), (), s32[]{:S(2)}) async-start(), calls=%async_computation.28 | async-start | bytes 1474560 | tf_op jit(solution)/shard_map/reduce_scatter | solution.py:131
  1537.7 95.2 %copy-start.104 = (f32[1536]{0:T(1024)S(1)}, f32[1536]{0:T(1024)}, u32[]{:S(2)}) copy-start(f32[1536]{0:T(1024)} %convert_element_type.327) | copy-start | bytes 18436
  1540.6 92.3 %copy-start.26 = (bf16[256,1536]{1,0:T(8,128)(2,1)S(1)}, bf16[256,1536]{1,0:T(8,128)(2,1)}, u32[]{:S(2)}) copy-start(bf16[256,1536]{1,0:T(8,128)(2,1)} %copy-done.25) | copy-start | bytes 2359300
  1540.6 246.4 %copy-start.28 = (bf16[256,1536]{1,0:T(8,128)(2,1)S(1)}, bf16[256,1536]{1,0:T(8,128)(2,1)}, u32[]{:S(2)}) copy-start(bf16[256,1536]{1,0:T(8,128)(2,1)} %copy-done.27) | copy-start | bytes 2359300
  1556.0 231.0 %copy-start.60 = (bf16[128,1536]{1,0:T(8,128)(2,1)S(1)}, bf16[128,1536]{1,0:T(8,128)(2,1)}, u32[]{:S(2)}) copy-start(bf16[128,1536]{1,0:T(8,128)(2,1)} %reduce-scatter.28.cloned.1.call-done) | copy-start | bytes 1179652
  1632.8 154.1 %copy-start.61 = (bf16[128,1536]{1,0:T(8,128)(2,1)S(1)}, bf16[128,1536]{1,0:T(8,128)(2,1)}, u32[]{:S(2)}) copy-start(bf16[128,1536]{1,0:T(8,128)(2,1)} %reduce-scatter.24.cloned.1.call-done) | copy-start | bytes 1179652
  1791.0 15.8 all-to-all-start.3
  1801.5 10.3 copy-start.121
  1801.5 10.3 copy-start.122
  1801.5 11.9 copy-start.171
  1801.6 11.9 copy-start.159
  1801.6 11.9 copy-start.160
  1801.6 11.9 copy-start.161
  1801.6 11.9 copy-start.162
  1806.8 148.8 %all-to-all-start.1 = ((bf16[4,64,1536]{2,1,0:T(8,128)(2,1)}), bf16[4,64,1536]{2,1,0:T(8,128)(2,1)S(1)}, u32[]{:S(2)}, u32[]{:S(2)}) async-start(bf16[4,64,1536]{2,1,0:T(8,128)(2,1)} %bitcast.14), calls=%async_computation.3 | async-start | bytes 1572864 | tf_op jit(solution)/shard_map/all_to_all | solution.py:367
  (299 other events, 1115.1 us)
Sparse Core Ops, SparseCore 0:
  61.9 60.9 all-gather.15
  125.6 59.0 all-gather.7
  186.2 17.3 all-gather.9
  205.0 17.4 all-gather.11
  223.9 17.4 all-gather.13
  243.4 59.2 all-gather.19
  304.7 59.0 all-gather.17
  1326.0 78.6 reduce-scatter.21
  1408.9 60.9 reduce-scatter.25
  1481.5 74.3 reduce-scatter.27
  1559.6 73.2 reduce-scatter.23
  1636.3 73.5 reduce-scatter.17
  1713.5 73.4 reduce-scatter.19
  1789.9 20.7 reduce-scatter.35
  1813.6 20.8 reduce-scatter.33
  1836.9 25.7 reduce-scatter.37
  1865.2 25.7 reduce-scatter.31
  1893.4 25.7 reduce-scatter.29
where the time goes:
time: 1990 us; the launch traced here: 1960 us
  local copies, waits for them, and re-layouts  566 us (28%)
  waiting for transfers between devices  529 us (27%)
  other arithmetic  380 us (19%)
  matrix products  306 us (15%)
  blocking collectives  143 us (7%)
    dynamic_update_slice x40, local copies, waits for them, and re-layouts, ssd_scan(): lax.scan(jax.checkpoint(one_block), start_carry, blocks)  182 us
    another operation x68, other arithmetic  156 us
    reduce_scatter x2, waiting for transfers between devices, per_device(): lax.psum_scatter(partial_out.astype(jnp.bfloat16), ('row', 'col'), scatte...  152 us
    another operation x129, local copies, waits for them, and re-layouts  107 us
    reduce_scatter x2, waiting for transfers between devices, per_device(): lax.psum_scatter(grad_shared.astype(jnp.bfloat16), ('row', 'col'), scatte...  93.5 us
    reduce_scatter x2, waiting for transfers between devices, per_device(): lax.psum_scatter(grad_in.astype(jnp.bfloat16), ('row', 'col'), scatter_di...  92.2 us
    all_gather x2, waiting for transfers between devices, per_device(): full_rows = lax.all_gather(row_local, ('row', 'col'), axis=0, tiled=True)  80.8 us
    dot_general x24, matrix products, one_block(): jnp.einsum('tsh,shp->thp', mix_grid, block_values, precision=PRECISE)  76.9 us
  transfers between devices with their start and end apart: 21, of which 14 were waited for; matrix products, arithmetic and copies ran while one was open for 25% of the time, Pallas kernels for 0%

commit v1 on v0

v1 whole, which is shorter than its diff:
```python
from functools import partial

import jax
import jax.numpy as jnp
import numpy as np
from jax import lax
from jax.experimental import pallas as pl
from jax.experimental.pallas import tpu as pltpu
from jax.sharding import PartitionSpec as P

EPS = 1e-05
EXACT = lax.Precision.HIGHEST
F32 = jnp.float32
BF16 = jnp.bfloat16
SUB = 128
ROWS = 256
LANES = 128
VMEM_BYTES = 56 * 1024 * 1024


def dot_nn(a, b):
    return jnp.dot(a, b, preferred_element_type=F32)


def dot_nt(a, b):
    return lax.dot_general(a, b, (((1,), (1,)), ((), ())), preferred_element_type=F32)


def dot_tn(a, b):
    return lax.dot_general(a, b, (((0,), (0,)), ((), ())), preferred_element_type=F32)


def sigmoid(v):
    return 1.0 / (1.0 + jnp.exp(-v))


def softplus(v):
    return jnp.maximum(v, 0.0) + jnp.log1p(jnp.exp(-jnp.abs(v)))


def split_two(v):
    high = v.astype(BF16)
    return high, (v - high.astype(F32)).astype(BF16)


def read_bounds(bounds_ref, micro):
    return [bounds_ref[micro, k] for k in range(bounds_ref.shape[1])]


def segment_of(places, bounds):
    total = (places >= bounds[0]).astype(jnp.int32)
    for bound in bounds[1:]:
        total = total + (places >= bound).astype(jnp.int32)
    return total


def segment_scalar(place, bounds):
    total = jnp.int32(0)
    for bound in bounds:
        total = total + jnp.where(place >= bound, 1, 0)
    return total


def iota(shape, axis):
    return lax.broadcasted_iota(jnp.int32, shape, axis)


def same_masks(places, bounds, count):
    own = segment_of(places, bounds)
    return [
        (segment_of(places - shift, bounds) == own) & (places >= shift) & (places < count)
        for shift in range(1, 4)
    ]


def expand_heads(parts, spread_ref):
    stacked = jnp.concatenate(parts, axis=0)
    high, low = split_two(stacked)
    lane = iota(stacked.shape, 1)
    joined = jnp.where(lane < 8, high.astype(F32), pltpu.roll(low.astype(F32), 8, 1))
    wide = dot_nn(joined.astype(BF16), spread_ref[...])
    sizes = np.cumsum([0] + [part.shape[0] for part in parts])
    return [wide[sizes[k] : sizes[k + 1]] for k in range(len(parts))]


def reduce_heads(v, gather_ref):
    high, low = split_two(v)
    return dot_nn(high, gather_ref[...]) + dot_nn(low, gather_ref[...])


def scan_frame(base, bounds, steps, rate, lower_ref):
    start_place = base
    col = start_place + iota((SUB, LANES), 0)
    row = start_place + iota((SUB, SUB), 1)
    seg_col = segment_of(col, bounds)
    seg_row = segment_of(row, bounds)
    allowed = (seg_col == seg_row) & (col >= row)
    last_seg = jnp.where(start_place > 0, segment_scalar(start_place - 1, bounds), -1)
    end_seg = segment_scalar(start_place + SUB - 1, bounds)
    log_decay = jnp.dot(
        lower_ref[...], steps * rate, preferred_element_type=F32, precision=EXACT
    )
    reach = jnp.where(seg_col == last_seg, jnp.exp(log_decay), 0.0)
    tail = jnp.where(
        seg_col == end_seg, jnp.exp(log_decay[SUB - 1 : SUB, :] - log_decay), 0.0
    )
    return allowed, log_decay, reach, tail


def decay_grid(log_decay, log_rows, head):
    gap = log_decay[:, head : head + 1] - log_rows[head : head + 1, :]
    return jnp.exp(jnp.minimum(gap, 0.0))


def forward_kernel(
    pair_count,
    bounds_ref,
    x_ref,
    norm_in_ref,
    w_value_ref,
    w_gate_ref,
    w_small_ref,
    taps_value_ref,
    taps_pair_ref,
    heads_ref,
    skip_ref,
    norm_gate_ref,
    w_out_ref,
    spread_ref,
    lower_ref,
    normed_ref,
    gate_ref,
    value_ref,
    conv_value_ref,
    pair_ref,
    conv_pair_ref,
    step_ref,
    scanned_ref,
    states_ref,
    partial_ref,
    square_ref,
    halo_value,
    halo_pair,
    state,
):
    micro = pl.program_id(0)
    block = pl.program_id(1)
    count = pl.num_programs(1) * ROWS
    bounds = read_bounds(bounds_ref, micro)
    base = block * ROWS

    @pl.when(block == 0)
    def _():
        halo_value[...] = jnp.zeros_like(halo_value)
        halo_pair[...] = jnp.zeros_like(halo_pair)
        state[...] = jnp.zeros_like(state)

    x = x_ref[...].reshape(ROWS, x_ref.shape[-1]).astype(F32)
    rms = lax.rsqrt(jnp.mean(x * x, axis=1, keepdims=True) + EPS)
    normed = (x * rms * norm_in_ref[...].astype(F32)).astype(BF16)
    normed_ref[...] = normed
    value = dot_nn(normed, w_value_ref[...])
    gate = dot_nn(normed, w_gate_ref[...])
    small = dot_nt(normed, w_small_ref[...])
    pair_width = conv_pair_ref.shape[-1]
    pair = small[:, :pair_width]
    step = small[:, pair_width : pair_width + LANES]
    value_ref[...] = value
    gate_ref[...] = gate
    pair_ref[...] = pair
    step_ref[...] = step

    places = base + iota((ROWS, LANES), 0)
    masks = same_masks(places, bounds, count)

    def convolve(v, halo, taps):
        longer = jnp.concatenate([halo, v], axis=0)
        width = v.shape[1]
        out = taps[4:5, :] + taps[3:4, :] * v
        for shift in range(1, 4):
            moved = pltpu.roll(longer, shift, 0)[8:, :]
            mask = jnp.concatenate([masks[shift - 1]] * (width // LANES), axis=1)
            out = out + jnp.where(mask, moved * taps[3 - shift : 4 - shift, :], 0.0)
        return out

    conv_value = convolve(value, halo_value[...], taps_value_ref[...])
    conv_pair = convolve(pair, halo_pair[...], taps_pair_ref[...])
    halo_value[...] = value[ROWS - 8 :, :]
    halo_pair[...] = pair[ROWS - 8 :, :]
    conv_value_ref[...] = conv_value
    conv_pair_ref[...] = conv_pair
    mixed = conv_value * sigmoid(conv_value)
    shared = (conv_pair * sigmoid(conv_pair)).astype(BF16)
    steps = softplus(step + heads_ref[0:1, :])
    rate = heads_ref[1:2, :]
    lane = iota((SUB, LANES), 1)
    left = lane < 64

    scanned_parts = []
    for sub in range(ROWS // SUB):
        rows = slice(sub * SUB, (sub + 1) * SUB)
        sub_steps = steps[rows]
        allowed, log_decay, reach, tail = scan_frame(
            base + sub * SUB, bounds, sub_steps, rate, lower_ref
        )
        steps_wide, reach_wide, tail_wide = expand_heads(
            [sub_steps, reach, tail], spread_ref
        )
        log_rows = log_decay.T
        keys = shared[rows, :LANES]
        reads = shared[rows, LANES:]
        scores = jnp.where(allowed, dot_nt(reads, keys), 0.0)
        stepped = mixed[rows] * steps_wide
        stepped_low = stepped.astype(BF16)
        held = state[...]
        states_ref[sub] = held
        outside = dot_nn(reads, held.astype(BF16)) * reach_wide
        inside = []
        for p in range(pair_count):
            cols = slice(p * LANES, (p + 1) * LANES)
            grids = [
                (scores * decay_grid(log_decay, log_rows, 2 * p + k)).astype(BF16)
                for k in range(2)
            ]
            both = stepped_low[:, cols]
            zero = jnp.zeros_like(both)
            inside.append(
                dot_nn(
                    jnp.concatenate(grids, axis=1),
                    jnp.concatenate(
                        [jnp.where(left, both, zero), jnp.where(left, zero, both)], axis=0
                    ),
                )
            )
        scanned_parts.append(
            jnp.concatenate(inside, axis=1) + outside + mixed[rows] * skip_ref[...]
        )
        state[...] = held * reach_wide[SUB - 1 : SUB, :] + dot_tn(
            keys, (stepped * tail_wide).astype(BF16)
        )
    scanned = jnp.concatenate(scanned_parts, axis=0)
    scanned_ref[...] = scanned
    gated = scanned * (gate * sigmoid(gate))
    high, low = split_two(gated * gated)
    ones = jnp.ones((8, gated.shape[1]), BF16)
    square_ref[...] = dot_nt(ones, high) + dot_nt(ones, low)
    scaled = (gated * norm_gate_ref[...]).astype(BF16)
    partial_ref[...] = (
        dot_nn(scaled, w_out_ref[...]).astype(BF16).reshape(partial_ref.shape)
    )


def back_kernel(
    live_ids,
    bounds_ref,
    back_ref,
    w_out_ref,
    norm_gate_ref,
    scanned_ref,
    gate_ref,
    square_ref,
    grad_normed_ref,
    stats_ref,
):
    micro = pl.program_id(0)
    bounds = read_bounds(bounds_ref, micro)
    base = pl.program_id(1) * ROWS
    places = base + iota((ROWS, LANES), 0)
    live = segment_of(places, bounds) < live_ids
    grad = dot_nt(back_ref[...].reshape(ROWS, back_ref.shape[-1]), w_out_ref[...])
    live_wide = jnp.concatenate([live] * (grad.shape[1] // LANES), axis=1)
    grad = jnp.where(live_wide, grad, 0.0)
    grad_normed_ref[...] = grad
    gate = gate_ref[...]
    gated = scanned_ref[...] * (gate * sigmoid(gate))
    high, low = split_two(grad * norm_gate_ref[...] * gated)
    ones = jnp.ones((8, gated.shape[1]), BF16)
    cross = dot_nt(ones, high) + dot_nt(ones, low)
    stats_ref[...] = jnp.where(iota(cross.shape, 0) == 0, square_ref[...], cross)


def backward_kernel(
    pair_count,
    live_ids,
    inner_full,
    bounds_ref,
    stats_ref,
    grad_normed_ref,
    normed_ref,
    gate_ref,
    value_ref,
    conv_value_ref,
    pair_ref,
    conv_pair_ref,
    step_ref,
    scanned_ref,
    states_ref,
    w_value_ref,
    w_gate_ref,
    w_small_ref,
    taps_value_ref,
    taps_pair_ref,
    heads_ref,
    skip_ref,
    norm_gate_ref,
    spread_ref,
    gather_ref,
    lower_ref,
    upper_ref,
    low_gate_ref,
    low_value_ref,
    low_small_ref,
    normed_out_ref,
    grad_in_ref,
    sums_ref,
    sums_in_ref,
    halo_value,
    halo_pair,
    state,
):
    micro = pl.program_id(0)
    turn = pl.program_id(1)
    block_count = pl.num_programs(1)
    block = block_count - 1 - turn
    count = block_count * ROWS
    bounds = read_bounds(bounds_ref, micro)
    base = block * ROWS

    @pl.when((micro == 0) & (turn == 0))
    def _():
        sums_ref[...] = jnp.zeros_like(sums_ref)
        sums_in_ref[...] = jnp.zeros_like(sums_in_ref)

    @pl.when(turn == 0)
    def _():
        halo_value[...] = jnp.zeros_like(halo_value)
        halo_pair[...] = jnp.zeros_like(halo_pair)
        state[...] = jnp.zeros_like(state)

    width = gate_ref.shape[1]
    tiles = width // LANES
    places = base + iota((ROWS, LANES), 0)
    live = segment_of(places, bounds) < live_ids

    gate = gate_ref[...]
    scanned = scanned_ref[...]
    grad_normed = grad_normed_ref[...]
    norm_gate = norm_gate_ref[...]
    spread = lax.rsqrt(stats_ref[:, 0:1] / inner_full + EPS)
    cross = stats_ref[:, 1:2] / inner_full
    sg = sigmoid(gate)
    act = gate * sg
    gated = scanned * act
    normed_gated = gated * spread
    live_wide = jnp.concatenate([live] * tiles, axis=1)
    normed_out_ref[...] = jnp.where(live_wide, normed_gated * norm_gate, 0.0).astype(BF16)
    grad_gated = spread * (grad_normed * norm_gate - normed_gated * (spread * cross))
    grad_scanned = grad_gated * act
    low_gate = (grad_gated * scanned * (sg * (1.0 + gate * (1.0 - sg)))).astype(BF16)
    low_gate_ref[...] = low_gate

    conv_value = conv_value_ref[...]
    sig_value = sigmoid(conv_value)
    mixed = conv_value * sig_value
    conv_pair = conv_pair_ref[...]
    sig_pair = sigmoid(conv_pair)
    shared = (conv_pair * sig_pair).astype(BF16)
    step_in = step_ref[...] + heads_ref[0:1, :]
    steps = softplus(step_in)
    rate = heads_ref[1:2, :]
    skip = skip_ref[...]
    lane = iota((SUB, LANES), 1)
    left = lane < 64

    grad_mixed_parts = []
    grad_shared_parts = []
    grad_step_parts = []
    decay_sum = jnp.zeros((1, LANES), F32)
    for sub in reversed(range(ROWS // SUB)):
        rows = slice(sub * SUB, (sub + 1) * SUB)
        sub_steps = steps[rows]
        allowed, log_decay, reach, tail = scan_frame(
            base + sub * SUB, bounds, sub_steps, rate, lower_ref
        )
        steps_wide, reach_wide, tail_wide = expand_heads(
            [sub_steps, reach, tail], spread_ref
        )
        log_rows = log_decay.T
        keys = shared[rows, :LANES]
        reads = shared[rows, LANES:]
        scores = jnp.where(allowed, dot_nt(reads, keys), 0.0)
        sub_mixed = mixed[rows]
        stepped = sub_mixed * steps_wide
        stepped_low = stepped.astype(BF16)
        grad_y = grad_scanned[rows]
        grad_low = grad_y.astype(BF16)
        held = states_ref[sub]
        later = state[...]
        later_low = later.astype(BF16)
        grad_scores = jnp.zeros((SUB, SUB), F32)
        inner = []
        for p in range(pair_count):
            cols = slice(p * LANES, (p + 1) * LANES)
            both_x = stepped_low[:, cols]
            both_y = grad_low[:, cols]
            zero = jnp.zeros_like(both_y)
            halves = [jnp.where(left, both_y, zero), jnp.where(left, zero, both_y)]
            grids = []
            for k in range(2):
                fade = decay_grid(log_decay, log_rows, 2 * p + k)
                grids.append((scores * fade).astype(BF16))
                grad_scores = grad_scores + dot_nt(halves[k], both_x) * fade
            inner.append(
                dot_tn(jnp.concatenate(grids, axis=0), jnp.concatenate(halves, axis=0))
            )
        grad_scores = jnp.where(allowed, grad_scores, 0.0).astype(BF16)
        tail_part = tail_wide * dot_nn(keys, later_low)
        grad_stepped = jnp.concatenate(inner, axis=1) + tail_part
        reached = (grad_y * reach_wide).astype(BF16)
        tailed = (stepped * tail_wide).astype(BF16)
        grad_reads = dot_nn(grad_scores, keys) + dot_nt(reached, held.astype(BF16))
        grad_keys = dot_tn(grad_scores, reads) + dot_nt(tailed, later_low)
        stepped_back = stepped_low.astype(F32)
        per_log = reduce_heads(
            grad_low.astype(F32) * (scanned[rows] - skip * sub_mixed)
            - stepped_back * grad_stepped,
            gather_ref,
        )
        kept_wide = reach_wide[SUB - 1 : SUB, :]
        at_end = jnp.sum(stepped_back * tail_part, axis=0, keepdims=True) + kept_wide * jnp.sum(
            later * held, axis=0, keepdims=True
        )
        at_end = reduce_heads(jnp.broadcast_to(at_end, (8, width)), gather_ref)[0:1, :]
        grad_log = (
            jnp.dot(upper_ref[...], per_log, preferred_element_type=F32, precision=EXACT)
            + at_end
        )
        decay_sum = decay_sum + jnp.sum(grad_log * sub_steps, axis=0, keepdims=True) * rate
        grad_steps = reduce_heads(grad_stepped * sub_mixed, gather_ref) + rate * grad_log
        grad_step_parts.insert(0, grad_steps)
        grad_shared_parts.insert(0, jnp.concatenate([grad_keys, grad_reads], axis=1))
        grad_mixed_parts.insert(0, grad_stepped * steps_wide + skip * grad_y)
        state[...] = later * kept_wide + dot_tn(reads, reached)
    grad_mixed = jnp.concatenate(grad_mixed_parts, axis=0)
    grad_shared = jnp.concatenate(grad_shared_parts, axis=0)
    grad_step = jnp.concatenate(grad_step_parts, axis=0) * sigmoid(step_in)

    longer_places = base + iota((ROWS + 8, LANES), 0)
    masks = same_masks(longer_places, bounds, count)

    def convolve_back(q, halo, v, taps):
        longer = jnp.concatenate([q, halo], axis=0)
        grad = taps[3:4, :] * q
        tap_sums = [jnp.sum(v * q, axis=0, keepdims=True)]
        for shift in range(1, 4):
            mask = jnp.concatenate([masks[shift - 1]] * (q.shape[1] // LANES), axis=1)
            kept = jnp.where(mask, longer, 0.0)
            moved = pltpu.roll(kept, ROWS + 8 - shift, 0)[:ROWS, :]
            grad = grad + taps[3 - shift : 4 - shift, :] * moved
            tap_sums.insert(0, jnp.sum(v * moved, axis=0, keepdims=True))
        return grad, tap_sums + [jnp.sum(q, axis=0, keepdims=True)]

    q_value = grad_mixed * (sig_value * (1.0 + conv_value * (1.0 - sig_value)))
    q_pair = grad_shared * (sig_pair * (1.0 + conv_pair * (1.0 - sig_pair)))
    grad_value, value_sums = convolve_back(
        q_value, halo_value[...], value_ref[...], taps_value_ref[...]
    )
    grad_pair, pair_sums = convolve_back(
        q_pair, halo_pair[...], pair_ref[...], taps_pair_ref[...]
    )
    halo_value[...] = q_value[:8, :]
    halo_pair[...] = q_pair[:8, :]
    low_value = grad_value.astype(BF16)
    low_small = jnp.concatenate([grad_pair, grad_step], axis=1).astype(BF16)
    low_value_ref[...] = low_value
    low_small_ref[...] = low_small
    grad_in = (
        dot_nt(low_gate, w_gate_ref[...])
        + dot_nt(low_value, w_value_ref[...])
        + dot_nn(low_small, w_small_ref[...])
    )
    grad_in_ref[...] = grad_in.astype(BF16).reshape(grad_in_ref.shape)
    sums_in_ref[0:1, :] += jnp.sum(grad_in * normed_ref[...].astype(F32), axis=0, keepdims=True)
    gate_sum = jnp.sum(grad_normed * normed_gated, axis=0, keepdims=True)
    skip_sum = jnp.sum(grad_scanned * mixed, axis=0, keepdims=True)
    step_sum = jnp.sum(grad_step, axis=0, keepdims=True)
    for k in range(5):
        sums_ref[k : k + 1, :] += value_sums[k]
    sums_ref[5:6, :] += gate_sum
    sums_ref[6:7, :] += skip_sum
    sums_ref[7:8, :LANES] += step_sum
    sums_ref[7:8, LANES : 2 * LANES] += decay_sum
    for k in range(5):
        sums_ref[8 + k : 9 + k, : pair_sums[k].shape[1]] += pair_sums[k]


def whole_spec(shape):
    return pl.BlockSpec(shape, lambda *_: (0,) * len(shape))


def smem_spec():
    return pl.BlockSpec(memory_space=pltpu.SMEM)


def kernel_params():
    return pltpu.CompilerParams(vmem_limit_bytes=VMEM_BYTES)


def head_constants(head_count, head_width):
    width = head_count * head_width
    spread = np.zeros((LANES, width), np.float32)
    for h in range(head_count):
        spread[h, h * head_width : (h + 1) * head_width] = 1.0
        spread[h + 8, h * head_width : (h + 1) * head_width] = 1.0
    gather = np.zeros((width, LANES), np.float32)
    for h in range(head_count):
        gather[h * head_width : (h + 1) * head_width, h] = 1.0
    lower = np.tril(np.ones((SUB, SUB), np.float32))
    return (
        jnp.asarray(spread, BF16),
        jnp.asarray(gather, BF16),
        jnp.asarray(lower),
        jnp.asarray(lower.T),
    )


def run_forward(bounds, rows, weights, consts):
    micro_count, block_len = rows.shape[1], rows.shape[0] * rows.shape[2]
    blocks = block_len // ROWS
    per_block = ROWS // rows.shape[2]
    norm_in, w_value, w_gate, w_small, taps_value, taps_pair, heads, skip, norm_gate, w_out = weights
    spread, _, lower, _ = consts
    full = rows.shape[3]
    width = w_value.shape[1]
    pair_width = taps_pair.shape[1]
    length = micro_count * block_len
    subs = ROWS // SUB

    def by_rows(cols):
        return pl.BlockSpec((ROWS, cols), lambda b, i: (b * blocks + i, 0))

    row_block = pl.BlockSpec((per_block, None, rows.shape[2], full), lambda b, i: (i, b, 0, 0))
    wholes = [norm_in, w_value, w_gate, w_small, taps_value, taps_pair, heads, skip, norm_gate, w_out, spread, lower]
    widths = [width, width, width, pair_width, pair_width, LANES, width]
    return pl.pallas_call(
        partial(forward_kernel, width // LANES),
        grid=(micro_count, blocks),
        in_specs=[smem_spec(), row_block] + [whole_spec(item.shape) for item in wholes],
        out_specs=[by_rows(full)]
        + [by_rows(cols) for cols in widths]
        + [
            pl.BlockSpec((subs, LANES, width), lambda b, i: (b * blocks + i, 0, 0)),
            row_block,
            pl.BlockSpec((8, ROWS), lambda b, i: (0, b * blocks + i)),
        ],
        out_shape=[jax.ShapeDtypeStruct((length, full), BF16)]
        + [jax.ShapeDtypeStruct((length, cols), F32) for cols in widths]
        + [
            jax.ShapeDtypeStruct((length // SUB, LANES, width), F32),
            jax.ShapeDtypeStruct(rows.shape, BF16),
            jax.ShapeDtypeStruct((8, length), F32),
        ],
        scratch_shapes=[
            pltpu.VMEM((8, width), F32),
            pltpu.VMEM((8, pair_width), F32),
            pltpu.VMEM((LANES, width), F32),
        ],
        compiler_params=kernel_params(),
        name="forward",
    )(bounds, rows, *wholes)


def run_back(bounds, back, w_out, norm_gate, scanned, gate, square, live_ids):
    micro_count, block_len = back.shape[1], back.shape[0] * back.shape[2]
    blocks = block_len // ROWS
    per_block = ROWS // back.shape[2]
    width = gate.shape[1]
    length = micro_count * block_len
    by_rows = pl.BlockSpec((ROWS, width), lambda b, i: (b * blocks + i, 0))
    by_cols = pl.BlockSpec((8, ROWS), lambda b, i: (0, b * blocks + i))
    row_block = pl.BlockSpec((per_block, None, back.shape[2], back.shape[3]), lambda b, i: (i, b, 0, 0))
    return pl.pallas_call(
        partial(back_kernel, live_ids),
        grid=(micro_count, blocks),
        in_specs=[
            smem_spec(),
            row_block,
            whole_spec(w_out.shape),
            whole_spec(norm_gate.shape),
            by_rows,
            by_rows,
            by_cols,
        ],
        out_specs=[by_rows, by_cols],
        out_shape=[
            jax.ShapeDtypeStruct((length, width), F32),
            jax.ShapeDtypeStruct((8, length), F32),
        ],
        compiler_params=kernel_params(),
        name="back",
    )(bounds, back, w_out, norm_gate, scanned, gate, square)


def run_backward(bounds, stats, grad_normed, kept, weights, consts, rows_shape, live_ids, inner_full):
    micro_count, block_len = rows_shape[1], rows_shape[0] * rows_shape[2]
    blocks = block_len // ROWS
    per_block = ROWS // rows_shape[2]
    normed, gate, value, conv_value, pair, conv_pair, step, scanned, states = kept
    _, w_value, w_gate, w_small, taps_value, taps_pair, heads, skip, norm_gate, _ = weights
    spread, gather, lower, upper = consts
    full = rows_shape[3]
    width = gate.shape[1]
    pair_width = pair.shape[1]
    length = micro_count * block_len
    subs = ROWS // SUB

    def place(b, i):
        return b * blocks + blocks - 1 - i

    def by_rows(item):
        return pl.BlockSpec((ROWS, item.shape[1]), lambda b, i: (place(b, i), 0))

    row_block = pl.BlockSpec(
        (per_block, None, rows_shape[2], full), lambda b, i: (blocks - 1 - i, b, 0, 0)
    )
    rowwise = [stats, grad_normed, normed, gate, value, conv_value, pair, conv_pair, step, scanned]
    wholes = [w_value, w_gate, w_small, taps_value, taps_pair, heads, skip, norm_gate, spread, gather, lower, upper]
    outs = [
        jax.ShapeDtypeStruct((length, width), BF16),
        jax.ShapeDtypeStruct((length, width), BF16),
        jax.ShapeDtypeStruct((length, w_small.shape[0]), BF16),
        jax.ShapeDtypeStruct((length, width), BF16),
        jax.ShapeDtypeStruct(rows_shape, BF16),
        jax.ShapeDtypeStruct((16, width), F32),
        jax.ShapeDtypeStruct((8, full), F32),
    ]
    return pl.pallas_call(
        partial(backward_kernel, width // LANES, live_ids, inner_full),
        grid=(micro_count, blocks),
        in_specs=[smem_spec()]
        + [by_rows(item) for item in rowwise]
        + [pl.BlockSpec((subs, LANES, width), lambda b, i: (place(b, i), 0, 0))]
        + [whole_spec(item.shape) for item in wholes],
        out_specs=[by_rows(item) for item in outs[:4]]
        + [row_block, whole_spec(outs[5].shape), whole_spec(outs[6].shape)],
        out_shape=outs,
        scratch_shapes=[
            pltpu.VMEM((8, width), F32),
            pltpu.VMEM((8, pair_width), F32),
            pltpu.VMEM((LANES, width), F32),
        ],
        compiler_params=kernel_params(),
        name="backward",
    )(bounds, *rowwise, states, *wholes)


def deal_kernel(
    group_shift,
    place_ref,
    listed_ref,
    listed_cols_ref,
    own_ref,
    own_col_ref,
    tokens_ref,
    cotangent_ref,
    send_tokens_ref,
    send_cotangent_ref,
    send_map_ref,
    take_map_ref,
):
    start, group, target = place_ref[0], place_ref[1], place_ref[2]
    share = tokens_ref.shape[0]
    group_count = listed_cols_ref.shape[1]
    quota = share // group_count
    natural = start + iota((share, share), 1)
    found = []
    for g in range(group_count):
        hits = (listed_cols_ref[:, g : g + 1] == natural).astype(F32)
        found.append(jnp.sum(hits, axis=0, keepdims=True))
    pad = -group_count % 8
    found = jnp.concatenate(found + [jnp.zeros((pad, share), F32)] * (pad > 0), axis=0)
    before = (iota((share, share), 0) < iota((share, share), 1)).astype(BF16)
    rank = dot_nn(found.astype(BF16), before)
    slot = (iota(found.shape, 0) ^ group) * quota
    place = jnp.sum(found * (rank + slot.astype(F32)), axis=0, keepdims=True)
    send_map = (iota((share, share), 0).astype(F32) == place).astype(BF16)
    send_map_ref[...] = send_map
    own_row = jnp.broadcast_to(own_ref[...], (share, share))
    own_col = jnp.broadcast_to(own_col_ref[...], (share, share))
    src_row = lax.shift_right_logical(own_row, group_shift)
    src_col = lax.shift_right_logical(own_col, group_shift)
    ahead = ((src_row == src_col) & (own_row < own_col)).astype(F32)
    order = jnp.sum(ahead, axis=1, keepdims=True)
    wanted = ((src_col ^ target) * quota).astype(F32) + order
    take_map_ref[...] = (iota((share, share), 1).astype(F32) == wanted).astype(BF16)
    send_tokens_ref[...] = dot_nn(send_map, tokens_ref[...]).astype(BF16)
    send_cotangent_ref[...] = dot_nn(send_map, cotangent_ref[...]).astype(BF16)


def run_deal(place, listed, own, tokens, cotangent, group_len):
    share, width = tokens.shape
    vmem = pl.BlockSpec(memory_space=pltpu.VMEM)
    return pl.pallas_call(
        partial(deal_kernel, group_len.bit_length() - 1),
        in_specs=[smem_spec()] + [vmem] * 6,
        out_specs=[vmem] * 4,
        out_shape=[jax.ShapeDtypeStruct((share, width), BF16)] * 2
        + [jax.ShapeDtypeStruct((share, share), BF16)] * 2,
        compiler_params=kernel_params(),
        name="deal",
    )(place, listed, listed.T, own[None, :], own[:, None], tokens, cotangent)


def pick_kernel(transposed, map_ref, rows_ref, out_ref):
    dot = dot_tn if transposed else dot_nn
    out_ref[...] = dot(map_ref[...], rows_ref[...]).astype(BF16)


def run_pick(take_map, rows, transposed):
    vmem = pl.BlockSpec(memory_space=pltpu.VMEM)
    return pl.pallas_call(
        partial(pick_kernel, transposed),
        in_specs=[vmem] * 2,
        out_specs=vmem,
        out_shape=jax.ShapeDtypeStruct((take_map.shape[0], rows.shape[1]), BF16),
        compiler_params=kernel_params(),
        name="pick",
    )(take_map, rows)


def close_out_kernel(map_ref, dealt_ref, branch_ref, weight_ref, out_ref):
    shape = dealt_ref.shape
    out = dealt_ref[...].astype(F32) + weight_ref[...] * branch_ref[...].reshape(shape).astype(F32)
    out_ref[...] = dot_tn(map_ref[...], out.astype(BF16)).astype(BF16)


def close_back_kernel(map_ref, dealt_ref, back_ref, grad_ref, norm_in_ref, out_ref):
    shape = dealt_ref.shape
    x = dealt_ref[...].astype(F32)
    rms = lax.rsqrt(jnp.mean(x * x, axis=1, keepdims=True) + EPS)
    xhat = x * rms
    win = grad_ref[...].reshape(shape).astype(F32) * norm_in_ref[...].astype(F32)
    cross = jnp.mean(win * xhat, axis=1, keepdims=True)
    out = back_ref[...].astype(F32) + rms * (win - xhat * cross)
    out_ref[...] = dot_tn(map_ref[...], out.astype(BF16)).astype(BF16)


def run_close(body, take_map, *items):
    vmem = pl.BlockSpec(memory_space=pltpu.VMEM)
    return pl.pallas_call(
        body,
        in_specs=[vmem] * (1 + len(items)),
        out_specs=vmem,
        out_shape=jax.ShapeDtypeStruct(items[0].shape, BF16),
        compiler_params=kernel_params(),
        name="close",
    )(take_map, *items)


ALL = ("pair", "core", "row", "half", "near")
TEAM = ("row", "core", "near")


def make_perm(sizes, move):
    ranks = np.arange(int(np.prod(sizes))).reshape(sizes)
    return [
        (int(ranks[where]), int(ranks[move(*where)])) for where in np.ndindex(*sizes)
    ]


def turned(perm):
    return [(target, source) for source, target in perm]


def swap(v, perm):
    return lax.ppermute(v, ALL, perm)


def choose(bit, first, second, axis):
    return jnp.where(
        bit == 0,
        jnp.concatenate([first, second], axis=axis),
        jnp.concatenate([second, first], axis=axis),
    )


def per_device(
    sizes,
    tokens,
    cotangent,
    seq_lengths,
    token_order,
    norm_in,
    w_gate,
    w_value,
    w_pair,
    w_step,
    conv_value,
    bias_value,
    conv_pair,
    bias_pair,
    step_bias,
    decay_log,
    skip_gain,
    norm_gate,
    w_out,
):
    pair_count = sizes[0]
    group_count = sizes[0] * sizes[1]
    team_size = sizes[2] * sizes[3] * sizes[4]
    my_pair, my_core, my_row, my_half, my_near = [lax.axis_index(name) for name in ALL]
    group = my_pair * 2 + my_core
    target = my_pair * 2 + my_half
    member = my_row * (sizes[3] * sizes[4]) + my_half * sizes[4] + my_near
    seat = my_row * (sizes[3] * sizes[4]) + my_core * sizes[4] + my_near

    share_len, width_full = tokens.shape
    quota_len = share_len // group_count
    micro_count = seq_lengths.shape[0]
    piece_len = share_len // micro_count
    block_len = piece_len * team_size
    group_len = share_len * team_size
    width = w_gate.shape[1]
    inner_full = width * team_size
    head_count = step_bias.shape[0]
    head_width = width // head_count
    pair_part = w_pair.shape[1]
    pair_width = pair_part * team_size
    small_width = pair_width + LANES

    deal_perms = [
        make_perm(
            sizes,
            lambda p, c, r, h, n, e=e: (p ^ (e // 2), h, r, c ^ (e % 2), n),
        )
        for e in range(group_count)
    ]
    cross_perms = [
        make_perm(sizes, lambda p, c, r, h, n, f=f: (p, h, r, c ^ f, n)) for f in range(2)
    ]
    pair_bits = [k for k in range(pair_count.bit_length() - 1)]
    pair_perms = [
        make_perm(sizes, lambda p, c, r, h, n, k=k: (p ^ (1 << k), c, r, h, n))
        for k in pair_bits
    ]

    def gather_groups(block, axis):
        first = swap(block, cross_perms[0])
        second = swap(block, cross_perms[1])
        current = choose(my_half, first, second, axis)
        for k in pair_bits:
            other = swap(current, pair_perms[k])
            current = choose((my_pair >> k) & 1, current, other, axis)
        return current

    def scatter_groups(total, axis):
        current = total
        for k in reversed(pair_bits):
            half = current.shape[axis] // 2
            bit = (my_pair >> k) & 1
            kept = lax.dynamic_slice_in_dim(current, bit * half, half, axis)
            sent = lax.dynamic_slice_in_dim(current, (1 - bit) * half, half, axis)
            arrived = swap(sent.astype(BF16), pair_perms[k])
            current = kept + arrived.astype(F32)
        half = current.shape[axis] // 2
        first = lax.dynamic_slice_in_dim(current, my_half * half, half, axis)
        second = lax.dynamic_slice_in_dim(current, (1 - my_half) * half, half, axis)
        first = swap(first.astype(BF16), turned(cross_perms[0]))
        second = swap(second.astype(BF16), turned(cross_perms[1]))
        return first.astype(F32) + second.astype(F32)

    listed = lax.dynamic_index_in_dim(
        token_order.reshape(group_count, micro_count, team_size, piece_len),
        member,
        2,
        keepdims=False,
    ).reshape(group_count, share_len)
    seat_listed = lax.dynamic_slice(
        token_order.reshape(group_count, micro_count, team_size, piece_len),
        (target, 0, seat, 0),
        (1, micro_count, 1, piece_len),
    ).reshape(share_len)
    start = (group * team_size + member) * share_len
    send_tokens, send_cotangent, send_map, take_map = run_deal(
        jnp.stack([start, group, target]).astype(jnp.int32),
        listed,
        seat_listed,
        tokens,
        cotangent,
        group_len,
    )

    def deal(rows):
        pieces = [
            swap(rows[e * quota_len : (e + 1) * quota_len], deal_perms[e])
            for e in range(group_count)
        ]
        return run_pick(take_map, jnp.concatenate(pieces, axis=0), False)

    def undeal(rows):
        pieces = [
            swap(rows[e * quota_len : (e + 1) * quota_len], turned(deal_perms[e]))
            for e in range(group_count)
        ]
        return run_pick(send_map, jnp.concatenate(pieces, axis=0), True)

    bounds = lax.ppermute(
        seq_lengths.astype(F32), ALL, cross_perms[0]
    ).astype(jnp.int32)
    bounds = jnp.cumsum(bounds, axis=1).astype(jnp.int32)
    live_ids = seq_lengths.shape[1] - 1

    def regroup(item):
        return swap(item, cross_perms[0])

    dealt_tokens = deal(send_tokens)
    full_rows = lax.all_gather(
        dealt_tokens.reshape(micro_count, piece_len, width_full), TEAM, axis=0
    )
    dealt_back = deal(send_cotangent)
    full_back = lax.all_gather(
        dealt_back.reshape(micro_count, piece_len, width_full), TEAM, axis=0
    )

    value_w = gather_groups(w_value, 0)
    gate_w = gather_groups(w_gate, 0)
    small_pad = -(pair_part + head_count) % 16
    small_own = jnp.concatenate(
        [w_pair.T, w_step.T, jnp.zeros((small_pad, w_pair.shape[0]), BF16)], axis=0
    )
    small_w = gather_groups(small_own, 1)
    pair_w = lax.all_gather(small_w[:pair_part], TEAM, axis=0, tiled=True)
    step_w = jnp.pad(
        small_w[pair_part : pair_part + head_count], ((0, LANES - head_count), (0, 0))
    )
    small_w = jnp.concatenate([pair_w, step_w], axis=0)
    out_w = gather_groups(w_out, 1)

    def pack_taps(taps, bias):
        return jnp.concatenate(
            [taps, bias[None, :], jnp.zeros((3, bias.shape[0]), F32)], axis=0
        )

    heads_own = jnp.pad(jnp.stack([step_bias, decay_log, skip_gain]), ((0, 5), (0, 0)))
    local_params = jnp.concatenate(
        [
            pack_taps(conv_value, bias_value),
            jnp.broadcast_to(norm_gate[None, :], (8, width)),
            jnp.pad(heads_own, ((0, 0), (0, width - head_count))),
            jnp.pad(pack_taps(conv_pair, bias_pair), ((0, 0), (0, width - pair_part))),
        ],
        axis=0,
    )
    local_params = regroup(local_params)
    taps_value = local_params[:8]
    norm_gate_row = local_params[8:9]
    heads_got = local_params[16:24, :head_count]
    skip_row = jnp.repeat(heads_got[2:3], head_width, axis=1)
    heads_row = jnp.pad(
        jnp.concatenate([heads_got[0:1], -jnp.exp(heads_got[1:2])], axis=0),
        ((0, 6), (0, LANES - head_count)),
    )
    taps_pair = lax.all_gather(local_params[24:32, :pair_part], TEAM, axis=1, tiled=True)

    consts = head_constants(head_count, head_width)
    weights = (
        norm_in[None, :],
        value_w,
        gate_w,
        small_w,
        taps_value,
        taps_pair,
        heads_row,
        skip_row,
        norm_gate_row,
        out_w,
    )
    outs = run_forward(bounds, full_rows, weights, consts)
    kept = outs[:9]
    partial_out, square = outs[9], outs[10]
    branch = lax.psum_scatter(partial_out, TEAM, scatter_dimension=0)
    normed, gate, scanned = kept[0], kept[1], kept[7]
    grad_normed, stats = run_back(
        bounds, full_back, out_w, norm_gate_row, scanned, gate, square, live_ids
    )
    stats = lax.psum(stats[:2], TEAM)
    stats_cols = jnp.pad(stats.T, ((0, 0), (0, 6)))
    low_gate, low_value, low_small, normed_out, grad_in, sums, sums_in = run_backward(
        bounds, stats_cols, grad_normed, kept, weights, consts, full_rows.shape, live_ids, inner_full
    )
    grad_in = lax.psum_scatter(grad_in, TEAM, scatter_dimension=0)

    flat_back = (
        jnp.swapaxes(full_back, 0, 1).reshape(micro_count * block_len, width_full)
    )
    g_out = scatter_groups(dot_tn(normed_out, flat_back), 1)
    g_gate = scatter_groups(dot_tn(normed, low_gate), 0)
    g_value = scatter_groups(dot_tn(normed, low_value), 0)
    g_small = dot_tn(low_small, normed)
    g_pair = lax.psum_scatter(
        g_small[:pair_width].astype(BF16), TEAM, scatter_dimension=0, tiled=True
    )
    g_small = jnp.concatenate(
        [
            g_pair.astype(F32),
            g_small[pair_width : pair_width + head_count],
            jnp.zeros((small_pad, width_full), F32),
        ],
        axis=0,
    )
    g_small = scatter_groups(g_small, 1)
    g_pair = g_small[:pair_part].T
    g_step = g_small[pair_part : pair_part + head_count].T

    sums_group = lax.psum(sums[:8], ("pair", "half"))
    sums_group = swap(sums_group, turned(cross_perms[0]))
    sums_team = lax.psum((sums[8:13, :pair_width], sums_in[0]), ALL)
    pair_sums = lax.dynamic_slice_in_dim(sums_team[0], member * pair_part, pair_part, 1)
    g_norm_in = sums_team[1] / norm_in.astype(F32)
    g_skip = jnp.sum(sums_group[6].reshape(head_count, head_width), axis=1)

    live_start = seat * piece_len
    local_stats = lax.dynamic_slice_in_dim(
        stats.reshape(2, micro_count, block_len)[0], live_start, piece_len, 1
    )
    local_places = live_start + jnp.arange(piece_len, dtype=jnp.int32)
    local_seg = jnp.sum(
        (local_places[None, :, None] >= bounds[:, None, :]).astype(jnp.int32), axis=2
    )
    weight = jnp.where(
        local_seg < live_ids, lax.rsqrt(local_stats / inner_full + EPS), 0.0
    ).reshape(share_len, 1)
    block_out = undeal(run_close(close_out_kernel, take_map, dealt_tokens, branch, weight))
    grad_tokens = undeal(
        run_close(
            close_back_kernel, take_map, dealt_tokens, dealt_back, grad_in, norm_in[None, :]
        )
    )
    return (
        block_out,
        grad_tokens,
        g_norm_in,
        g_gate,
        g_value,
        g_pair,
        g_step,
        sums_group[0:4],
        sums_group[4],
        pair_sums[0:4],
        pair_sums[4],
        sums_group[7, :head_count],
        sums_group[7, LANES : LANES + head_count],
        g_skip,
        sums_group[5],
        g_out,
    )


def solution(mesh):
    shape = mesh.devices.shape
    sizes = (shape[0] // 2, 2, shape[1], 2, shape[2] // 2)
    fine = jax.sharding.Mesh(mesh.devices.reshape(sizes), ALL)
    dp, team = ("pair", "core"), ("row", "half", "near")
    everything = ("pair", "core", "row", "half", "near")
    placed = (
        P(everything, None),
        P(everything, None),
        P(dp, None),
        P(),
        P(),
        P(dp, team),
        P(dp, team),
        P(dp, team),
        P(dp, team),
        P(None, team),
        P(team),
        P(None, team),
        P(team),
        P(team),
        P(team),
        P(team),
        P(team),
        P(team, dp),
    )
    return jax.shard_map(
        partial(per_device, sizes),
        mesh=fine,
        in_specs=placed,
        out_specs=(
            P(everything, None),
            P(everything, None),
            P(),
            P(dp, team),
            P(dp, team),
            P(dp, team),
            P(dp, team),
            P(None, team),
            P(team),
            P(None, team),
            P(team),
            P(team),
            P(team),
            P(team),
            P(team),
            P(team, dp),
        ),
        check_vma=False,
    )
```

time: 1990 us -> 715 us (0.36); the launches traced: 1960 us -> 714 us
  local copies, waits for them, and re-layouts: 566 us -> 33.8 us
  other arithmetic: 380 us -> 20.5 us
  matrix products: 306 us -> 17.7 us
  waiting for transfers between devices: 529 us -> 262 us
  Pallas kernels: 0 us -> 111 us
  starting transfers between devices: 15.1 us -> 77.2 us
  blocking collectives: 143 us -> 177 us
    dot_general x142 -> x4, matrix products: 306 us -> 17.7 us  [dot_tn(): lax.dot_general(a, b, (((0,), (0,)), ((), ())), preferred_element_type=F32)]
    reduce_scatter x8 -> x3, waiting for transfers between devices: 391 us -> 146 us  [the longest x1 126 us: per_device(): grad_in = lax.psum_scatter(grad_in, TEAM, scatter_dimension=0)]
    dynamic_update_slice x40 -> x0, local copies, waits for them, and re-layouts: 182 us -> none  [ssd_scan(): lax.scan(jax.checkpoint(one_block), start_carry, blocks)]
    another operation x76 -> x3, other arithmetic: 162 us -> 1.33 us  [the longest x1 0.73 us: per_device(): bounds = jnp.cumsum(bounds, axis=1).astype(jnp.int32)]
    ppermute x0 -> x43, waiting for transfers between devices: none -> 115 us  [the longest x42 108 us: swap(): return lax.ppermute(v, ALL, perm)]
    pallas_call x0 -> x10, Pallas kernels: none -> 111 us  [the longest x1 44.2 us: run_backward(): pl.pallas_call(partial(backward_kernel, width // LANES, live_ids, inner_f...]
    another operation x129 -> x3, local copies, waits for them, and re-layouts: 107 us -> 2.14 us  [the longest x2 2.06 us: run_deal(): own[:, None]]
    all_gather x7 -> x2, waiting for transfers between devices: 80.8 us -> 0.02 us  [the longest x1 0.02 us: per_device(): lax.all_gather(dealt_back.reshape(micro_count, piece_len, width_full), TE...]
  transfers between devices with their start and end apart: 21 -> 48, of which waited for: 14 -> 24; matrix products, arithmetic and copies ran while one was open for 25% -> 7% of each run, Pallas kernels for 0% -> 7%
where the time goes in v1:
time: 715 us; the launch traced here: 714 us
  waiting for transfers between devices  262 us (37%)
  blocking collectives  177 us (25%)
  Pallas kernels  111 us (16%)
  starting transfers between devices  77.2 us (11%)
  local copies, waits for them, and re-layouts  33.8 us (5%)
  other arithmetic  20.5 us (3%)
  matrix products  17.7 us (2%)
  between operations  14.6 us (2%)
    reduce_scatter x1, waiting for transfers between devices, per_device(): grad_in = lax.psum_scatter(grad_in, TEAM, scatter_dimension=0)  126 us
    ppermute x42, waiting for transfers between devices, swap(): return lax.ppermute(v, ALL, perm)  108 us
    ppermute x42, starting transfers between devices, swap(): return lax.ppermute(v, ALL, perm)  75.1 us
    psum x1, blocking collectives, per_device(): stats = lax.psum(stats[:2], TEAM)  69.3 us
    pallas_call x1, Pallas kernels, run_backward(): pl.pallas_call(partial(backward_kernel, width // LANES, live_ids, inner_f...  44.2 us
    psum x1, blocking collectives, per_device(): sums_team = lax.psum((sums[8:13, :pair_width], sums_in[0]), ALL)  39.5 us
    pallas_call x1, Pallas kernels, run_forward(): pl.pallas_call(partial(forward_kernel, width // LANES), grid=(micro_count...  35.5 us
    all_gather x1, blocking collectives, per_device(): pair_w = lax.all_gather(small_w[:pair_part], TEAM, axis=0, tiled=True)  33.4 us
  transfers between devices with their start and end apart: 48, of which 24 were waited for; matrix products, arithmetic and copies ran while one was open for 7% of the time, Pallas kernels for 7%

profile of v1, /device:TPU:1, one launch (start us, length us, event | category | flops | bytes accessed | tf_op | source)
XLA Modules:
  0.0 713.6 jit_solution(9858565570490621770)
XLA Ops:
  11.5 3.6 deal.1
  16.3 2.7 collective-permute-start.3
  19.0 2.1 collective-permute-start.2
  21.9 1.9 collective-permute-start
  23.9 9.0 %collective-permute-done.3 = bf16[64,1536]{1,0:T(8,128)(2,1)S(1)} collective-permute-done((bf16[64,1536]{1,0:T(8,128)(2,1)S(1)}, bf16[64,1536]{1,0:T(8,128)(2,1)S(1)}, u32[]{:S(2)}, u32[]{:S(2)}) %collective-permute-start.3) | collective-permute-done | bytes 196640 | tf_op jit(solution)/shard_map/ppermute | solution.py:776
  32.9 2.4 collective-permute-done.2
  35.3 2.3 collective-permute-done.1
  39.3 2.5 pick.4.dealt_ref
  42.2 1.4 collective-permute-start.19
  43.7 4.1 collective-permute-start.18
  47.8 10.0 %collective-permute-done.21 = bf16[64,1536]{1,0:T(8,128)(2,1)S(1)} collective-permute-done((bf16[64,1536]{1,0:T(8,128)(2,1)S(1)}, bf16[64,1536]{1,0:T(8,128)(2,1)S(1)}, u32[]{:S(2)}, u32[]{:S(2)}) %collective-permute-start.21) | collective-permute-done | bytes 196640 | tf_op jit(solution)/shard_map/ppermute | solution.py:776
  57.8 1.7 collective-permute-done.20
  59.5 2.1 collective-permute-done.19
  63.2 2.6 pick.5.back_ref
  66.0 1.9 collective-permute-start.5
  68.1 4.5 collective-permute-start.11
  72.6 1.9 collective-permute-start.4
  75.5 7.3 %collective-permute-done.4 = f32[2,4]{1,0:T(2,128)S(1)} collective-permute-done((f32[2,4]{1,0:T(2,128)S(1)}, f32[2,4]{1,0:T(2,128)S(1)}, u32[]{:S(2)}, u32[]{:S(2)}) %collective-permute-start.4) | collective-permute-done | bytes 64 | tf_op jit(solution)/shard_map/ppermute | solution.py:907
  83.5 1.9 collective-permute-start.8
  85.4 4.5 collective-permute-start.14
  90.0 9.7 %collective-permute-done.14 = f32[32,384]{1,0:T(8,128)S(1)} collective-permute-done((f32[32,384]{1,0:T(8,128)S(1)}, f32[32,384]{1,0:T(8,128)S(1)}, u32[]{:S(2)}, u32[]{:S(2)}) %collective-permute-start.14) | collective-permute-done | bytes 49184 | tf_op jit(solution)/shard_map/ppermute | solution.py:776
  100.8 19.9 %all-gather = f32[8,32,8]{1,2,0:T(8,128)S(1)} all-gather(f32[1,32,8]{1,2,0:T(8,128)S(1)} %slice_bitcast_fusion.2), channel_id=1, replica_groups=mesh['pair'=2,'core'=2,'row'=2,'half'=2,'near'=2] {'row','core','near'}, dimensions={0}, use_global_device_ids=true | all-gather | bytes 9216 | tf_op jit(solution)/shard_map/all_gather | solution.py:963
  124.2 3.7 collective-permute-start.15
  128.6 33.4 %all_gather.13 = bf16[256,1536]{1,0:T(8,128)(2,1)S(1)} all-gather(bf16[32,1536]{1,0:T(8,128)(2,1)S(1)} %slice.173), channel_id=1, replica_groups=mesh['pair'=2,'core'=2,'row'=2,'half'=2,'near'=2] {'row','core','near'}, dimensions={0}, use_global_device_ids=true | all-gather | bytes 884736 | tf_op jit(solution)/shard_map/all_gather | solution.py:932
  166.5 10.5 %collective-permute-done.10 = bf16[768,384]{1,0:T(8,128)(2,1)S(1)} collective-permute-done((bf16[768,384]{1,0:T(8,128)(2,1)S(1)}, bf16[768,384]{1,0:T(8,128)(2,1)S(1)}, u32[]{:S(2)}, u32[]{:S(2)}) %collective-permute-start.10) | collective-permute-done | bytes 589856 | tf_op jit(solution)/shard_map/ppermute | solution.py:776
  177.0 1.4 maximum_select_fusion.1.w_gate_ref
  178.4 11.2 %collective-permute-done.17 = bf16[384,768]{1,0:T(8,128)(2,1)S(1)} collective-permute-done((bf16[384,768]{1,0:T(8,128)(2,1)S(1)}, bf16[384,768]{1,0:T(8,128)(2,1)S(1)}, u32[]{:S(2)}, u32[]{:S(2)}) %collective-permute-start.17) | collective-permute-done | bytes 589856 | tf_op jit(solution)/shard_map/ppermute | solution.py:776
  191.0 35.5 %forward.1 = (bf16[2048,1536]{1,0:T(8,128)(2,1)}, f32[2048,384]{1,0:T(8,128)}, f32[2048,384]{1,0:T(8,128)}, f32[2048,384]{1,0:T(8,128)}, f32[2048,256]{1,0:T(8,1...) custom-call(s32[2,4]{1,0:T(2,128)} %reduce_window_sum.11.bounds_ref,, ...), custom_call_target="tpu_custom_call" | custom-call | tf_op jit(solution)/shard_map/forward/pallas_call | solution.py:545
  226.5 11.0 %back.1 = (f32[2048,384]{1,0:T(8,128)}, f32[8,2048]{1,0:T(8,128)}) custom-call(s32[2,4]{1,0:T(2,128)} %reduce_window_sum.11.bounds_ref, bf16[8,2,128,1536]{3,2,1,0:T(8,128)(2,1)} %all-gather.6.cloned.1.call-done.back_ref, bf16[384,1536]{1,0:T(8,128)(2,1)} %maximum_select_fusion.2.w_out_ref, f32[1,384]{1,0:T(1,128)} %slice.180.norm_gate_ref, ...), custom_call_target="tpu_custom_call" | custom-call | tf_op jit(solution)/shard_map/back/pallas_call | solution.py:582
  238.7 69.3 %psum.28 = f32[2,2048]{0,1:T(8,128)S(1)} all-reduce(f32[2,2048]{0,1:T(8,128)S(1)} %copy.59), channel_id=1, replica_groups=mesh['pair'=2,'core'=2,'row'=2,'half'=2,'near'=2] {'row','core','near'}, use_global_device_ids=true, to_apply=%region_3.4 | all-reduce | flops 4096 | bytes 32768 | tf_op jit(solution)/shard_map/psum | solution.py:986
  309.2 44.2 %backward.1 = (bf16[2048,384]{1,0:T(8,128)(2,1)}, bf16[2048,384]{1,0:T(8,128)(2,1)}, bf16[2048,384]{1,0:T(8,128)(2,1)}, bf16[2048,384]{1,0:T(8,128)(2,1)}, bf16[...) custom-call(s32[2,4]{1,0:T(2,128)} %reduce_window_sum.11.bounds_ref, f32[2048,8]{1,0:T(8,128)} %pad.29.stats_ref, ...), custom_call_target="tpu_custom_call" | custom-call | tf_op jit(solution)/shard_map/backward/pallas_call | solution.py:637
  353.4 5.4 fusion.14
  358.9 2.4 slice.216
  366.3 6.1 fusion.12
  374.1 3.5 fusion.13
  377.6 1.4 copy-done.1
  380.8 14.9 %psum.30 = f32[8,384]{1,0:T(8,128)} all-reduce(f32[8,384]{1,0:T(8,128)S(1)} %slice.163), channel_id=1, replica_groups=mesh['pair'=2,'core'=2,'row'=2,'half'=2,'near'=2] {'pair','half'}, use_global_device_ids=true, to_apply=%region_7.8 | all-reduce | flops 3072 | bytes 24576 | tf_op jit(solution)/shard_map/psum | solution.py:1015
  395.7 6.0 collective-permute-start.39
  402.5 39.5 %all-reduce.6 = (f32[1536]{0:T(1024)S(1)}, f32[5,256]{1,0:T(8,128)S(1)}) all-reduce(f32[1536]{0:T(1024)S(1)} %slice_reduce_fusion.1, f32[5,256]{1,0:T(8,128)S(1)} %copy-done.6), channel_id=1, replica_groups=mesh['pair'=2,'core'=2,'row'=2,'half'=2,'near'=2] {'pair','core','row','..., use_global_device_ids=true, to_apply=%region_5.6 | all-reduce | flops 2816 | bytes 22528 | tf_op jit(solution)/shard_map/psum | solution.py:1017
  442.6 3.5 copy.61
  446.8 2.6 fusion.15
  455.5 1.5 convert_add_fusion.2
  457.1 1.5 collective-permute-start.32
  458.6 5.1 collective-permute-start.31
  464.1 1.9 collective-permute-start.34
  468.8 3.9 collective-permute-start.41
  472.7 5.6 collective-permute-done.31
  481.7 6.0 collective-permute-done.35
  487.7 9.5 %collective-permute-done.34 = bf16[384,384]{1,0:T(8,128)(2,1)S(1)} collective-permute-done((bf16[384,384]{1,0:T(8,128)(2,1)S(1)}, bf16[384,384]{1,0:T(8,128)(2,1)S(1)}, u32[]{:S(2)}, u32[]{:S(2)}) %collective-permute-start.34) | collective-permute-done | bytes 294944 | tf_op jit(solution)/shard_map/ppermute | solution.py:776
  498.2 5.3 collective-permute-start.37
  503.5 3.2 collective-permute-done.42
  506.7 9.5 %collective-permute-done.41 = bf16[384,384]{1,0:T(8,128)(2,1)S(1)} collective-permute-done((bf16[384,384]{1,0:T(8,128)(2,1)S(1)}, bf16[384,384]{1,0:T(8,128)(2,1)S(1)}, u32[]{:S(2)}, u32[]{:S(2)}) %collective-permute-start.41) | collective-permute-done | bytes 294944 | tf_op jit(solution)/shard_map/ppermute | solution.py:776
  519.8 19.9 %reduce-scatter.4.cloned.1.call-done = bf16[1,2,128,1536]{3,2,1,0:T(8,128)(2,1)} async-done(((bf16[8,2,128,1536]{3,2,1,0:T(8,128)(2,1)}), bf16[1,2,128,1536]{3,2,1,0:T(8,128)(2,1)}) %reduce-scatter.4.cloned.1.call-update) | async-done | bytes 786448 | tf_op jit(solution)/shard_map/reduce_scatter | solution.py:981
  539.7 2.8 close.2
  543.8 3.1 collective-permute-start.25
  547.9 3.5 collective-permute-start.22
  551.4 126.1 %reduce-scatter.6.cloned.1.call-done = bf16[1,2,128,1536]{3,2,1,0:T(8,128)(2,1)} async-done(((bf16[8,2,128,1536]{3,2,1,0:T(8,128)(2,1)}), bf16[1,2,128,1536]{3,2,1,0:T(8,128)(2,1)}) %reduce-scatter.6.cloned.1.call-update) | async-done | bytes 786448 | tf_op jit(solution)/shard_map/reduce_scatter | solution.py:991
  677.6 3.5 close.3
  683.6 2.8 collective-permute-start.28
  686.5 2.5 collective-permute-start.26
  690.0 2.5 pick.6
  692.5 7.2 %collective-permute-done.28 = bf16[64,1536]{1,0:T(8,128)(2,1)S(1)} collective-permute-done((bf16[64,1536]{1,0:T(8,128)(2,1)S(1)}, bf16[64,1536]{1,0:T(8,128)(2,1)S(1)}, u32[]{:S(2)}, u32[]{:S(2)}) %collective-permute-start.28) | collective-permute-done | bytes 196640 | tf_op jit(solution)/shard_map/ppermute | solution.py:776
  699.6 3.9 collective-permute-done.26
  704.5 2.5 pick.7
  (217 shorter events, 59.8 us)
Async XLA Ops:
  7.2 183.8 %all-gather.4.cloned.1.call-start = ((), (), s32[]{:S(2)}) async-start(), calls=%async_computation.3 | async-start | bytes 7077888 | tf_op jit(solution)/shard_map/all_gather | solution.py:917
  16.3 16.6 %collective-permute-start.3 = (bf16[64,1536]{1,0:T(8,128)(2,1)S(1)}, bf16[64,1536]{1,0:T(8,128)(2,1)S(1)}, u32[]{:S(2)}, u32[]{:S(2)}) collective-permute-start(bf16[64,1536]{1,0:T(8,128)(2,1)S(1)} %get-tuple-element.82), channel_id=1, source_target_pairs={{0,18},{1,19},{2,26},{3,27},{4,22},{5,23},{6,30},{7,31},{8,16},{9,... | collective-permute-start | bytes 589832 | tf_op jit(solution)/shard_map/ppermute | solution.py:776
  19.0 16.2 %collective-permute-start.2 = (bf16[64,1536]{1,0:T(8,128)(2,1)S(1)}, bf16[64,1536]{1,0:T(8,128)(2,1)S(1)}, u32[]{:S(2)}, u32[]{:S(2)}) collective-permute-start(bf16[64,1536]{1,0:T(8,128)(2,1)S(1)} %get-tuple-element.83), channel_id=1, source_target_pairs={{0,16},{1,17},{2,24},{3,25},{4,20},{5,21},{6,28},{7,29},{8,18},{9,... | collective-permute-start | bytes 589832 | tf_op jit(solution)/shard_map/ppermute | solution.py:776
  21.1 16.4 %collective-permute-start.1 = (bf16[64,1536]{1,0:T(8,128)(2,1)S(1)}, bf16[64,1536]{1,0:T(8,128)(2,1)S(1)}, u32[]{:S(2)}, u32[]{:S(2)}) collective-permute-start(bf16[64,1536]{1,0:T(8,128)(2,1)S(1)} %get-tuple-element.84), channel_id=1, source_target_pairs={{0,2},{1,3},{2,10},{3,11},{4,6},{5,7},{6,14},{7,15},{8,0},{9,1},{1... | collective-permute-start | bytes 589832 | tf_op jit(solution)/shard_map/ppermute | solution.py:776
  21.9 16.4 %collective-permute-start = (bf16[64,1536]{1,0:T(8,128)(2,1)S(1)}, bf16[64,1536]{1,0:T(8,128)(2,1)S(1)}, u32[]{:S(2)}, u32[]{:S(2)}) collective-permute-start(bf16[64,1536]{1,0:T(8,128)(2,1)S(1)} %get-tuple-element.81), channel_id=1, source_target_pairs={{0,0},{1,1},{2,8},{3,9},{4,4},{5,5},{6,12},{7,13},{8,2},{9,3},{10,... | collective-permute-start | bytes 589832 | tf_op jit(solution)/shard_map/ppermute | solution.py:776
  41.8 184.7 %all-gather.6.cloned.1.call-start = ((), (), s32[]{:S(2)}) async-start(), calls=%async_computation.5 | async-start | bytes 7077888 | tf_op jit(solution)/shard_map/all_gather | solution.py:921
  41.9 15.9 %collective-permute-start.21 = (bf16[64,1536]{1,0:T(8,128)(2,1)S(1)}, bf16[64,1536]{1,0:T(8,128)(2,1)S(1)}, u32[]{:S(2)}, u32[]{:S(2)}) collective-permute-start(bf16[64,1536]{1,0:T(8,128)(2,1)S(1)} %get-tuple-element.78), channel_id=1, source_target_pairs={{0,18},{1,19},{2,26},{3,27},{4,22},{5,23},{6,30},{7,31},{8,16},{9,... | collective-permute-start | bytes 589832 | tf_op jit(solution)/shard_map/ppermute | solution.py:776
  42.0 17.5 %collective-permute-start.20 = (bf16[64,1536]{1,0:T(8,128)(2,1)S(1)}, bf16[64,1536]{1,0:T(8,128)(2,1)S(1)}, u32[]{:S(2)}, u32[]{:S(2)}) collective-permute-start(bf16[64,1536]{1,0:T(8,128)(2,1)S(1)} %get-tuple-element.79), channel_id=1, source_target_pairs={{0,16},{1,17},{2,24},{3,25},{4,20},{5,21},{6,28},{7,29},{8,18},{9,... | collective-permute-start | bytes 589832 | tf_op jit(solution)/shard_map/ppermute | solution.py:776
  42.2 19.3 %collective-permute-start.19 = (bf16[64,1536]{1,0:T(8,128)(2,1)S(1)}, bf16[64,1536]{1,0:T(8,128)(2,1)S(1)}, u32[]{:S(2)}, u32[]{:S(2)}) collective-permute-start(bf16[64,1536]{1,0:T(8,128)(2,1)S(1)} %get-tuple-element.80), channel_id=1, source_target_pairs={{0,2},{1,3},{2,10},{3,11},{4,6},{5,7},{6,14},{7,15},{8,0},{9,1},{1... | collective-permute-start | bytes 589832 | tf_op jit(solution)/shard_map/ppermute | solution.py:776
  43.7 18.5 %collective-permute-start.18 = (bf16[64,1536]{1,0:T(8,128)(2,1)S(1)}, bf16[64,1536]{1,0:T(8,128)(2,1)S(1)}, u32[]{:S(2)}, u32[]{:S(2)}) collective-permute-start(bf16[64,1536]{1,0:T(8,128)(2,1)S(1)} %get-tuple-element.77), channel_id=1, source_target_pairs={{0,0},{1,1},{2,8},{3,9},{4,4},{5,5},{6,12},{7,13},{8,2},{9,3},{10,... | collective-permute-start | bytes 589832 | tf_op jit(solution)/shard_map/ppermute | solution.py:776
  63.1 9.5 %copy-start.17 = (s32[2,4]{1,0:T(2,128)S(1)}, s32[2,4]{1,0:T(2,128)}, u32[]{:S(2)}) copy-start(s32[2,4]{1,0:T(2,128)} %param.24) | copy-start | bytes 100
  63.1 11.5 %copy-start.14 = (f32[4,32]{1,0:T(4,128)S(1)}, f32[4,32]{1,0:T(4,128)}, u32[]{:S(2)}) copy-start(f32[4,32]{1,0:T(4,128)} %param.33) | copy-start | bytes 1540
  63.1 11.5 %copy-start.19 = (f32[32]{0:T(128)S(1)}, f32[32]{0:T(128)}, u32[]{:S(2)}) copy-start(f32[32]{0:T(128)} %param.34) | copy-start | bytes 388
  63.1 11.6 %copy-start.20 = (f32[6]{0:T(128)S(1)}, f32[6]{0:T(128)}, u32[]{:S(2)}) copy-start(f32[6]{0:T(128)} %param.37) | copy-start | bytes 76
  63.1 11.6 %copy-start.21 = (f32[6]{0:T(128)S(1)}, f32[6]{0:T(128)}, u32[]{:S(2)}) copy-start(f32[6]{0:T(128)} %param.36) | copy-start | bytes 76
  63.2 11.6 %copy-start.22 = (f32[6]{0:T(128)S(1)}, f32[6]{0:T(128)}, u32[]{:S(2)}) copy-start(f32[6]{0:T(128)} %param.35) | copy-start | bytes 76
  63.2 11.6 %copy-start.10 = (bf16[1536]{0:T(1024)(128)(2,1)S(1)}, bf16[1536]{0:T(1024)(128)(2,1)}, u32[]{:S(2)}) copy-start(bf16[1536]{0:T(1024)(128)(2,1)} %param.26) | copy-start | bytes 9220
  63.2 12.2 %copy-start.16 = (f32[384]{0:T(512)S(1)}, f32[384]{0:T(512)}, u32[]{:S(2)}) copy-start(f32[384]{0:T(512)} %param.32) | copy-start | bytes 4612
  63.2 12.2 %copy-start.15 = (f32[384]{0:T(512)S(1)}, f32[384]{0:T(512)}, u32[]{:S(2)}) copy-start(f32[384]{0:T(512)} %param.38) | copy-start | bytes 4612
  63.2 12.2 %copy-start.13 = (f32[4,384]{1,0:T(4,128)S(1)}, f32[4,384]{1,0:T(4,128)}, u32[]{:S(2)}) copy-start(f32[4,384]{1,0:T(4,128)} %param.31) | copy-start | bytes 18436
  63.2 19.6 %copy-start.25 = (bf16[384,384]{1,0:T(8,128)(2,1)S(1)}, bf16[384,384]{1,0:T(8,128)(2,1)}, u32[]{:S(2)}) copy-start(bf16[384,384]{1,0:T(8,128)(2,1)} %param.27) | copy-start | bytes 884740
  63.2 60.6 %copy-start.26 = (bf16[384,384]{1,0:T(8,128)(2,1)S(1)}, bf16[384,384]{1,0:T(8,128)(2,1)}, u32[]{:S(2)}) copy-start(bf16[384,384]{1,0:T(8,128)(2,1)} %param.39) | copy-start | bytes 884740
  65.8 413.3 %reduce-scatter.8.cloned.1.call-start = ((), (), s32[]{:S(2)}) async-start(), calls=%async_computation.7 | async-start | bytes 884736 | tf_op jit(solution)/shard_map/reduce_scatter | solution.py:1000
  65.9 58.3 %collective-permute-start.6 = (bf16[384,384]{1,0:T(8,128)(2,1)S(1)}, bf16[384,384]{1,0:T(8,128)(2,1)S(1)}, u32[]{:S(2)}, u32[]{:S(2)}) collective-permute-start(bf16[384,384]{1,0:T(8,128)(2,1)S(1)} %copy-done.24), channel_id=1, source_target_pairs={{0,2},{1,3},{2,10},{3,11},{4,6},{5,7},{6,14},{7,15},{8,0},{9,1},{1... | collective-permute-start | bytes 884744 | tf_op jit(solution)/shard_map/ppermute | solution.py:776
  66.0 62.0 %collective-permute-start.5 = (bf16[384,384]{1,0:T(8,128)(2,1)S(1)}, bf16[384,384]{1,0:T(8,128)(2,1)S(1)}, u32[]{:S(2)}, u32[]{:S(2)}) collective-permute-start(bf16[384,384]{1,0:T(8,128)(2,1)S(1)} %copy-done.24), channel_id=1, source_target_pairs={{0,0},{1,1},{2,8},{3,9},{4,4},{5,5},{6,12},{7,13},{8,2},{9,3},{10,... | collective-permute-start | bytes 884744 | tf_op jit(solution)/shard_map/ppermute | solution.py:776
  68.0 15.5 %collective-permute-start.12 = (bf16[48,384]{1,0:T(8,128)(2,1)S(1)}, bf16[48,384]{1,0:T(8,128)(2,1)S(1)}, u32[]{:S(2)}, u32[]{:S(2)}) collective-permute-start(bf16[48,384]{1,0:T(8,128)(2,1)S(1)} %maximum_maximum_fusion.1), channel_id=1, source_target_pairs={{0,2},{1,3},{2,10},{3,11},{4,6},{5,7},{6,14},{7,15},{8,0},{9,1},{1... | collective-permute-start | bytes 110600 | tf_op jit(solution)/shard_map/ppermute | solution.py:776
  68.1 17.4 %collective-permute-start.11 = (bf16[48,384]{1,0:T(8,128)(2,1)S(1)}, bf16[48,384]{1,0:T(8,128)(2,1)S(1)}, u32[]{:S(2)}, u32[]{:S(2)}) collective-permute-start(bf16[48,384]{1,0:T(8,128)(2,1)S(1)} %maximum_maximum_fusion.1), channel_id=1, source_target_pairs={{0,0},{1,1},{2,8},{3,9},{4,4},{5,5},{6,12},{7,13},{8,2},{9,3},{10,... | collective-permute-start | bytes 110600 | tf_op jit(solution)/shard_map/ppermute | solution.py:776
  72.6 10.1 %collective-permute-start.4 = (f32[2,4]{1,0:T(2,128)S(1)}, f32[2,4]{1,0:T(2,128)S(1)}, u32[]{:S(2)}, u32[]{:S(2)}) collective-permute-start(f32[2,4]{1,0:T(2,128)S(1)} %convert_element_type.100), channel_id=1, source_target_pairs={{0,0},{1,1},{2,8},{3,9},{4,4},{5,5},{6,12},{7,13},{8,2},{9,3},{10,... | collective-permute-start | bytes 104 | tf_op jit(solution)/shard_map/ppermute | solution.py:907
  82.8 79.2 %collective-permute-start.9 = (bf16[384,384]{1,0:T(8,128)(2,1)S(1)}, bf16[384,384]{1,0:T(8,128)(2,1)S(1)}, u32[]{:S(2)}, u32[]{:S(2)}) collective-permute-start(bf16[384,384]{1,0:T(8,128)(2,1)S(1)} %copy-done.25), channel_id=1, source_target_pairs={{0,2},{1,3},{2,10},{3,11},{4,6},{5,7},{6,14},{7,15},{8,0},{9,1},{1... | collective-permute-start | bytes 884744 | tf_op jit(solution)/shard_map/ppermute | solution.py:776
  83.5 78.4 %collective-permute-start.8 = (bf16[384,384]{1,0:T(8,128)(2,1)S(1)}, bf16[384,384]{1,0:T(8,128)(2,1)S(1)}, u32[]{:S(2)}, u32[]{:S(2)}) collective-permute-start(bf16[384,384]{1,0:T(8,128)(2,1)S(1)} %copy-done.25), channel_id=1, source_target_pairs={{0,0},{1,1},{2,8},{3,9},{4,4},{5,5},{6,12},{7,13},{8,2},{9,3},{10,... | collective-permute-start | bytes 884744 | tf_op jit(solution)/shard_map/ppermute | solution.py:776
  85.4 14.3 %collective-permute-start.14 = (f32[32,384]{1,0:T(8,128)S(1)}, f32[32,384]{1,0:T(8,128)S(1)}, u32[]{:S(2)}, u32[]{:S(2)}) collective-permute-start(f32[32,384]{1,0:T(8,128)S(1)} %concatenate.94), channel_id=1, source_target_pairs={{0,0},{1,1},{2,8},{3,9},{4,4},{5,5},{6,12},{7,13},{8,2},{9,3},{10,... | collective-permute-start | bytes 147464 | tf_op jit(solution)/shard_map/ppermute | solution.py:776
  99.7 24.1 %collective-permute-start.13 = (bf16[48,768]{1,0:T(8,128)(2,1)S(1)}, bf16[48,768]{1,0:T(8,128)(2,1)S(1)}, u32[]{:S(2)}, u32[]{:S(2)}) collective-permute-start(bf16[48,768]{1,0:T(8,128)(2,1)S(1)} %maximum_select_fusion.7), channel_id=1, source_target_pairs={{0,16},{1,17},{2,18},{3,19},{4,20},{5,21},{6,22},{7,23},{8,24},{9,... | collective-permute-start | bytes 221192 | tf_op jit(solution)/shard_map/ppermute | solution.py:776
  123.8 38.7 %collective-permute-start.16 = (bf16[384,384]{1,0:T(8,128)(2,1)S(1)}, bf16[384,384]{1,0:T(8,128)(2,1)S(1)}, u32[]{:S(2)}, u32[]{:S(2)}) collective-permute-start(bf16[384,384]{1,0:T(8,128)(2,1)S(1)} %copy-done.26), channel_id=1, source_target_pairs={{0,2},{1,3},{2,10},{3,11},{4,6},{5,7},{6,14},{7,15},{8,0},{9,1},{1... | collective-permute-start | bytes 884744 | tf_op jit(solution)/shard_map/ppermute | solution.py:776
  124.2 38.4 %collective-permute-start.15 = (bf16[384,384]{1,0:T(8,128)(2,1)S(1)}, bf16[384,384]{1,0:T(8,128)(2,1)S(1)}, u32[]{:S(2)}, u32[]{:S(2)}) collective-permute-start(bf16[384,384]{1,0:T(8,128)(2,1)S(1)} %copy-done.26), channel_id=1, source_target_pairs={{0,0},{1,1},{2,8},{3,9},{4,4},{5,5},{6,12},{7,13},{8,2},{9,3},{10,... | collective-permute-start | bytes 884744 | tf_op jit(solution)/shard_map/ppermute | solution.py:776
  128.1 37.0 %collective-permute-start.7 = (bf16[768,384]{1,0:T(8,128)(2,1)S(1)}, bf16[768,384]{1,0:T(8,128)(2,1)S(1)}, u32[]{:S(2)}, u32[]{:S(2)}) collective-permute-start(bf16[768,384]{1,0:T(8,128)(2,1)S(1)} %maximum_select_fusion.3), channel_id=1, source_target_pairs={{0,16},{1,17},{2,18},{3,19},{4,20},{5,21},{6,22},{7,23},{8,24},{9,... | collective-permute-start | bytes 1769480 | tf_op jit(solution)/shard_map/ppermute | solution.py:776
  162.2 14.8 %collective-permute-start.10 = (bf16[768,384]{1,0:T(8,128)(2,1)S(1)}, bf16[768,384]{1,0:T(8,128)(2,1)S(1)}, u32[]{:S(2)}, u32[]{:S(2)}) collective-permute-start(bf16[768,384]{1,0:T(8,128)(2,1)S(1)} %maximum_select_fusion.4), channel_id=1, source_target_pairs={{0,16},{1,17},{2,18},{3,19},{4,20},{5,21},{6,22},{7,23},{8,24},{9,... | collective-permute-start | bytes 1769480 | tf_op jit(solution)/shard_map/ppermute | solution.py:776
  162.7 26.9 %collective-permute-start.17 = (bf16[384,768]{1,0:T(8,128)(2,1)S(1)}, bf16[384,768]{1,0:T(8,128)(2,1)S(1)}, u32[]{:S(2)}, u32[]{:S(2)}) collective-permute-start(bf16[384,768]{1,0:T(8,128)(2,1)S(1)} %maximum_select_fusion.5), channel_id=1, source_target_pairs={{0,16},{1,17},{2,18},{3,19},{4,20},{5,21},{6,22},{7,23},{8,24},{9,... | collective-permute-start | bytes 1769480 | tf_op jit(solution)/shard_map/ppermute | solution.py:776
  308.1 45.3 %slice-start = ((s8[6291456]{0:T(1024)(128)(4,1)}), s8[4194304]{0:T(1024)(128)(4,1)S(1)}, s32[]{:S(2)}) async-start(s8[6291456]{0:T(1024)(128)(4,1)} %bitcast.53), calls=%async_computation.8 | async-start | bytes 8388608
  309.2 44.2 %slice-start.1 = ((s8[6291456]{0:T(1024)(128)(4,1)}), s8[2097152]{0:T(1024)(128)(4,1)S(1)}, s32[]{:S(2)}) async-start(s8[6291456]{0:T(1024)(128)(4,1)} %bitcast.53), calls=%async_computation.9 | async-start | bytes 4194304
  361.2 178.5 %reduce-scatter.4.cloned.1.call-start = ((), (), s32[]{:S(2)}) async-start(), calls=%async_computation.4 | async-start | bytes 7077888 | tf_op jit(solution)/shard_map/reduce_scatter | solution.py:981
  361.8 315.7 %reduce-scatter.6.cloned.1.call-start = ((), (), s32[]{:S(2)}) async-start(), calls=%async_computation.6 | async-start | bytes 7077888 | tf_op jit(solution)/shard_map/reduce_scatter | solution.py:991
  373.5 82.0 %collective-permute-start.30 = (bf16[768,384]{1,0:T(8,128)(2,1)}, bf16[768,384]{1,0:T(8,128)(2,1)S(1)}, u32[]{:S(2)}, u32[]{:S(2)}) collective-permute-start(bf16[768,384]{1,0:T(8,128)(2,1)} %dynamic-slice_convert_fusion.2), channel_id=1, source_target_pairs={{0,16},{1,17},{2,18},{3,19},{4,20},{5,21},{6,22},{7,23},{8,24},{9,... | collective-permute-start | bytes 1769480 | tf_op jit(solution)/shard_map/ppermute | solution.py:776
  374.1 28.4 %copy-start.6 = (f32[5,256]{1,0:T(8,128)S(1)}, f32[5,256]{1,0:T(8,128)}, u32[]{:S(2)}) copy-start(f32[5,256]{1,0:T(8,128)} %slice.166) | copy-start | bytes 15364
  379.9 83.9 %collective-permute-start.33 = (bf16[768,384]{1,0:T(8,128)(2,1)}, bf16[768,384]{1,0:T(8,128)(2,1)S(1)}, u32[]{:S(2)}, u32[]{:S(2)}) collective-permute-start(bf16[768,384]{1,0:T(8,128)(2,1)} %dynamic-slice_convert_fusion.1), channel_id=1, source_target_pairs={{0,16},{1,17},{2,18},{3,19},{4,20},{5,21},{6,22},{7,23},{8,24},{9,... | collective-permute-start | bytes 1769480 | tf_op jit(solution)/shard_map/ppermute | solution.py:776
  395.7 56.0 %collective-permute-start.39 = (f32[8,384]{1,0:T(8,128)}, f32[8,384]{1,0:T(8,128)S(1)}, u32[]{:S(2)}, u32[]{:S(2)}) collective-permute-start(f32[8,384]{1,0:T(8,128)} %psum.30), channel_id=1, source_target_pairs={{0,0},{1,1},{8,2},{9,3},{4,4},{5,5},{12,6},{13,7},{2,8},{3,9},{10,... | collective-permute-start | bytes 36872 | tf_op jit(solution)/shard_map/ppermute | solution.py:776
  450.8 15.2 %collective-permute-start.40 = (bf16[384,768]{1,0:T(8,128)(2,1)}, bf16[384,768]{1,0:T(8,128)(2,1)}, u32[]{:S(2)}, u32[]{:S(2)}) collective-permute-start(bf16[384,768]{1,0:T(8,128)(2,1)} %dynamic-slice_convert_fusion), channel_id=1, source_target_pairs={{0,16},{1,17},{2,18},{3,19},{4,20},{5,21},{6,22},{7,23},{8,24},{9,... | collective-permute-start | bytes 1769480 | tf_op jit(solution)/shard_map/ppermute | solution.py:776
  457.1 11.7 %collective-permute-start.32 = (bf16[384,384]{1,0:T(8,128)(2,1)S(1)}, bf16[384,384]{1,0:T(8,128)(2,1)S(1)}, u32[]{:S(2)}, u32[]{:S(2)}) collective-permute-start(bf16[384,384]{1,0:T(8,128)(2,1)S(1)} %get-tuple-element.90), channel_id=1, source_target_pairs={{2,0},{3,1},{10,2},{11,3},{6,4},{7,5},{14,6},{15,7},{0,8},{1,9},{8... | collective-permute-start | bytes 884744 | tf_op jit(solution)/shard_map/ppermute | solution.py:776
  458.6 19.6 %collective-permute-start.31 = (bf16[384,384]{1,0:T(8,128)(2,1)S(1)}, bf16[384,384]{1,0:T(8,128)(2,1)S(1)}, u32[]{:S(2)}, u32[]{:S(2)}) collective-permute-start(bf16[384,384]{1,0:T(8,128)(2,1)S(1)} %get-tuple-element.89), channel_id=1, source_target_pairs={{0,0},{1,1},{8,2},{9,3},{4,4},{5,5},{12,6},{13,7},{2,8},{3,9},{10,... | collective-permute-start | bytes 884744 | tf_op jit(solution)/shard_map/ppermute | solution.py:776
  464.0 23.7 %collective-permute-start.35 = (bf16[384,384]{1,0:T(8,128)(2,1)S(1)}, bf16[384,384]{1,0:T(8,128)(2,1)S(1)}, u32[]{:S(2)}, u32[]{:S(2)}) collective-permute-start(bf16[384,384]{1,0:T(8,128)(2,1)S(1)} %get-tuple-element.88), channel_id=1, source_target_pairs={{2,0},{3,1},{10,2},{11,3},{6,4},{7,5},{14,6},{15,7},{0,8},{1,9},{8... | collective-permute-start | bytes 884744 | tf_op jit(solution)/shard_map/ppermute | solution.py:776
  464.1 33.1 %collective-permute-start.34 = (bf16[384,384]{1,0:T(8,128)(2,1)S(1)}, bf16[384,384]{1,0:T(8,128)(2,1)S(1)}, u32[]{:S(2)}, u32[]{:S(2)}) collective-permute-start(bf16[384,384]{1,0:T(8,128)(2,1)S(1)} %get-tuple-element.87), channel_id=1, source_target_pairs={{0,0},{1,1},{8,2},{9,3},{4,4},{5,5},{12,6},{13,7},{2,8},{3,9},{10,... | collective-permute-start | bytes 884744 | tf_op jit(solution)/shard_map/ppermute | solution.py:776
  467.3 12.8 %copy-start.18 = (f32[48]{0:T(128)S(1)}, f32[48]{0:T(128)}, u32[]{:S(2)}) copy-start(f32[48]{0:T(128)} %pad.32.clone) | copy-start | bytes 580
  467.4 39.3 %collective-permute-start.42 = (bf16[384,384]{1,0:T(8,128)(2,1)S(1)}, bf16[384,384]{1,0:T(8,128)(2,1)S(1)}, u32[]{:S(2)}, u32[]{:S(2)}) collective-permute-start(bf16[384,384]{1,0:T(8,128)(2,1)S(1)} %get-tuple-element.86), channel_id=1, source_target_pairs={{2,0},{3,1},{10,2},{11,3},{6,4},{7,5},{14,6},{15,7},{0,8},{1,9},{8... | collective-permute-start | bytes 884744 | tf_op jit(solution)/shard_map/ppermute | solution.py:776
  468.8 47.4 %collective-permute-start.41 = (bf16[384,384]{1,0:T(8,128)(2,1)S(1)}, bf16[384,384]{1,0:T(8,128)(2,1)S(1)}, u32[]{:S(2)}, u32[]{:S(2)}) collective-permute-start(bf16[384,384]{1,0:T(8,128)(2,1)S(1)} %get-tuple-element.85), channel_id=1, source_target_pairs={{0,0},{1,1},{8,2},{9,3},{4,4},{5,5},{12,6},{13,7},{2,8},{3,9},{10,... | collective-permute-start | bytes 884744 | tf_op jit(solution)/shard_map/ppermute | solution.py:776
  481.0 17.1 %collective-permute-start.36 = (bf16[48,768]{1,0:T(8,128)(2,1)S(1)}, bf16[48,768]{1,0:T(8,128)(2,1)S(1)}, u32[]{:S(2)}, u32[]{:S(2)}) collective-permute-start(bf16[48,768]{1,0:T(8,128)(2,1)S(1)} %dynamic-slice_convert_fusion.9), channel_id=1, source_target_pairs={{0,16},{1,17},{2,18},{3,19},{4,20},{5,21},{6,22},{7,23},{8,24},{9,... | collective-permute-start | bytes 221192 | tf_op jit(solution)/shard_map/ppermute | solution.py:776
  498.1 19.2 %collective-permute-start.38 = (bf16[48,384]{1,0:T(8,128)(2,1)S(1)}, bf16[48,384]{1,0:T(8,128)(2,1)S(1)}, u32[]{:S(2)}, u32[]{:S(2)}) collective-permute-start(bf16[48,384]{1,0:T(8,128)(2,1)S(1)} %get-tuple-element.92), channel_id=1, source_target_pairs={{2,0},{3,1},{10,2},{11,3},{6,4},{7,5},{14,6},{15,7},{0,8},{1,9},{8... | collective-permute-start | bytes 110600 | tf_op jit(solution)/shard_map/ppermute | solution.py:776
  498.2 20.3 %collective-permute-start.37 = (bf16[48,384]{1,0:T(8,128)(2,1)S(1)}, bf16[48,384]{1,0:T(8,128)(2,1)S(1)}, u32[]{:S(2)}, u32[]{:S(2)}) collective-permute-start(bf16[48,384]{1,0:T(8,128)(2,1)S(1)} %get-tuple-element.91), channel_id=1, source_target_pairs={{0,0},{1,1},{8,2},{9,3},{4,4},{5,5},{12,6},{13,7},{2,8},{3,9},{10,... | collective-permute-start | bytes 110600 | tf_op jit(solution)/shard_map/ppermute | solution.py:776
  543.8 139.9 %collective-permute-start.25 = (bf16[64,1536]{1,0:T(8,128)(2,1)S(1)}, bf16[64,1536]{1,0:T(8,128)(2,1)S(1)}, u32[]{:S(2)}, u32[]{:S(2)}) collective-permute-start(bf16[64,1536]{1,0:T(8,128)(2,1)S(1)} %get-tuple-element.74), channel_id=1, source_target_pairs={{18,0},{19,1},{26,2},{27,3},{22,4},{23,5},{30,6},{31,7},{16,8},{17... | collective-permute-start | bytes 589832 | tf_op jit(solution)/shard_map/ppermute | solution.py:776
  546.9 139.6 %collective-permute-start.24 = (bf16[64,1536]{1,0:T(8,128)(2,1)S(1)}, bf16[64,1536]{1,0:T(8,128)(2,1)S(1)}, u32[]{:S(2)}, u32[]{:S(2)}) collective-permute-start(bf16[64,1536]{1,0:T(8,128)(2,1)S(1)} %get-tuple-element.75), channel_id=1, source_target_pairs={{16,0},{17,1},{24,2},{25,3},{20,4},{21,5},{28,6},{29,7},{18,8},{19... | collective-permute-start | bytes 589832 | tf_op jit(solution)/shard_map/ppermute | solution.py:776
  547.9 138.6 %collective-permute-start.23 = (bf16[64,1536]{1,0:T(8,128)(2,1)S(1)}, bf16[64,1536]{1,0:T(8,128)(2,1)S(1)}, u32[]{:S(2)}, u32[]{:S(2)}) collective-permute-start(bf16[64,1536]{1,0:T(8,128)(2,1)S(1)} %get-tuple-element.76), channel_id=1, source_target_pairs={{2,0},{3,1},{10,2},{11,3},{6,4},{7,5},{14,6},{15,7},{0,8},{1,9},{8... | collective-permute-start | bytes 589832 | tf_op jit(solution)/shard_map/ppermute | solution.py:776
  547.9 141.1 %collective-permute-start.22 = (bf16[64,1536]{1,0:T(8,128)(2,1)S(1)}, bf16[64,1536]{1,0:T(8,128)(2,1)S(1)}, u32[]{:S(2)}, u32[]{:S(2)}) collective-permute-start(bf16[64,1536]{1,0:T(8,128)(2,1)S(1)} %get-tuple-element.73), channel_id=1, source_target_pairs={{0,0},{1,1},{8,2},{9,3},{4,4},{5,5},{12,6},{13,7},{2,8},{3,9},{10,... | collective-permute-start | bytes 589832 | tf_op jit(solution)/shard_map/ppermute | solution.py:776
  682.4 10.1 %collective-permute-start.29 = (bf16[64,1536]{1,0:T(8,128)(2,1)S(1)}, bf16[64,1536]{1,0:T(8,128)(2,1)S(1)}, u32[]{:S(2)}, u32[]{:S(2)}) collective-permute-start(bf16[64,1536]{1,0:T(8,128)(2,1)S(1)} %get-tuple-element.70), channel_id=1, source_target_pairs={{18,0},{19,1},{26,2},{27,3},{22,4},{23,5},{30,6},{31,7},{16,8},{17... | collective-permute-start | bytes 589832 | tf_op jit(solution)/shard_map/ppermute | solution.py:776
  683.6 16.0 %collective-permute-start.28 = (bf16[64,1536]{1,0:T(8,128)(2,1)S(1)}, bf16[64,1536]{1,0:T(8,128)(2,1)S(1)}, u32[]{:S(2)}, u32[]{:S(2)}) collective-permute-start(bf16[64,1536]{1,0:T(8,128)(2,1)S(1)} %get-tuple-element.71), channel_id=1, source_target_pairs={{16,0},{17,1},{24,2},{25,3},{20,4},{21,5},{28,6},{29,7},{18,8},{19... | collective-permute-start | bytes 589832 | tf_op jit(solution)/shard_map/ppermute | solution.py:776
  686.5 13.1 %collective-permute-start.27 = (bf16[64,1536]{1,0:T(8,128)(2,1)S(1)}, bf16[64,1536]{1,0:T(8,128)(2,1)S(1)}, u32[]{:S(2)}, u32[]{:S(2)}) collective-permute-start(bf16[64,1536]{1,0:T(8,128)(2,1)S(1)} %get-tuple-element.72), channel_id=1, source_target_pairs={{2,0},{3,1},{10,2},{11,3},{6,4},{7,5},{14,6},{15,7},{0,8},{1,9},{8... | collective-permute-start | bytes 589832 | tf_op jit(solution)/shard_map/ppermute | solution.py:776
  686.5 17.1 %collective-permute-start.26 = (bf16[64,1536]{1,0:T(8,128)(2,1)S(1)}, bf16[64,1536]{1,0:T(8,128)(2,1)S(1)}, u32[]{:S(2)}, u32[]{:S(2)}) collective-permute-start(bf16[64,1536]{1,0:T(8,128)(2,1)S(1)} %get-tuple-element.69), channel_id=1, source_target_pairs={{0,0},{1,1},{8,2},{9,3},{4,4},{5,5},{12,6},{13,7},{2,8},{3,9},{10,... | collective-permute-start | bytes 589832 | tf_op jit(solution)/shard_map/ppermute | solution.py:776
  (15 other events, 62.8 us)
Sparse Core Ops, SparseCore 0:
  41.9 54.9 all-gather.3
  99.0 65.1 all-gather.5
  361.4 28.0 reduce-scatter.7
  391.8 147.9 reduce-scatter.3
  542.0 135.5 reduce-scatter.5

commit v2 on v1

--- a/solution.py
+++ b/solution.py
@@ -1,4 +1,5 @@
 from functools import partial
+from functools import reduce
 
 import jax
 import jax.numpy as jnp
@@ -118,18 +119,14 @@
     x_ref,
     norm_in_ref,
     w_value_ref,
-    w_gate_ref,
     w_small_ref,
     taps_value_ref,
     taps_pair_ref,
     heads_ref,
     skip_ref,
-    norm_gate_ref,
-    w_out_ref,
     spread_ref,
     lower_ref,
     normed_ref,
-    gate_ref,
     value_ref,
     conv_value_ref,
     pair_ref,
@@ -137,8 +134,6 @@
     step_ref,
     scanned_ref,
     states_ref,
-    partial_ref,
-    square_ref,
     halo_value,
     halo_pair,
     state,
@@ -160,13 +155,11 @@
     normed = (x * rms * norm_in_ref[...].astype(F32)).astype(BF16)
     normed_ref[...] = normed
     value = dot_nn(normed, w_value_ref[...])
-    gate = dot_nn(normed, w_gate_ref[...])
     small = dot_nt(normed, w_small_ref[...])
     pair_width = conv_pair_ref.shape[-1]
     pair = small[:, :pair_width]
     step = small[:, pair_width : pair_width + LANES]
     value_ref[...] = value
-    gate_ref[...] = gate
     pair_ref[...] = pair
     step_ref[...] = step
 
@@ -238,27 +231,20 @@
         state[...] = held * reach_wide[SUB - 1 : SUB, :] + dot_tn(
             keys, (stepped * tail_wide).astype(BF16)
         )
-    scanned = jnp.concatenate(scanned_parts, axis=0)
-    scanned_ref[...] = scanned
-    gated = scanned * (gate * sigmoid(gate))
-    high, low = split_two(gated * gated)
-    ones = jnp.ones((8, gated.shape[1]), BF16)
-    square_ref[...] = dot_nt(ones, high) + dot_nt(ones, low)
-    scaled = (gated * norm_gate_ref[...]).astype(BF16)
-    partial_ref[...] = (
-        dot_nn(scaled, w_out_ref[...]).astype(BF16).reshape(partial_ref.shape)
-    )
+    scanned_ref[...] = jnp.concatenate(scanned_parts, axis=0)
 
 
 def back_kernel(
     live_ids,
     bounds_ref,
     back_ref,
+    normed_ref,
+    w_gate_ref,
     w_out_ref,
     norm_gate_ref,
     scanned_ref,
     gate_ref,
-    square_ref,
+    scaled_ref,
     grad_normed_ref,
     stats_ref,
 ):
@@ -267,27 +253,78 @@
     base = pl.program_id(1) * ROWS
     places = base + iota((ROWS, LANES), 0)
     live = segment_of(places, bounds) < live_ids
-    grad = dot_nt(back_ref[...].reshape(ROWS, back_ref.shape[-1]), w_out_ref[...])
+    gate = dot_nn(normed_ref[...], w_gate_ref[...])
+    gate_ref[...] = gate
+    gated = scanned_ref[...] * (gate * sigmoid(gate))
+    normed_gated = gated * norm_gate_ref[...]
+    scaled_ref[...] = normed_gated.astype(BF16).reshape(scaled_ref.shape)
+    grad = dot_nn(back_ref[...].reshape(ROWS, back_ref.shape[-1]), w_out_ref[...])
     live_wide = jnp.concatenate([live] * (grad.shape[1] // LANES), axis=1)
     grad = jnp.where(live_wide, grad, 0.0)
     grad_normed_ref[...] = grad
-    gate = gate_ref[...]
-    gated = scanned_ref[...] * (gate * sigmoid(gate))
-    high, low = split_two(grad * norm_gate_ref[...] * gated)
     ones = jnp.ones((8, gated.shape[1]), BF16)
+    high, low = split_two(gated * gated)
+    square = dot_nt(ones, high) + dot_nt(ones, low)
+    high, low = split_two(grad * normed_gated)
     cross = dot_nt(ones, high) + dot_nt(ones, low)
-    stats_ref[...] = jnp.where(iota(cross.shape, 0) == 0, square_ref[...], cross)
-
-
-def backward_kernel(
-    pair_count,
+    stats_ref[...] = jnp.where(iota(cross.shape, 0) == 0, square, cross)
+
+
+def gate_kernel(
     live_ids,
     inner_full,
     bounds_ref,
     stats_ref,
     grad_normed_ref,
+    gate_ref,
+    scanned_ref,
+    norm_gate_ref,
+    low_gate_ref,
+    normed_out_ref,
+    grad_scanned_ref,
+    sums_ref,
+):
+    micro = pl.program_id(0)
+    block = pl.program_id(1)
+    bounds = read_bounds(bounds_ref, micro)
+
+    @pl.when((micro == 0) & (block == 0))
+    def _():
+        sums_ref[...] = jnp.zeros_like(sums_ref)
+
+    tiles = gate_ref.shape[1] // LANES
+    live = segment_of(block * ROWS + iota((ROWS, LANES), 0), bounds) < live_ids
+    gate = gate_ref[...]
+    scanned = scanned_ref[...]
+    grad_normed = grad_normed_ref[...]
+    norm_gate = norm_gate_ref[...]
+    stats = stats_ref[...].T / inner_full
+    spread = lax.rsqrt(stats[:, 0:1] + EPS)
+    cross = stats[:, 1:2]
+    sg = sigmoid(gate)
+    act = gate * sg
+    gated = scanned * act
+    normed_gated = gated * spread
+    live_wide = jnp.concatenate([live] * tiles, axis=1)
+    normed_out = jnp.where(live_wide, normed_gated * norm_gate, 0.0).astype(BF16)
+    normed_out_ref[...] = normed_out.reshape(normed_out_ref.shape)
+    grad_gated = spread * (grad_normed * norm_gate - normed_gated * (spread * cross))
+    grad_scanned_ref[...] = grad_gated * act
+    low_gate_ref[...] = (
+        grad_gated * scanned * (sg * (1.0 + gate * (1.0 - sg)))
+    ).astype(BF16)
+    sums_ref[0:1, :] += jnp.sum(grad_normed * normed_gated, axis=0, keepdims=True)
+
+
+def backward_kernel(
+    pair_count,
+    micro,
+    first,
+    apart,
+    bounds_ref,
+    grad_scanned_ref,
+    low_gate_ref,
     normed_ref,
-    gate_ref,
     value_ref,
     conv_value_ref,
     pair_ref,
@@ -302,62 +339,43 @@
     taps_pair_ref,
     heads_ref,
     skip_ref,
-    norm_gate_ref,
     spread_ref,
     gather_ref,
     lower_ref,
     upper_ref,
-    low_gate_ref,
-    low_value_ref,
-    low_small_ref,
-    normed_out_ref,
-    grad_in_ref,
-    sums_ref,
-    sums_in_ref,
-    halo_value,
-    halo_pair,
-    state,
+    *rest,
 ):
-    micro = pl.program_id(0)
-    turn = pl.program_id(1)
-    block_count = pl.num_programs(1)
+    if not first:
+        rest = rest[2:]
+    (
+        low_value_ref,
+        low_small_ref,
+        *grad_in_refs,
+        sums_ref,
+        sums_in_ref,
+        halo_value,
+        halo_pair,
+        state,
+    ) = rest
+    turn = pl.program_id(0)
+    block_count = pl.num_programs(0)
     block = block_count - 1 - turn
     count = block_count * ROWS
     bounds = read_bounds(bounds_ref, micro)
     base = block * ROWS
 
-    @pl.when((micro == 0) & (turn == 0))
+    @pl.when(turn == 0)
     def _():
         sums_ref[...] = jnp.zeros_like(sums_ref)
         sums_in_ref[...] = jnp.zeros_like(sums_in_ref)
-
-    @pl.when(turn == 0)
-    def _():
         halo_value[...] = jnp.zeros_like(halo_value)
         halo_pair[...] = jnp.zeros_like(halo_pair)
         state[...] = jnp.zeros_like(state)
 
-    width = gate_ref.shape[1]
-    tiles = width // LANES
-    places = base + iota((ROWS, LANES), 0)
-    live = segment_of(places, bounds) < live_ids
-
-    gate = gate_ref[...]
+    width = value_ref.shape[1]
     scanned = scanned_ref[...]
-    grad_normed = grad_normed_ref[...]
-    norm_gate = norm_gate_ref[...]
-    spread = lax.rsqrt(stats_ref[:, 0:1] / inner_full + EPS)
-    cross = stats_ref[:, 1:2] / inner_full
-    sg = sigmoid(gate)
-    act = gate * sg
-    gated = scanned * act
-    normed_gated = gated * spread
-    live_wide = jnp.concatenate([live] * tiles, axis=1)
-    normed_out_ref[...] = jnp.where(live_wide, normed_gated * norm_gate, 0.0).astype(BF16)
-    grad_gated = spread * (grad_normed * norm_gate - normed_gated * (spread * cross))
-    grad_scanned = grad_gated * act
-    low_gate = (grad_gated * scanned * (sg * (1.0 + gate * (1.0 - sg)))).astype(BF16)
-    low_gate_ref[...] = low_gate
+    grad_scanned = grad_scanned_ref[...]
+    low_gate = low_gate_ref[...]
 
     conv_value = conv_value_ref[...]
     sig_value = sigmoid(conv_value)
@@ -479,14 +497,25 @@
         + dot_nt(low_value, w_value_ref[...])
         + dot_nn(low_small, w_small_ref[...])
     )
-    grad_in_ref[...] = grad_in.astype(BF16).reshape(grad_in_ref.shape)
+    grad_in_low = grad_in.astype(BF16).reshape(grad_in_refs[0].shape)
+    if apart:
+        mine = block % 2 == bounds_ref[bounds_ref.shape[0] - 1, 0]
+
+        @pl.when(mine)
+        def _():
+            grad_in_refs[0][...] = grad_in_low
+
+        @pl.when(jnp.logical_not(mine))
+        def _():
+            grad_in_refs[1][...] = grad_in_low
+
+    else:
+        grad_in_refs[0][...] = grad_in_low
     sums_in_ref[0:1, :] += jnp.sum(grad_in * normed_ref[...].astype(F32), axis=0, keepdims=True)
-    gate_sum = jnp.sum(grad_normed * normed_gated, axis=0, keepdims=True)
     skip_sum = jnp.sum(grad_scanned * mixed, axis=0, keepdims=True)
     step_sum = jnp.sum(grad_step, axis=0, keepdims=True)
     for k in range(5):
         sums_ref[k : k + 1, :] += value_sums[k]
-    sums_ref[5:6, :] += gate_sum
     sums_ref[6:7, :] += skip_sum
     sums_ref[7:8, :LANES] += step_sum
     sums_ref[7:8, LANES : 2 * LANES] += decay_sum
@@ -524,13 +553,24 @@
     )
 
 
-def run_forward(bounds, rows, weights, consts):
-    micro_count, block_len = rows.shape[1], rows.shape[0] * rows.shape[2]
+def seat_spec(piece, cols):
+    return pl.BlockSpec((None, 2, None, piece, cols), lambda b, i: (i // 2, 0, i % 2, b, 0))
+
+
+def seat_view(item):
+    return item.reshape((item.shape[0] // 4, 2, 2) + item.shape[1:])
+
+
+def cost(flops, count, moved):
+    return pl.CostEstimate(flops=int(flops), transcendentals=int(count), bytes_accessed=int(moved))
+
+
+def run_forward(bounds, rows, weights, consts, micro_count, piece):
+    block_len = 8 * piece
     blocks = block_len // ROWS
-    per_block = ROWS // rows.shape[2]
-    norm_in, w_value, w_gate, w_small, taps_value, taps_pair, heads, skip, norm_gate, w_out = weights
+    norm_in, w_value, _, w_small, taps_value, taps_pair, heads, skip = weights
     spread, _, lower, _ = consts
-    full = rows.shape[3]
+    full = rows.shape[4]
     width = w_value.shape[1]
     pair_width = taps_pair.shape[1]
     length = micro_count * block_len
@@ -539,26 +579,21 @@
     def by_rows(cols):
         return pl.BlockSpec((ROWS, cols), lambda b, i: (b * blocks + i, 0))
 
-    row_block = pl.BlockSpec((per_block, None, rows.shape[2], full), lambda b, i: (i, b, 0, 0))
-    wholes = [norm_in, w_value, w_gate, w_small, taps_value, taps_pair, heads, skip, norm_gate, w_out, spread, lower]
-    widths = [width, width, width, pair_width, pair_width, LANES, width]
+    wholes = [norm_in, w_value, w_small, taps_value, taps_pair, heads, skip, spread, lower]
+    widths = [width, width, pair_width, pair_width, LANES, width]
     return pl.pallas_call(
         partial(forward_kernel, width // LANES),
         grid=(micro_count, blocks),
-        in_specs=[smem_spec(), row_block] + [whole_spec(item.shape) for item in wholes],
+        in_specs=[smem_spec(), seat_spec(piece, full)] + [whole_spec(item.shape) for item in wholes],
         out_specs=[by_rows(full)]
         + [by_rows(cols) for cols in widths]
         + [
             pl.BlockSpec((subs, LANES, width), lambda b, i: (b * blocks + i, 0, 0)),
-            row_block,
-            pl.BlockSpec((8, ROWS), lambda b, i: (0, b * blocks + i)),
         ],
         out_shape=[jax.ShapeDtypeStruct((length, full), BF16)]
         + [jax.ShapeDtypeStruct((length, cols), F32) for cols in widths]
         + [
             jax.ShapeDtypeStruct((length // SUB, LANES, width), F32),
-            jax.ShapeDtypeStruct(rows.shape, BF16),
-            jax.ShapeDtypeStruct((8, length), F32),
         ],
         scratch_shapes=[
             pltpu.VMEM((8, width), F32),
@@ -566,92 +601,142 @@
             pltpu.VMEM((LANES, width), F32),
         ],
         compiler_params=kernel_params(),
+        cost_estimate=cost(length * full * width * 12, length * width * 8, length * width * 40),
         name="forward",
     )(bounds, rows, *wholes)
 
 
-def run_back(bounds, back, w_out, norm_gate, scanned, gate, square, live_ids):
-    micro_count, block_len = back.shape[1], back.shape[0] * back.shape[2]
+def run_back(bounds, back, normed, w_gate, w_out, norm_gate, scanned, live_ids, micro_count, piece):
+    block_len = 8 * piece
     blocks = block_len // ROWS
-    per_block = ROWS // back.shape[2]
-    width = gate.shape[1]
-    length = micro_count * block_len
-    by_rows = pl.BlockSpec((ROWS, width), lambda b, i: (b * blocks + i, 0))
+    length, width = scanned.shape
+    full = normed.shape[1]
+
+    def by_rows(cols):
+        return pl.BlockSpec((ROWS, cols), lambda b, i: (b * blocks + i, 0))
+
     by_cols = pl.BlockSpec((8, ROWS), lambda b, i: (0, b * blocks + i))
-    row_block = pl.BlockSpec((per_block, None, back.shape[2], back.shape[3]), lambda b, i: (i, b, 0, 0))
     return pl.pallas_call(
         partial(back_kernel, live_ids),
         grid=(micro_count, blocks),
         in_specs=[
             smem_spec(),
-            row_block,
+            seat_spec(piece, full),
+            by_rows(full),
+            whole_spec(w_gate.shape),
             whole_spec(w_out.shape),
             whole_spec(norm_gate.shape),
-            by_rows,
-            by_rows,
-            by_cols,
+            by_rows(width),
         ],
-        out_specs=[by_rows, by_cols],
+        out_specs=[by_rows(width), seat_spec(piece, width), by_rows(width), by_cols],
         out_shape=[
+            jax.ShapeDtypeStruct((length, width), F32),
+            jax.ShapeDtypeStruct(back.shape[:4] + (width,), BF16),
             jax.ShapeDtypeStruct((length, width), F32),
             jax.ShapeDtypeStruct((8, length), F32),
         ],
         compiler_params=kernel_params(),
+        cost_estimate=cost(length * full * width * 4, length * width, length * width * 30),
         name="back",
-    )(bounds, back, w_out, norm_gate, scanned, gate, square)
-
-
-def run_backward(bounds, stats, grad_normed, kept, weights, consts, rows_shape, live_ids, inner_full):
-    micro_count, block_len = rows_shape[1], rows_shape[0] * rows_shape[2]
+    )(bounds, back, normed, w_gate, w_out, norm_gate, scanned)
+
+
+def run_gate(bounds, stats, grad_normed, gate, scanned, norm_gate, live_ids, inner_full, micro_count, piece):
+    block_len = 8 * piece
     blocks = block_len // ROWS
-    per_block = ROWS // rows_shape[2]
-    normed, gate, value, conv_value, pair, conv_pair, step, scanned, states = kept
-    _, w_value, w_gate, w_small, taps_value, taps_pair, heads, skip, norm_gate, _ = weights
+    length, width = gate.shape
+    by_rows = pl.BlockSpec((ROWS, width), lambda b, i: (b * blocks + i, 0))
+    return pl.pallas_call(
+        partial(gate_kernel, live_ids, inner_full),
+        grid=(micro_count, blocks),
+        in_specs=[
+            smem_spec(),
+            pl.BlockSpec((8, ROWS), lambda b, i: (0, b * blocks + i)),
+            by_rows,
+            by_rows,
+            by_rows,
+            whole_spec(norm_gate.shape),
+        ],
+        out_specs=[
+            by_rows,
+            seat_spec(piece, width),
+            by_rows,
+            whole_spec((8, width)),
+        ],
+        out_shape=[
+            jax.ShapeDtypeStruct((length, width), BF16),
+            jax.ShapeDtypeStruct((blocks // 2, 2, 2, micro_count * piece, width), BF16),
+            jax.ShapeDtypeStruct((length, width), F32),
+            jax.ShapeDtypeStruct((8, width), F32),
+        ],
+        compiler_params=kernel_params(),
+        cost_estimate=cost(length * width * 20, length * width, length * width * 20),
+        name="gate",
+    )(bounds, stats, grad_normed, gate, scanned, norm_gate)
+
+
+def run_backward(bounds, grad_scanned, low_gate, kept, weights, consts, micro, piece, earlier, apart):
+    block_len = 8 * piece
+    blocks = block_len // ROWS
+    normed, value, conv_value, pair, conv_pair, step, scanned, states = kept
+    _, w_value, w_gate, w_small, taps_value, taps_pair, heads, skip = weights
     spread, gather, lower, upper = consts
-    full = rows_shape[3]
-    width = gate.shape[1]
+    full = normed.shape[1]
+    length, width = value.shape
     pair_width = pair.shape[1]
-    length = micro_count * block_len
     subs = ROWS // SUB
 
-    def place(b, i):
-        return b * blocks + blocks - 1 - i
+    def place(i):
+        return micro * blocks + blocks - 1 - i
 
     def by_rows(item):
-        return pl.BlockSpec((ROWS, item.shape[1]), lambda b, i: (place(b, i), 0))
-
-    row_block = pl.BlockSpec(
-        (per_block, None, rows_shape[2], full), lambda b, i: (blocks - 1 - i, b, 0, 0)
-    )
-    rowwise = [stats, grad_normed, normed, gate, value, conv_value, pair, conv_pair, step, scanned]
-    wholes = [w_value, w_gate, w_small, taps_value, taps_pair, heads, skip, norm_gate, spread, gather, lower, upper]
+        return pl.BlockSpec((ROWS, item.shape[1]), lambda i: (place(i), 0))
+
+    if apart:
+        row_blocks = [
+            pl.BlockSpec((None, 2, piece, full), lambda i: ((blocks - 1 - i) // 2, 0, 0, 0))
+        ] * 2
+        row_shapes = [jax.ShapeDtypeStruct((blocks // 2, 2, piece, full), BF16)] * 2
+    else:
+        row_blocks = [
+            pl.BlockSpec(
+                (None, 2, None, piece, full),
+                lambda i: ((blocks - 1 - i) // 2, 0, (blocks - 1 - i) % 2, 0, 0),
+            )
+        ]
+        row_shapes = [jax.ShapeDtypeStruct((blocks // 2, 2, 2, piece, full), BF16)]
+    rowwise = [grad_scanned, low_gate, normed, value, conv_value, pair, conv_pair, step, scanned]
+    wholes = [w_value, w_gate, w_small, taps_value, taps_pair, heads, skip, spread, gather, lower, upper]
     outs = [
         jax.ShapeDtypeStruct((length, width), BF16),
-        jax.ShapeDtypeStruct((length, width), BF16),
         jax.ShapeDtypeStruct((length, w_small.shape[0]), BF16),
-        jax.ShapeDtypeStruct((length, width), BF16),
-        jax.ShapeDtypeStruct(rows_shape, BF16),
+        *row_shapes,
         jax.ShapeDtypeStruct((16, width), F32),
         jax.ShapeDtypeStruct((8, full), F32),
     ]
+    ins = [bounds] + rowwise + [states] + wholes
     return pl.pallas_call(
-        partial(backward_kernel, width // LANES, live_ids, inner_full),
-        grid=(micro_count, blocks),
+        partial(backward_kernel, width // LANES, micro, earlier is None, apart),
+        grid=(blocks,),
         in_specs=[smem_spec()]
         + [by_rows(item) for item in rowwise]
-        + [pl.BlockSpec((subs, LANES, width), lambda b, i: (place(b, i), 0, 0))]
-        + [whole_spec(item.shape) for item in wholes],
-        out_specs=[by_rows(item) for item in outs[:4]]
-        + [row_block, whole_spec(outs[5].shape), whole_spec(outs[6].shape)],
+        + [pl.BlockSpec((subs, LANES, width), lambda i: (place(i), 0, 0))]
+        + [whole_spec(item.shape) for item in wholes]
+        + ([] if earlier is None else [pl.BlockSpec(memory_space=pl.ANY)] * 2),
+        out_specs=[by_rows(item) for item in outs[:2]]
+        + row_blocks
+        + [whole_spec(item.shape) for item in outs[-2:]],
         out_shape=outs,
+        input_output_aliases={} if earlier is None else {len(ins): 0, len(ins) + 1: 1},
         scratch_shapes=[
             pltpu.VMEM((8, width), F32),
             pltpu.VMEM((8, pair_width), F32),
             pltpu.VMEM((LANES, width), F32),
         ],
         compiler_params=kernel_params(),
+        cost_estimate=cost(block_len * full * width * 14, block_len * width * 16, block_len * width * 40),
         name="backward",
-    )(bounds, *rowwise, states, *wholes)
+    )(*ins, *([] if earlier is None else earlier))
 
 
 def deal_kernel(
@@ -734,12 +819,13 @@
     out_ref[...] = dot_tn(map_ref[...], out.astype(BF16)).astype(BF16)
 
 
-def close_back_kernel(map_ref, dealt_ref, back_ref, grad_ref, norm_in_ref, out_ref):
-    shape = dealt_ref.shape
+def close_back_kernel(map_ref, dealt_ref, back_ref, norm_in_ref, *refs):
+    grad_refs, out_ref = refs[:-1], refs[-1]
     x = dealt_ref[...].astype(F32)
     rms = lax.rsqrt(jnp.mean(x * x, axis=1, keepdims=True) + EPS)
     xhat = x * rms
-    win = grad_ref[...].reshape(shape).astype(F32) * norm_in_ref[...].astype(F32)
+    grad = jnp.concatenate([item[...].astype(F32) for item in grad_refs], axis=0)
+    win = grad * norm_in_ref[...].astype(F32)
     cross = jnp.mean(win * xhat, axis=1, keepdims=True)
     out = back_ref[...].astype(F32) + rms * (win - xhat * cross)
     out_ref[...] = dot_tn(map_ref[...], out.astype(BF16)).astype(BF16)
@@ -758,7 +844,7 @@
 
 
 ALL = ("pair", "core", "row", "half", "near")
-TEAM = ("row", "core", "near")
+TEAM = ("row", "near", "core")
 
 
 def make_perm(sizes, move):
@@ -844,30 +930,63 @@
         for k in pair_bits
     ]
 
-    def gather_groups(block, axis):
-        first = swap(block, cross_perms[0])
-        second = swap(block, cross_perms[1])
+    team_perms = {
+        "core": make_perm(sizes, lambda p, c, r, h, n: (p, 1 - c, r, h, n)),
+        "near": make_perm(sizes, lambda p, c, r, h, n: (p, c, r, h, 1 - n)),
+        "row": make_perm(sizes, lambda p, c, r, h, n: (p, c, 1 - r, h, n)),
+    }
+
+    def after(v, *others):
+        return lax.optimization_barrier((v,) + others)[0]
+
+    def cross_groups(block):
+        return swap(block, cross_perms[0]), swap(block, cross_perms[1])
+
+    def gather_groups(crossed, axis):
+        first, second = crossed
         current = choose(my_half, first, second, axis)
         for k in pair_bits:
             other = swap(current, pair_perms[k])
             current = choose((my_pair >> k) & 1, current, other, axis)
         return current
 
-    def scatter_groups(total, axis):
-        current = total
+    def scatter_groups(current, sums=None, split=None, join=None, waits=(), ends=()):
+        def pack(v):
+            v = v.astype(BF16)
+            if sums is None:
+                return v
+            rows = split(sums)
+            rows = jnp.broadcast_to(rows, v.shape[:-2] + rows.shape)
+            return jnp.concatenate([v, rows], axis=-2)
+
+        length = current.shape[-2]
+
+        def unpack(v, total):
+            if total is None:
+                return v.astype(F32), None
+            first = v if v.ndim == 2 else v[0]
+            return v[..., :length, :].astype(F32), total + join(
+                first[length:], total.shape[0]
+            )
+
         for k in reversed(pair_bits):
-            half = current.shape[axis] // 2
+            half = current.shape[0] // 2
             bit = (my_pair >> k) & 1
-            kept = lax.dynamic_slice_in_dim(current, bit * half, half, axis)
-            sent = lax.dynamic_slice_in_dim(current, (1 - bit) * half, half, axis)
-            arrived = swap(sent.astype(BF16), pair_perms[k])
-            current = kept + arrived.astype(F32)
-        half = current.shape[axis] // 2
-        first = lax.dynamic_slice_in_dim(current, my_half * half, half, axis)
-        second = lax.dynamic_slice_in_dim(current, (1 - my_half) * half, half, axis)
-        first = swap(first.astype(BF16), turned(cross_perms[0]))
-        second = swap(second.astype(BF16), turned(cross_perms[1]))
-        return first.astype(F32) + second.astype(F32)
+            kept = lax.dynamic_slice_in_dim(current, bit * half, half, 0)
+            sent = lax.dynamic_slice_in_dim(current, (1 - bit) * half, half, 0)
+            arrived = after(swap(pack(sent), pair_perms[k]), *waits)
+            arrived, sums = unpack(arrived, sums)
+            current = kept + arrived
+        first = lax.dynamic_index_in_dim(current, my_half, 0, keepdims=False)
+        second = lax.dynamic_index_in_dim(current, 1 - my_half, 0, keepdims=False)
+        first = after(swap(pack(first), turned(cross_perms[0])), *ends)
+        second = after(swap(pack(second), turned(cross_perms[1])), *ends)
+        if sums is None:
+            return first.astype(F32) + second.astype(F32)
+        zero = jnp.zeros_like(sums)
+        first, sums_first = unpack(first, zero)
+        second, sums_second = unpack(second, zero)
+        return first + second, sums_first + sums_second
 
     listed = lax.dynamic_index_in_dim(
         token_order.reshape(group_count, micro_count, team_size, piece_len),
@@ -890,51 +1009,27 @@
         group_len,
     )
 
-    def deal(rows):
-        pieces = [
+    def deal_pieces(rows):
+        return [
             swap(rows[e * quota_len : (e + 1) * quota_len], deal_perms[e])
             for e in range(group_count)
         ]
-        return run_pick(take_map, jnp.concatenate(pieces, axis=0), False)
-
-    def undeal(rows):
+
+    def undeal(rows, *waits):
         pieces = [
             swap(rows[e * quota_len : (e + 1) * quota_len], turned(deal_perms[e]))
             for e in range(group_count)
         ]
+        pieces = [after(piece, *waits) for piece in pieces]
         return run_pick(send_map, jnp.concatenate(pieces, axis=0), True)
 
-    bounds = lax.ppermute(
-        seq_lengths.astype(F32), ALL, cross_perms[0]
-    ).astype(jnp.int32)
-    bounds = jnp.cumsum(bounds, axis=1).astype(jnp.int32)
-    live_ids = seq_lengths.shape[1] - 1
-
-    def regroup(item):
-        return swap(item, cross_perms[0])
-
-    dealt_tokens = deal(send_tokens)
-    full_rows = lax.all_gather(
-        dealt_tokens.reshape(micro_count, piece_len, width_full), TEAM, axis=0
-    )
-    dealt_back = deal(send_cotangent)
-    full_back = lax.all_gather(
-        dealt_back.reshape(micro_count, piece_len, width_full), TEAM, axis=0
-    )
-
-    value_w = gather_groups(w_value, 0)
-    gate_w = gather_groups(w_gate, 0)
-    small_pad = -(pair_part + head_count) % 16
-    small_own = jnp.concatenate(
-        [w_pair.T, w_step.T, jnp.zeros((small_pad, w_pair.shape[0]), BF16)], axis=0
-    )
-    small_w = gather_groups(small_own, 1)
-    pair_w = lax.all_gather(small_w[:pair_part], TEAM, axis=0, tiled=True)
-    step_w = jnp.pad(
-        small_w[pair_part : pair_part + head_count], ((0, LANES - head_count), (0, 0))
-    )
-    small_w = jnp.concatenate([pair_w, step_w], axis=0)
-    out_w = gather_groups(w_out, 1)
+    def exchange(v, axis_name):
+        return swap(v, team_perms[axis_name])
+
+    def sum_over(v, names):
+        for name in names:
+            v = v + exchange(v, name)
+        return v
 
     def pack_taps(taps, bias):
         return jnp.concatenate(
@@ -942,25 +1037,82 @@
         )
 
     heads_own = jnp.pad(jnp.stack([step_bias, decay_log, skip_gain]), ((0, 5), (0, 0)))
+    lengths_own = jnp.pad(
+        seq_lengths.astype(F32),
+        ((0, 8 - micro_count), (0, width - seq_lengths.shape[1])),
+    )
     local_params = jnp.concatenate(
         [
             pack_taps(conv_value, bias_value),
             jnp.broadcast_to(norm_gate[None, :], (8, width)),
             jnp.pad(heads_own, ((0, 0), (0, width - head_count))),
             jnp.pad(pack_taps(conv_pair, bias_pair), ((0, 0), (0, width - pair_part))),
+            lengths_own,
         ],
         axis=0,
     )
-    local_params = regroup(local_params)
+    local_params = swap(after(local_params, send_tokens), cross_perms[0])
     taps_value = local_params[:8]
     norm_gate_row = local_params[8:9]
     heads_got = local_params[16:24, :head_count]
+    own_taps = local_params[24:32, :pair_part]
+    live_ids = seq_lengths.shape[1] - 1
+    bounds = jnp.cumsum(
+        local_params[32 : 32 + micro_count, : live_ids + 1].astype(jnp.int32), axis=1
+    )
     skip_row = jnp.repeat(heads_got[2:3], head_width, axis=1)
     heads_row = jnp.pad(
         jnp.concatenate([heads_got[0:1], -jnp.exp(heads_got[1:2])], axis=0),
         ((0, 6), (0, LANES - head_count)),
     )
-    taps_pair = lax.all_gather(local_params[24:32, :pair_part], TEAM, axis=1, tiled=True)
+    tap_high = lax.reduce_precision(own_taps, 8, 7)
+    tap_mid = lax.reduce_precision(own_taps - tap_high, 8, 7)
+    tap_low = own_taps - tap_high - tap_mid
+    tap_row = jnp.stack([tap_high, tap_mid, tap_low]).astype(BF16).reshape(1, -1)
+    tap_count = tap_row.shape[1]
+
+    small_pad = -(pair_part + head_count) % 16
+    small_own = jnp.concatenate(
+        [w_pair.T, w_step.T, jnp.zeros((small_pad, w_pair.shape[0]), BF16)], axis=0
+    )
+    small_w = gather_groups(cross_groups(after(small_own, send_tokens)), 1)
+
+    pieces = deal_pieces(send_tokens)
+    dealt_tokens = run_pick(take_map, jnp.concatenate(pieces, axis=0), False)
+    full_rows = seat_view(
+        lax.all_gather(
+            jnp.concatenate(
+                [
+                    dealt_tokens,
+                    small_w[:pair_part],
+                    jnp.pad(tap_row, ((0, 15), (0, width_full - tap_count))),
+                ],
+                axis=0,
+            ),
+            TEAM,
+            axis=0,
+        )
+    )
+    value_w = cross_groups(after(w_value, *pieces))
+    pieces = deal_pieces(after(send_cotangent, *value_w))
+    value_w = gather_groups(value_w, 0)
+    dealt_back = run_pick(take_map, jnp.concatenate(pieces, axis=0), False)
+    full_back = seat_view(lax.all_gather(dealt_back, TEAM, axis=0))
+    later_w = cross_groups(after(jnp.stack([w_gate, w_out.T]), *pieces))
+    full_rows, *later_w = lax.optimization_barrier((full_rows, *later_w))
+    later_w = gather_groups(later_w, 1)
+    gate_w, out_w = later_w[0], later_w[1]
+
+    extra = full_rows[:, :, :, share_len:]
+    pair_w = extra[:, :, :, :pair_part].reshape(pair_width, width_full)
+    taps_got = extra[:, :, :, pair_part, :tap_count].astype(F32)
+    taps_got = taps_got.reshape(team_size, 3, 8, pair_part)
+    taps_got = taps_got[:, 0] + (taps_got[:, 1] + taps_got[:, 2])
+    taps_pair = jnp.swapaxes(taps_got, 0, 1).reshape(8, pair_width)
+    step_w = jnp.pad(
+        small_w[pair_part : pair_part + head_count], ((0, LANES - head_count), (0, 0))
+    )
+    small_w = jnp.concatenate([pair_w, step_w], axis=0)
 
     consts = head_constants(head_count, head_width)
     weights = (
@@ -972,56 +1124,135 @@
         taps_pair,
         heads_row,
         skip_row,
-        norm_gate_row,
-        out_w,
-    )
-    outs = run_forward(bounds, full_rows, weights, consts)
-    kept = outs[:9]
-    partial_out, square = outs[9], outs[10]
-    branch = lax.psum_scatter(partial_out, TEAM, scatter_dimension=0)
-    normed, gate, scanned = kept[0], kept[1], kept[7]
-    grad_normed, stats = run_back(
-        bounds, full_back, out_w, norm_gate_row, scanned, gate, square, live_ids
-    )
-    stats = lax.psum(stats[:2], TEAM)
-    stats_cols = jnp.pad(stats.T, ((0, 0), (0, 6)))
-    low_gate, low_value, low_small, normed_out, grad_in, sums, sums_in = run_backward(
-        bounds, stats_cols, grad_normed, kept, weights, consts, full_rows.shape, live_ids, inner_full
-    )
-    grad_in = lax.psum_scatter(grad_in, TEAM, scatter_dimension=0)
-
-    flat_back = (
-        jnp.swapaxes(full_back, 0, 1).reshape(micro_count * block_len, width_full)
-    )
-    g_out = scatter_groups(dot_tn(normed_out, flat_back), 1)
-    g_gate = scatter_groups(dot_tn(normed, low_gate), 0)
-    g_value = scatter_groups(dot_tn(normed, low_value), 0)
+    )
+    outs = run_forward(bounds, full_rows, weights, consts, micro_count, piece_len)
+    normed, value, conv_v, pair, conv_p, step, scanned, states = outs
+    flat = micro_count * block_len
+    gate, scaled, grad_normed, stats = run_back(
+        bounds, full_back, normed, gate_w, out_w, norm_gate_row, scanned, live_ids, micro_count, piece_len
+    )
+    partial_out = dot_nt(scaled.reshape(flat, width), out_w).astype(BF16)
+    partial_out, stats = lax.optimization_barrier((partial_out, stats))
+    branch = lax.psum_scatter(partial_out, TEAM, scatter_dimension=0, tiled=True)
+    stats = sum_over(stats, ("core", "near", "row"))
+    low_gate, normed_out, grad_scanned, gate_sums = run_gate(
+        bounds, stats, grad_normed, gate, scanned, norm_gate_row, live_ids, inner_full, micro_count, piece_len
+    )
+    kept = (normed, value, conv_v, pair, conv_p, step, scanned, states)
+    g_out = dot_tn(full_back.reshape(flat, width_full), normed_out.reshape(flat, width))
+    g_gate = dot_tn(normed, low_gate)
+    g_out, g_gate, grad_scanned = lax.optimization_barrier(
+        (g_out.astype(BF16), g_gate.astype(BF16), grad_scanned)
+    )
+    flagged = jnp.concatenate(
+        [bounds, jnp.full((1, bounds.shape[1]), my_core, jnp.int32)], axis=0
+    )
+    totals = []
+    all_sums = []
+    earlier = None
+    for micro in range(micro_count):
+        low_value, low_small, keep, send, sums, sums_in = run_backward(
+            flagged, grad_scanned, low_gate, kept, weights, consts, micro, piece_len, earlier, True
+        )
+        earlier = (low_value, low_small)
+        totals.append(keep.astype(F32) + exchange(send, "core").astype(F32))
+        all_sums.append((sums, sums_in))
+    low_value, low_small, branch, g_out, g_gate, *totals = lax.optimization_barrier(
+        (low_value, low_small, branch, g_out, g_gate, *totals)
+    )
+    early = [
+        lax.psum_scatter(item, ("pair", "half"), scatter_dimension=0, tiled=True)
+        for item in (g_out, g_gate)
+    ]
+    sides = {"near": (my_near, 1), "row": (my_row, 0)}
+
+    def halve(total, name, other):
+        bit, axis = sides[name]
+        axis = min(axis, total.ndim - 3)
+        keep = lax.dynamic_index_in_dim(total, bit, axis, keepdims=False)
+        send = lax.dynamic_index_in_dim(total, 1 - bit, axis, keepdims=False)
+        return keep + exchange(send.astype(BF16), name).astype(F32)
+
+    orders = [("near", "row") if micro % 2 == 0 else ("row", "near") for micro in range(micro_count)]
+    totals = [halve(total, order[0], order[1]) for total, order in zip(totals, orders)]
+    branch, *totals = lax.optimization_barrier((branch, *totals))
+    middle = totals
+    totals = [halve(total, order[1], order[0]) for total, order in zip(totals, orders)]
+    grad_ins = totals
+
+    g_out, g_gate = [
+        swap(after(item, *grad_ins), turned(cross_perms[0])).astype(F32) for item in early
+    ]
+    g_out = g_out.T
+    g_value = dot_tn(normed, low_value)
     g_small = dot_tn(low_small, normed)
-    g_pair = lax.psum_scatter(
-        g_small[:pair_width].astype(BF16), TEAM, scatter_dimension=0, tiled=True
-    )
+    sums = reduce(jnp.add, [item[0] for item in all_sums])
+    sums_in = reduce(jnp.add, [item[1] for item in all_sums])[0:1]
+    pair_sums = sums[8:13, :pair_width].reshape(1, -1)
+    pair_sums = jnp.pad(pair_sums, ((0, 0), (0, -pair_sums.shape[1] % width_full)))
+    team_rows = jnp.concatenate(
+        [sums_in, pair_sums.reshape(-1, width_full)], axis=0
+    )
+
+    def split_rows(v, axis=0):
+        high = lax.reduce_precision(v, 8, 7)
+        both = jnp.concatenate([high, v - high], axis=0).astype(BF16)
+        return jnp.pad(both, ((0, -both.shape[0] % 16), (0, 0)))
+
+    def join_rows(v, count):
+        return v[:count].astype(F32) + v[count : 2 * count].astype(F32)
+
+    g_pair = g_small[:pair_width].reshape(sizes[2], sizes[4], 2, pair_part, width_full)
+    for name, bit, axis in (("core", my_core, 2), ("near", my_near, 1), ("row", my_row, 0)):
+        keep = lax.dynamic_index_in_dim(g_pair, bit, axis, keepdims=False)
+        send = lax.dynamic_index_in_dim(g_pair, 1 - bit, axis, keepdims=False)
+        count = send.size // width_full
+        packed = jnp.concatenate(
+            [send.astype(BF16).reshape(count, width_full), split_rows(team_rows)], axis=0
+        )
+        packed = exchange(packed, name)
+        if name != "core":
+            packed = after(packed, *middle)
+        g_pair = keep + packed[:count].reshape(keep.shape).astype(F32)
+        team_rows = team_rows + join_rows(packed[count:], team_rows.shape[0])
     g_small = jnp.concatenate(
         [
-            g_pair.astype(F32),
+            g_pair,
             g_small[pair_width : pair_width + head_count],
             jnp.zeros((small_pad, width_full), F32),
         ],
         axis=0,
     )
-    g_small = scatter_groups(g_small, 1)
+    sums = jnp.concatenate(
+        [sums[:5], gate_sums[0:1], sums[6:8], team_rows.reshape(-1, width)], axis=0
+    )
+    small_rows = g_small.shape[0]
+    value_rows = width_full // group_count
+    late = jnp.swapaxes(g_small.reshape(small_rows, group_count, -1), 0, 1)
+    if value_rows != width:
+        late = jnp.pad(late, ((0, 0), (0, 0), (0, width - value_rows)))
+    send_back = run_close(
+        close_back_kernel, take_map, dealt_tokens, dealt_back, norm_in[None, :], *grad_ins
+    )
+    late, sums = scatter_groups(
+        late, sums, split_rows, join_rows, grad_ins, [send_back]
+    )
+    g_value = g_value.reshape(group_count, -1, width)
+    g_value = scatter_groups(g_value, waits=middle, ends=[send_back])
+    g_small = late[:, :value_rows]
     g_pair = g_small[:pair_part].T
     g_step = g_small[pair_part : pair_part + head_count].T
-
-    sums_group = lax.psum(sums[:8], ("pair", "half"))
-    sums_group = swap(sums_group, turned(cross_perms[0]))
-    sums_team = lax.psum((sums[8:13, :pair_width], sums_in[0]), ALL)
-    pair_sums = lax.dynamic_slice_in_dim(sums_team[0], member * pair_part, pair_part, 1)
-    g_norm_in = sums_team[1] / norm_in.astype(F32)
-    g_skip = jnp.sum(sums_group[6].reshape(head_count, head_width), axis=1)
+    pair_sums = sums[8 + width_full // width :].reshape(-1)[: 5 * pair_width]
+    pair_sums = pair_sums.reshape(5, pair_width)
+    in_sums = sums[8 : 8 + width_full // width]
+    own_place = (my_row * sizes[4] + my_near) * sizes[3] + my_half
+    pair_sums = lax.dynamic_slice_in_dim(pair_sums, own_place * pair_part, pair_part, 1)
+    g_norm_in = in_sums.reshape(-1) / norm_in.astype(F32)
+    g_skip = jnp.sum(sums[6].reshape(head_count, head_width), axis=1)
 
     live_start = seat * piece_len
     local_stats = lax.dynamic_slice_in_dim(
-        stats.reshape(2, micro_count, block_len)[0], live_start, piece_len, 1
+        stats[0].reshape(micro_count, block_len), live_start, piece_len, 1
     )
     local_places = live_start + jnp.arange(piece_len, dtype=jnp.int32)
     local_seg = jnp.sum(
@@ -1030,12 +1261,8 @@
     weight = jnp.where(
         local_seg < live_ids, lax.rsqrt(local_stats / inner_full + EPS), 0.0
     ).reshape(share_len, 1)
-    block_out = undeal(run_close(close_out_kernel, take_map, dealt_tokens, branch, weight))
-    grad_tokens = undeal(
-        run_close(
-            close_back_kernel, take_map, dealt_tokens, dealt_back, grad_in, norm_in[None, :]
-        )
-    )
+    block_out = undeal(run_close(close_out_kernel, take_map, dealt_tokens, branch, weight), send_back)
+    grad_tokens = undeal(send_back)
     return (
         block_out,
         grad_tokens,
@@ -1044,14 +1271,14 @@
         g_value,
         g_pair,
         g_step,
-        sums_group[0:4],
-        sums_group[4],
+        sums[0:4],
+        sums[4],
         pair_sums[0:4],
         pair_sums[4],
-        sums_group[7, :head_count],
-        sums_group[7, LANES : LANES + head_count],
+        sums[7, :head_count],
+        sums[7, LANES : LANES + head_count],
         g_skip,
-        sums_group[5],
+        sums[5],
         g_out,
     )
 

time: 715 us -> 431 us (0.60)
  blocking collectives: 177 us -> 0 us
  waiting for transfers between devices: 262 us -> 113 us
  other arithmetic: 20.5 us -> 37.5 us
  matrix products: 17.7 us -> 31 us
  Pallas kernels: 111 us -> 120 us
    reduce_scatter x3, waiting for transfers between devices: 146 us -> 0.02 us  [the longest x2 0.02 us: per_device(): lax.psum_scatter(item, ('pair', 'half'), scatter_dimension=0, tiled=True)]
    psum x3 -> x0, blocking collectives: 124 us -> none  [the longest x1 69.3 us: per_device(): stats = lax.psum(stats[:2], TEAM)]
    all_gather x2 -> x0, blocking collectives: 53.3 us -> none  [the longest x1 33.4 us: per_device(): pair_w = lax.all_gather(small_w[:pair_part], TEAM, axis=0, tiled=True)]
    add x4 -> x19, other arithmetic: 2.93 us -> 17.6 us  [the longest x2 7.22 us: per_device(): totals.append(keep.astype(F32) + exchange(send, 'core').astype(F32))]
    pallas_call x1 -> x3, Pallas kernels: 44.2 us -> 58.4 us  [the longest x2 48.1 us: run_backward(): pl.pallas_call(partial(backward_kernel, width // LANES, micro, earlier is...]
    pallas_call x1, Pallas kernels: 35.5 us -> 26.2 us  [run_forward(): pl.pallas_call(partial(forward_kernel, width // LANES), grid=(micro_count...]
    ppermute x1 -> x0, waiting for transfers between devices: 7.31 us -> none  [per_device(): lax.ppermute(seq_lengths.astype(F32), ALL, cross_perms[0]).astype(jnp.int32)]
    ppermute x42 -> x46, waiting for transfers between devices: 108 us -> 113 us  [swap(): return lax.ppermute(v, ALL, perm)]
  transfers between devices with their start and end apart: 48 -> 51, of which waited for: 24 -> 23; matrix products, arithmetic and copies ran while one was open for 7% -> 20% of each run, Pallas kernels for 7% -> 23%
where the time goes in v2:
time: 431 us; the launch traced here: 426 us
  Pallas kernels  120 us (28%)
  waiting for transfers between devices  113 us (26%)
  starting transfers between devices  72.6 us (17%)
  other arithmetic  37.5 us (9%)
  local copies, waits for them, and re-layouts  36.7 us (9%)
  matrix products  31 us (7%)
  between operations  15.3 us (4%)
    ppermute x46, waiting for transfers between devices, swap(): return lax.ppermute(v, ALL, perm)  113 us
    ppermute x46, starting transfers between devices, swap(): return lax.ppermute(v, ALL, perm)  72.2 us
    pallas_call x2, Pallas kernels, run_backward(): pl.pallas_call(partial(backward_kernel, width // LANES, micro, earlier is...  48.1 us
    pallas_call x1, Pallas kernels, run_forward(): pl.pallas_call(partial(forward_kernel, width // LANES), grid=(micro_count...  26.2 us
    dot_general x4, matrix products, dot_tn(): lax.dot_general(a, b, (((0,), (0,)), ((), ())), preferred_element_type=F32)  24.1 us
    pallas_call x1, Pallas kernels, run_back(): pl.pallas_call(partial(back_kernel, live_ids), grid=(micro_count, blocks)...  14.8 us
    pallas_call x1, Pallas kernels, run_gate(): pl.pallas_call(partial(gate_kernel, live_ids, inner_full), grid=(micro_co...  10.3 us
    pallas_call x4, Pallas kernels, run_pick(): pl.pallas_call(partial(pick_kernel, transposed), in_specs=[vmem] * 2, out...  9.97 us
  transfers between devices with their start and end apart: 51, of which 23 were waited for; matrix products, arithmetic and copies ran while one was open for 20% of the time, Pallas kernels for 23%

profile of v2, /device:TPU:1, one launch (start us, length us, event | category | flops | bytes accessed | tf_op | source)
XLA Modules:
  0.0 425.5 jit_solution(7822615991504932607)
XLA Ops:
  12.5 3.5 deal.1
  16.1 5.6 %collective-permute-start.11 = (bf16[48,384]{1,0:T(8,128)(2,1)S(1)}, bf16[48,384]{1,0:T(8,128)(2,1)S(1)}, u32[]{:S(2)}, u32[]{:S(2)}) collective-permute-start(bf16[48,384]{1,0:T(8,128)(2,1)S(1)} %maximum_maximum_fusion.1), channel_id=1, source_target_pairs={{0,0},{1,1},{2,8},{3,9},{4,4},{5,5},{6,12},{7,13},{8,2},{9,3},{10,... | collective-permute-start | bytes 110600 | tf_op jit(solution)/shard_map/ppermute | solution.py:862
  22.0 1.9 collective-permute-start.4
  25.2 4.5 %collective-permute-start = (bf16[64,1536]{1,0:T(8,128)(2,1)S(1)}, bf16[64,1536]{1,0:T(8,128)(2,1)S(1)}, u32[]{:S(2)}, u32[]{:S(2)}) collective-permute-start(bf16[64,1536]{1,0:T(8,128)(2,1)S(1)} %get-tuple-element.223), channel_id=1, source_target_pairs={{0,0},{1,1},{2,8},{3,9},{4,4},{5,5},{6,12},{7,13},{8,2},{9,3},{10,... | collective-permute-start | bytes 589832 | tf_op jit(solution)/shard_map/ppermute | solution.py:862
  31.7 1.7 collective-permute-start.13
  33.6 2.6 collective-permute-done.13
  36.3 5.8 %collective-permute-done = bf16[64,1536]{1,0:T(8,128)(2,1)S(1)} collective-permute-done((bf16[64,1536]{1,0:T(8,128)(2,1)S(1)}, bf16[64,1536]{1,0:T(8,128)(2,1)S(1)}, u32[]{:S(2)}, u32[]{:S(2)}) %collective-permute-start) | collective-permute-done | bytes 196640 | tf_op jit(solution)/shard_map/ppermute | solution.py:862
  42.0 4.2 collective-permute-done.3
  46.2 1.9 collective-permute-done.2
  49.0 2.5 pick.4.dealt_ref
  51.5 2.3 fusion.3
  53.9 1.9 collective-permute-start.5
  55.9 13.9 %collective-permute-done.6 = bf16[384,384]{1,0:T(8,128)(2,1)S(1)} collective-permute-done((bf16[384,384]{1,0:T(8,128)(2,1)S(1)}, bf16[384,384]{1,0:T(8,128)(2,1)S(1)}, u32[]{:S(2)}, u32[]{:S(2)}) %collective-permute-start.6) | collective-permute-done | bytes 294944 | tf_op jit(solution)/shard_map/ppermute | solution.py:862
  69.9 1.9 collective-permute-start.7
  71.9 3.6 collective-permute-start.9
  76.4 6.6 %collective-permute-done.7 = bf16[64,1536]{1,0:T(8,128)(2,1)S(1)} collective-permute-done((bf16[64,1536]{1,0:T(8,128)(2,1)S(1)}, bf16[64,1536]{1,0:T(8,128)(2,1)S(1)}, u32[]{:S(2)}, u32[]{:S(2)}) %collective-permute-start.7) | collective-permute-done | bytes 196640 | tf_op jit(solution)/shard_map/ppermute | solution.py:862
  83.7 8.8 %collective-permute-done.9 = bf16[64,1536]{1,0:T(8,128)(2,1)S(1)} collective-permute-done((bf16[64,1536]{1,0:T(8,128)(2,1)S(1)}, bf16[64,1536]{1,0:T(8,128)(2,1)S(1)}, u32[]{:S(2)}, u32[]{:S(2)}) %collective-permute-start.9) | collective-permute-done | bytes 196640 | tf_op jit(solution)/shard_map/ppermute | solution.py:862
  93.4 2.5 pick.5.back_ref
  98.7 5.4 %collective-permute-start.14 = (bf16[2,384,384]{2,1,0:T(8,128)(2,1)S(1)}, bf16[2,384,384]{2,1,0:T(8,128)(2,1)S(1)}, u32[]{:S(2)}, u32[]{:S(2)}) collective-permute-start(bf16[2,384,384]{2,1,0:T(8,128)(2,1)S(1)} %pad_maximum_fusion.4), channel_id=1, source_target_pairs={{0,0},{1,1},{2,8},{3,9},{4,4},{5,5},{6,12},{7,13},{8,2},{9,3},{10,... | collective-permute-start | bytes 1769480 | tf_op jit(solution)/shard_map/ppermute | solution.py:862
  106.6 5.1 %collective-permute-done.16 = bf16[768,384]{1,0:T(8,128)(2,1)S(1)} collective-permute-done((bf16[768,384]{1,0:T(8,128)(2,1)S(1)}, bf16[768,384]{1,0:T(8,128)(2,1)S(1)}, u32[]{:S(2)}, u32[]{:S(2)}) %collective-permute-start.16) | collective-permute-done | bytes 589856 | tf_op jit(solution)/shard_map/ppermute | solution.py:862
  113.1 11.6 %collective-permute-done.15 = bf16[2,384,384]{2,1,0:T(8,128)(2,1)S(1)} collective-permute-done((bf16[2,384,384]{2,1,0:T(8,128)(2,1)S(1)}, bf16[2,384,384]{2,1,0:T(8,128)(2,1)S(1)}, u32[]{:S(2)}, u32[]{:S(2)}) %collective-permute-start.15) | collective-permute-done | bytes 589856 | tf_op jit(solution)/shard_map/ppermute | solution.py:862
  124.7 2.3 collective-permute-done.14
  132.7 26.2 %forward.1 = (bf16[2048,1536]{1,0:T(8,128)(2,1)}, f32[2048,384]{1,0:T(8,128)}, f32[2048,384]{1,0:T(8,128)}, f32[2048,256]{1,0:T(8,128)}, f32[2048,256]{1,0:T(8,1...) custom-call(s32[2,4]{1,0:T(2,128)} %reduce_window_sum.11.bounds_ref, ...), custom_call_target="tpu_custom_call" | custom-call | flops 14495514624 | bytes 31457280 | tf_op jit(solution)/shard_map/forward/pallas_call | solution.py:584
  159.4 1.7 slice_bitcast_fusion
  161.2 14.8 %back.1 = (f32[2048,384]{1,0:T(8,128)}, bf16[2,2,2,256,384]{4,3,2,1,0:T(8,128)(2,1)}, f32[2048,384]{1,0:T(8,128)}, f32[8,2048]{1,0:T(8,128)}) custom-call(s32[2,4]{1,0:T(2,128)} %reduce_window_sum.11.bounds_ref, bf16[2,2,2,256,1536]{4,3,2,1,0:T(8,128)(2,1)} %bitcast.127, bf16[2048,1536]{1,0:T(8,128)(2,1)} %get-tuple-element.95.normed_ref, ...), custom_call_target="tpu_custom_call" | custom-call | flops 4831838208 | bytes 23592960 | tf_op jit(solution)/shard_map/back/pallas_call | solution.py:619
  176.0 6.8 %convolution_convert_fusion = bf16[2048,1536]{1,0:T(8,128)(2,1)} fusion(bf16[2048,384]{1,0:T(8,128)(2,1)} %bitcast.158, bf16[2,1536,384]{2,1,0:T(8,128)(2,1)S(1)} %maximum_select_fusion), kind=kOutput, calls=%fused_computation | convolution fusion | flops 2419064832 | bytes 9043968 | tf_op jit(solution)/shard_map/dot_general | solution.py:27
  185.6 2.9 collective-permute-done.19
  189.6 3.5 collective-permute-done.20
  193.7 10.3 %gate.1 = (bf16[2048,384]{1,0:T(8,128)(2,1)}, bf16[2,2,2,256,384]{4,3,2,1,0:T(8,128)(2,1)}, f32[2048,384]{1,0:T(8,128)}, f32[8,384]{1,0:T(8,128)}) custom-call(s32[2,4]{1,0:T(2,128)} %reduce_window_sum.11.bounds_ref, f32[8,2048]{1,0:T(8,128)} %add.258.stats_ref, f32[2048,384]{1,0:T(8,128)} %get-tuple-element.102.grad_normed_ref, ...), custom_call_target="tpu_custom_call" | custom-call | flops 15728640 | bytes 15728640 | tf_op jit(solution)/shard_map/gate/pallas_call | solution.py:649
  204.1 5.9 %convolution_convert_fusion.1 = bf16[1536,384]{1,0:T(8,128)(2,1)} fusion(bf16[2048,1536]{1,0:T(8,128)(2,1)S(1)} %bitcast.126, bf16[2048,384]{1,0:T(8,128)(2,1)} %get-tuple-element.105.low_gate_ref), kind=kOutput, calls=%fused_computation.3 | convolution fusion | flops 2416508928 | bytes 9043968 | tf_op jit(solution)/shard_map/dot_general | solution.py:31
  210.0 7.8 %convolution_convert_fusion.2 = bf16[1536,384]{1,0:T(8,128)(2,1)} fusion(bf16[2048,1536]{1,0:T(8,128)(2,1)} %all-gather.5.cloned.1.call-done, bf16[2048,384]{1,0:T(8,128)(2,1)} %bitcast.157), kind=kOutput, calls=%fused_computation.4 | convolution fusion | flops 2416508928 | bytes 9043968 | tf_op jit(solution)/shard_map/dot_general | solution.py:31
  217.8 23.9 %backward.2 = (bf16[2048,384]{1,0:T(8,128)(2,1)}, bf16[2048,384]{1,0:T(8,128)(2,1)}, bf16[2,2,128,1536]{3,2,1,0:T(8,128)(2,1)}, bf16[2,2,128,1536]{3,2,1,0:T(8,1...) custom-call(s32[3,4]{1,0:T(4,128)} %concatenate.120.bounds_ref, f32[2048,384]{1,0:T(8,128)} %get-tuple-element.107.grad_scanned_ref, ...), custom_call_target="tpu_custom_call" | custom-call | flops 8455716864 | bytes 15728640 | tf_op jit(solution)/shard_map/backward/pallas_call | solution.py:718
  243.2 1.8 collective-permute-start.21
  245.0 24.2 %backward.3 = (bf16[2048,384]{1,0:T(8,128)(2,1)}, bf16[2048,384]{1,0:T(8,128)(2,1)}, bf16[2,2,128,1536]{3,2,1,0:T(8,128)(2,1)}, bf16[2,2,128,1536]{3,2,1,0:T(8,1...) custom-call(s32[3,4]{1,0:T(4,128)} %concatenate.120.bounds_ref, ...), custom_call_target="tpu_custom_call", output_to_operand_aliasing={{0}: (22, {}), {1}: (23, {})} | custom-call | flops 8455716864 | bytes 15728640 | tf_op jit(solution)/shard_map/backward/pallas_call | solution.py:718
  273.4 3.6 convert_add_fusion.1
  277.1 3.6 convert_add_fusion
  280.8 4.8 %fusion.48 = f32[384,1536]{1,0:T(8,128)S(1)} fusion(bf16[2048,384]{1,0:T(8,128)(2,1)S(1)} %copy-done, bf16[2048,1536]{1,0:T(8,128)(2,1)} %get-tuple-element.95.normed_ref), kind=kOutput, calls=%fused_computation.162 | convolution fusion | flops 2415919104 | bytes 10223616 | tf_op jit(solution)/shard_map/dot_general | solution.py:31
  286.9 3.4 fusion.5
  294.2 5.6 %fusion.49 = f32[1536,384]{1,0:T(8,128)S(1)} fusion(bf16[2048,1536]{1,0:T(8,128)(2,1)} %get-tuple-element.95.normed_ref, bf16[2048,384]{1,0:T(8,128)(2,1)S(1)} %copy-done.9), kind=kOutput, calls=%fused_computation.163 | convolution fusion | flops 2415919104 | bytes 10223616 | tf_op jit(solution)/shard_map/dot_general | solution.py:31
  305.5 1.7 collective-permute-start.36
  307.2 2.1 collective-permute-done.24
  310.7 8.4 %collective-permute-done.23 = bf16[2,128,1536]{2,1,0:T(8,128)(2,1)} collective-permute-done((bf16[2,128,1536]{2,1,0:T(8,128)(2,1)}, bf16[2,128,1536]{2,1,0:T(8,128)(2,1)}, u32[]{:S(2)}, u32[]{:S(2)}) %collective-permute-start.23) | collective-permute-done | bytes 786464 | tf_op jit(solution)/shard_map/ppermute | solution.py:862
  320.6 3.7 collective-permute-done.36
  324.4 2.8 close.2
  327.2 2.2 fusion.43
  329.4 2.3 collective-permute-start.25
  333.3 3.0 collective-permute-start.29
  339.9 2.4 collective-permute-done.37
  343.9 11.9 %collective-permute-done.27 = bf16[128,1536]{1,0:T(8,128)(2,1)S(1)} collective-permute-done((bf16[128,1536]{1,0:T(8,128)(2,1)S(1)}, bf16[128,1536]{1,0:T(8,128)(2,1)S(1)}, u32[]{:S(2)}, u32[]{:S(2)}) %collective-permute-start.27) | collective-permute-done | bytes 393248 | tf_op jit(solution)/shard_map/ppermute | solution.py:862
  355.8 2.2 collective-permute-start.43
  360.0 2.0 bitcast_add_fusion.4.refs_0_
  362.0 3.8 close.3
  367.3 3.1 collective-permute-start.28
  370.4 1.9 collective-permute-start.31
  372.3 6.8 %collective-permute-done.43 = bf16[384,384]{1,0:T(8,128)(2,1)S(1)} collective-permute-done((bf16[384,384]{1,0:T(8,128)(2,1)}, bf16[384,384]{1,0:T(8,128)(2,1)S(1)}, u32[]{:S(2)}, u32[]{:S(2)}) %collective-permute-start.43) | collective-permute-done | bytes 294944 | tf_op jit(solution)/shard_map/ppermute | solution.py:862
  379.1 3.9 collective-permute-start.33
  383.9 6.3 %collective-permute-start.39 = (bf16[80,384]{1,0:T(8,128)(2,1)S(1)}, bf16[80,384]{1,0:T(8,128)(2,1)S(1)}, u32[]{:S(2)}, u32[]{:S(2)}) collective-permute-start(bf16[80,384]{1,0:T(8,128)(2,1)S(1)} %get-tuple-element.251), channel_id=1, source_target_pairs={{0,0},{1,1},{8,2},{9,3},{4,4},{5,5},{12,6},{13,7},{2,8},{3,9},{10,... | collective-permute-start | bytes 184328 | tf_op jit(solution)/shard_map/ppermute | solution.py:862
  390.4 2.0 pad_maximum_fusion.2.rows_ref
  392.4 2.5 pick.6
  394.9 2.0 collective-permute-done.39
  400.5 2.9 collective-permute-start.45
  405.4 3.5 collective-permute-start.41
  409.8 2.5 pick.7
  413.4 4.5 %collective-permute-done.41 = bf16[384,384]{1,0:T(8,128)(2,1)S(1)} collective-permute-done((bf16[384,384]{1,0:T(8,128)(2,1)}, bf16[384,384]{1,0:T(8,128)(2,1)S(1)}, u32[]{:S(2)}, u32[]{:S(2)}) %collective-permute-start.41) | collective-permute-done | bytes 294944 | tf_op jit(solution)/shard_map/ppermute | solution.py:862
  (285 shorter events, 68.7 us)
Async XLA Ops:
  7.2 14.5 %copy-start.31 = (f32[6]{0:T(128)S(1)}, f32[6]{0:T(128)}, u32[]{:S(2)}) copy-start(f32[6]{0:T(128)} %param.37) | copy-start | bytes 76
  7.2 14.6 %copy-start.30 = (f32[32]{0:T(128)S(1)}, f32[32]{0:T(128)}, u32[]{:S(2)}) copy-start(f32[32]{0:T(128)} %param.34) | copy-start | bytes 388
  7.2 14.6 %copy-start.26 = (f32[4,32]{1,0:T(4,128)S(1)}, f32[4,32]{1,0:T(4,128)}, u32[]{:S(2)}) copy-start(f32[4,32]{1,0:T(4,128)} %param.33) | copy-start | bytes 1540
  7.3 14.7 %copy-start.25 = (f32[4,384]{1,0:T(4,128)S(1)}, f32[4,384]{1,0:T(4,128)}, u32[]{:S(2)}) copy-start(f32[4,384]{1,0:T(4,128)} %param.31) | copy-start | bytes 18436
  7.3 14.7 %copy-start.27 = (f32[384]{0:T(512)S(1)}, f32[384]{0:T(512)}, u32[]{:S(2)}) copy-start(f32[384]{0:T(512)} %param.38) | copy-start | bytes 4612
  7.3 119.7 %all-gather.7.cloned.1.call-start = ((), (), s32[]{:S(2)}) async-start(), calls=%async_computation.7 | async-start | bytes 8404992 | tf_op jit(solution)/shard_map/all_gather | solution.py:1083
  16.1 13.8 %collective-permute-start.12 = (bf16[48,384]{1,0:T(8,128)(2,1)S(1)}, bf16[48,384]{1,0:T(8,128)(2,1)S(1)}, u32[]{:S(2)}, u32[]{:S(2)}) collective-permute-start(bf16[48,384]{1,0:T(8,128)(2,1)S(1)} %maximum_maximum_fusion.1), channel_id=1, source_target_pairs={{0,2},{1,3},{2,10},{3,11},{4,6},{5,7},{6,14},{7,15},{8,0},{9,1},{1... | collective-permute-start | bytes 110600 | tf_op jit(solution)/shard_map/ppermute | solution.py:862
  16.1 15.2 %collective-permute-start.11 = (bf16[48,384]{1,0:T(8,128)(2,1)S(1)}, bf16[48,384]{1,0:T(8,128)(2,1)S(1)}, u32[]{:S(2)}, u32[]{:S(2)}) collective-permute-start(bf16[48,384]{1,0:T(8,128)(2,1)S(1)} %maximum_maximum_fusion.1), channel_id=1, source_target_pairs={{0,0},{1,1},{2,8},{3,9},{4,4},{5,5},{6,12},{7,13},{8,2},{9,3},{10,... | collective-permute-start | bytes 110600 | tf_op jit(solution)/shard_map/ppermute | solution.py:862
  22.0 9.7 %collective-permute-start.4 = (f32[40,384]{1,0:T(8,128)S(1)}, f32[40,384]{1,0:T(8,128)S(1)}, u32[]{:S(2)}, u32[]{:S(2)}) collective-permute-start(f32[40,384]{1,0:T(8,128)S(1)} %concatenate.119), channel_id=1, source_target_pairs={{0,0},{1,1},{2,8},{3,9},{4,4},{5,5},{6,12},{7,13},{8,2},{9,3},{10,... | collective-permute-start | bytes 184328 | tf_op jit(solution)/shard_map/ppermute | solution.py:862
  25.2 16.8 %collective-permute-start = (bf16[64,1536]{1,0:T(8,128)(2,1)S(1)}, bf16[64,1536]{1,0:T(8,128)(2,1)S(1)}, u32[]{:S(2)}, u32[]{:S(2)}) collective-permute-start(bf16[64,1536]{1,0:T(8,128)(2,1)S(1)} %get-tuple-element.223), channel_id=1, source_target_pairs={{0,0},{1,1},{2,8},{3,9},{4,4},{5,5},{6,12},{7,13},{8,2},{9,3},{10,... | collective-permute-start | bytes 589832 | tf_op jit(solution)/shard_map/ppermute | solution.py:862
  29.8 16.4 %collective-permute-start.3 = (bf16[64,1536]{1,0:T(8,128)(2,1)S(1)}, bf16[64,1536]{1,0:T(8,128)(2,1)S(1)}, u32[]{:S(2)}, u32[]{:S(2)}) collective-permute-start(bf16[64,1536]{1,0:T(8,128)(2,1)S(1)} %get-tuple-element.224), channel_id=1, source_target_pairs={{0,18},{1,19},{2,26},{3,27},{4,22},{5,23},{6,30},{7,31},{8,16},{9,... | collective-permute-start | bytes 589832 | tf_op jit(solution)/shard_map/ppermute | solution.py:862
  29.9 18.2 %collective-permute-start.2 = (bf16[64,1536]{1,0:T(8,128)(2,1)S(1)}, bf16[64,1536]{1,0:T(8,128)(2,1)S(1)}, u32[]{:S(2)}, u32[]{:S(2)}) collective-permute-start(bf16[64,1536]{1,0:T(8,128)(2,1)S(1)} %get-tuple-element.225), channel_id=1, source_target_pairs={{0,16},{1,17},{2,24},{3,25},{4,20},{5,21},{6,28},{7,29},{8,18},{9,... | collective-permute-start | bytes 589832 | tf_op jit(solution)/shard_map/ppermute | solution.py:862
  31.3 16.7 %collective-permute-start.1 = (bf16[64,1536]{1,0:T(8,128)(2,1)S(1)}, bf16[64,1536]{1,0:T(8,128)(2,1)S(1)}, u32[]{:S(2)}, u32[]{:S(2)}) collective-permute-start(bf16[64,1536]{1,0:T(8,128)(2,1)S(1)} %get-tuple-element.226), channel_id=1, source_target_pairs={{0,2},{1,3},{2,10},{3,11},{4,6},{5,7},{6,14},{7,15},{8,0},{9,1},{1... | collective-permute-start | bytes 589832 | tf_op jit(solution)/shard_map/ppermute | solution.py:862
  31.7 4.5 %collective-permute-start.13 = (bf16[48,768]{1,0:T(8,128)(2,1)S(1)}, bf16[48,768]{1,0:T(8,128)(2,1)S(1)}, u32[]{:S(2)}, u32[]{:S(2)}) collective-permute-start(bf16[48,768]{1,0:T(8,128)(2,1)S(1)} %maximum_select_fusion.5), channel_id=1, source_target_pairs={{0,16},{1,17},{2,18},{3,19},{4,20},{5,21},{6,22},{7,23},{8,24},{9,... | collective-permute-start | bytes 221192 | tf_op jit(solution)/shard_map/ppermute | solution.py:862
  36.3 70.3 %copy-start.16 = (bf16[48,1536]{1,0:T(8,128)(2,1)}, bf16[48,1536]{1,0:T(8,128)(2,1)S(1)}, u32[]{:S(2)}) copy-start(bf16[48,1536]{1,0:T(8,128)(2,1)S(1)} %maximum_select_fusion.4) | copy-start | bytes 442372
  51.5 18.3 %copy-start.15 = (bf16[256,1536]{1,0:T(8,128)(2,1)S(1)}, bf16[256,1536]{1,0:T(8,128)(2,1)}, u32[]{:S(2)}) copy-start(bf16[256,1536]{1,0:T(8,128)(2,1)} %get-tuple-element.91) | copy-start | bytes 2359300
  53.8 107.4 %all-gather.5.cloned.1.call-start = ((), (), s32[]{:S(2)}) async-start(), calls=%async_computation.6 | async-start | bytes 7077888 | tf_op jit(solution)/shard_map/all_gather | solution.py:1100
  53.9 15.9 %collective-permute-start.6 = (bf16[384,384]{1,0:T(8,128)(2,1)S(1)}, bf16[384,384]{1,0:T(8,128)(2,1)S(1)}, u32[]{:S(2)}, u32[]{:S(2)}) collective-permute-start(bf16[384,384]{1,0:T(8,128)(2,1)S(1)} %copy-done.34), channel_id=1, source_target_pairs={{0,2},{1,3},{2,10},{3,11},{4,6},{5,7},{6,14},{7,15},{8,0},{9,1},{1... | collective-permute-start | bytes 884744 | tf_op jit(solution)/shard_map/ppermute | solution.py:862
  53.9 15.9 %collective-permute-start.5 = (bf16[384,384]{1,0:T(8,128)(2,1)S(1)}, bf16[384,384]{1,0:T(8,128)(2,1)S(1)}, u32[]{:S(2)}, u32[]{:S(2)}) collective-permute-start(bf16[384,384]{1,0:T(8,128)(2,1)S(1)} %copy-done.34), channel_id=1, source_target_pairs={{0,0},{1,1},{2,8},{3,9},{4,4},{5,5},{6,12},{7,13},{8,2},{9,3},{10,... | collective-permute-start | bytes 884744 | tf_op jit(solution)/shard_map/ppermute | solution.py:862
  69.9 13.1 %collective-permute-start.7 = (bf16[64,1536]{1,0:T(8,128)(2,1)S(1)}, bf16[64,1536]{1,0:T(8,128)(2,1)S(1)}, u32[]{:S(2)}, u32[]{:S(2)}) collective-permute-start(bf16[64,1536]{1,0:T(8,128)(2,1)S(1)} %get-tuple-element.219), channel_id=1, source_target_pairs={{0,0},{1,1},{2,8},{3,9},{4,4},{5,5},{6,12},{7,13},{8,2},{9,3},{10,... | collective-permute-start | bytes 589832 | tf_op jit(solution)/shard_map/ppermute | solution.py:862
  71.8 11.9 %collective-permute-start.10 = (bf16[64,1536]{1,0:T(8,128)(2,1)S(1)}, bf16[64,1536]{1,0:T(8,128)(2,1)S(1)}, u32[]{:S(2)}, u32[]{:S(2)}) collective-permute-start(bf16[64,1536]{1,0:T(8,128)(2,1)S(1)} %get-tuple-element.220), channel_id=1, source_target_pairs={{0,18},{1,19},{2,26},{3,27},{4,22},{5,23},{6,30},{7,31},{8,16},{9,... | collective-permute-start | bytes 589832 | tf_op jit(solution)/shard_map/ppermute | solution.py:862
  71.9 20.6 %collective-permute-start.9 = (bf16[64,1536]{1,0:T(8,128)(2,1)S(1)}, bf16[64,1536]{1,0:T(8,128)(2,1)S(1)}, u32[]{:S(2)}, u32[]{:S(2)}) collective-permute-start(bf16[64,1536]{1,0:T(8,128)(2,1)S(1)} %get-tuple-element.221), channel_id=1, source_target_pairs={{0,16},{1,17},{2,24},{3,25},{4,20},{5,21},{6,28},{7,29},{8,18},{9,... | collective-permute-start | bytes 589832 | tf_op jit(solution)/shard_map/ppermute | solution.py:862
  75.6 16.9 %collective-permute-start.8 = (bf16[64,1536]{1,0:T(8,128)(2,1)S(1)}, bf16[64,1536]{1,0:T(8,128)(2,1)S(1)}, u32[]{:S(2)}, u32[]{:S(2)}) collective-permute-start(bf16[64,1536]{1,0:T(8,128)(2,1)S(1)} %get-tuple-element.222), channel_id=1, source_target_pairs={{0,2},{1,3},{2,10},{3,11},{4,6},{5,7},{6,14},{7,15},{8,0},{9,1},{1... | collective-permute-start | bytes 589832 | tf_op jit(solution)/shard_map/ppermute | solution.py:862
  96.0 184.7 %reduce-scatter.4.cloned.1.call-start = ((), (), s32[]{:S(2)}) async-start(), calls=%async_computation.3 | async-start | bytes 7077888 | tf_op jit(solution)/shard_map/reduce_scatter | solution.py:1136
  96.5 15.2 %collective-permute-start.16 = (bf16[768,384]{1,0:T(8,128)(2,1)S(1)}, bf16[768,384]{1,0:T(8,128)(2,1)S(1)}, u32[]{:S(2)}, u32[]{:S(2)}) collective-permute-start(bf16[768,384]{1,0:T(8,128)(2,1)S(1)} %maximum_select_fusion.3), channel_id=1, source_target_pairs={{0,16},{1,17},{2,18},{3,19},{4,20},{5,21},{6,22},{7,23},{8,24},{9,... | collective-permute-start | bytes 1769480 | tf_op jit(solution)/shard_map/ppermute | solution.py:862
  98.3 26.4 %collective-permute-start.15 = (bf16[2,384,384]{2,1,0:T(8,128)(2,1)S(1)}, bf16[2,384,384]{2,1,0:T(8,128)(2,1)S(1)}, u32[]{:S(2)}, u32[]{:S(2)}) collective-permute-start(bf16[2,384,384]{2,1,0:T(8,128)(2,1)S(1)} %pad_maximum_fusion.4), channel_id=1, source_target_pairs={{0,2},{1,3},{2,10},{3,11},{4,6},{5,7},{6,14},{7,15},{8,0},{9,1},{1... | collective-permute-start | bytes 1769480 | tf_op jit(solution)/shard_map/ppermute | solution.py:862
  98.7 28.4 %collective-permute-start.14 = (bf16[2,384,384]{2,1,0:T(8,128)(2,1)S(1)}, bf16[2,384,384]{2,1,0:T(8,128)(2,1)S(1)}, u32[]{:S(2)}, u32[]{:S(2)}) collective-permute-start(bf16[2,384,384]{2,1,0:T(8,128)(2,1)S(1)} %pad_maximum_fusion.4), channel_id=1, source_target_pairs={{0,0},{1,1},{2,8},{3,9},{4,4},{5,5},{6,12},{7,13},{8,2},{9,3},{10,... | collective-permute-start | bytes 1769480 | tf_op jit(solution)/shard_map/ppermute | solution.py:862
  130.4 28.4 %collective-permute-start.17 = (bf16[2,768,384]{2,1,0:T(8,128)(2,1)S(1)}, bf16[2,768,384]{2,1,0:T(8,128)(2,1)S(1)}, u32[]{:S(2)}, u32[]{:S(2)}) collective-permute-start(bf16[2,768,384]{2,1,0:T(8,128)(2,1)S(1)} %maximum_select_fusion.2), channel_id=1, source_target_pairs={{0,16},{1,17},{2,18},{3,19},{4,20},{5,21},{6,22},{7,23},{8,24},{9,... | collective-permute-start | bytes 3538952 | tf_op jit(solution)/shard_map/ppermute | solution.py:862
  182.8 21.3 %slice-start = ((s8[6291456]{0:T(1024)(128)(4,1)}), s8[2097152]{0:T(1024)(128)(4,1)S(1)}, s32[]{:S(2)}) async-start(s8[6291456]{0:T(1024)(128)(4,1)} %bitcast.125), calls=%async_computation.8 | async-start | bytes 4194304
  182.8 217.6 %reduce-scatter.8.cloned.1.call-start = ((), (), s32[]{:S(2)}) async-start(), calls=%async_computation.5 | async-start | bytes 1474560 | tf_op jit(solution)/shard_map/reduce_scatter | solution.py:1164
  183.6 1.3 collective-permute-start.18
  184.9 3.6 collective-permute-start.19
  188.5 4.6 %collective-permute-start.20 = (f32[8,2048]{1,0:T(8,128)S(1)}, f32[8,2048]{1,0:T(8,128)S(1)}, u32[]{:S(2)}, u32[]{:S(2)}) collective-permute-start(f32[8,2048]{1,0:T(8,128)S(1)} %add.257), channel_id=1, source_target_pairs={{0,4},{1,5},{2,6},{3,7},{4,0},{5,1},{6,2},{7,3},{8,12},{9,13},{10,... | collective-permute-start | bytes 196616 | tf_op jit(solution)/shard_map/ppermute | solution.py:862
  243.2 30.2 %collective-permute-start.21 = (bf16[2,2,128,1536]{3,2,0,1:T(8,128)(2,1)S(1)}, bf16[2,2,128,1536]{3,2,0,1:T(8,128)(2,1)}, u32[]{:S(2)}, u32[]{:S(2)}) collective-permute-start(bf16[2,2,128,1536]{3,2,0,1:T(8,128)(2,1)S(1)} %copy.78), channel_id=1, source_target_pairs={{0,8},{1,9},{2,10},{3,11},{4,12},{5,13},{6,14},{7,15},{8,0},{9,1},... | collective-permute-start | bytes 4718600 | tf_op jit(solution)/shard_map/ppermute | solution.py:862
  245.0 25.2 %copy-start.23 = (f32[16,384]{1,0:T(8,128)S(1)}, f32[16,384]{1,0:T(8,128)}, u32[]{:S(2)}) copy-start(f32[16,384]{1,0:T(8,128)} %get-tuple-element.138) | copy-start | bytes 73732
  245.0 28.4 %copy-start.10 = (bf16[2,2,128,1536]{3,2,1,0:T(8,128)(2,1)S(1)}, bf16[2,2,128,1536]{3,2,1,0:T(8,128)(2,1)}, u32[]{:S(2)}) copy-start(bf16[2,2,128,1536]{3,2,1,0:T(8,128)(2,1)} %get-tuple-element.121) | copy-start | bytes 4718596
  270.1 7.0 %collective-permute-start.22 = (bf16[2,2,128,1536]{3,2,1,0:T(8,128)(2,1)}, bf16[2,2,128,1536]{3,2,1,0:T(8,128)(2,1)}, u32[]{:S(2)}, u32[]{:S(2)}) collective-permute-start(bf16[2,2,128,1536]{3,2,1,0:T(8,128)(2,1)} %get-tuple-element.124), channel_id=1, source_target_pairs={{0,8},{1,9},{2,10},{3,11},{4,12},{5,13},{6,14},{7,15},{8,0},{9,1},... | collective-permute-start | bytes 4718600 | tf_op jit(solution)/shard_map/ppermute | solution.py:862
  280.7 124.7 %reduce-scatter.6.cloned.1.call-start = ((), (), s32[]{:S(2)}) async-start(), calls=%async_computation.4 | async-start | bytes 1474560 | tf_op jit(solution)/shard_map/reduce_scatter | solution.py:1164
  290.3 19.0 %collective-permute-start.24 = (bf16[2,128,1536]{2,1,0:T(8,128)(2,1)}, bf16[2,128,1536]{2,1,0:T(8,128)(2,1)}, u32[]{:S(2)}, u32[]{:S(2)}) collective-permute-start(bf16[2,128,1536]{2,1,0:T(8,128)(2,1)} %fusion.5), channel_id=1, source_target_pairs={{0,4},{1,5},{2,6},{3,7},{4,0},{5,1},{6,2},{7,3},{8,12},{9,13},{10,... | collective-permute-start | bytes 2359304 | tf_op jit(solution)/shard_map/ppermute | solution.py:862
  292.1 27.1 %collective-permute-start.23 = (bf16[2,128,1536]{2,1,0:T(8,128)(2,1)}, bf16[2,128,1536]{2,1,0:T(8,128)(2,1)}, u32[]{:S(2)}, u32[]{:S(2)}) collective-permute-start(bf16[2,128,1536]{2,1,0:T(8,128)(2,1)} %fusion.4), channel_id=1, source_target_pairs={{0,1},{1,0},{2,3},{3,2},{4,5},{5,4},{6,7},{7,6},{8,9},{9,8},{10,11... | collective-permute-start | bytes 2359304 | tf_op jit(solution)/shard_map/ppermute | solution.py:862
  293.2 8.9 %collective-permute-start.35 = (bf16[144,1536]{1,0:T(8,128)(2,1)}, bf16[144,1536]{1,0:T(8,128)(2,1)}, u32[]{:S(2)}, u32[]{:S(2)}) collective-permute-start(bf16[144,1536]{1,0:T(8,128)(2,1)} %pad_maximum_fusion.5), channel_id=1, source_target_pairs={{0,8},{1,9},{2,10},{3,11},{4,12},{5,13},{6,14},{7,15},{8,0},{9,1},... | collective-permute-start | bytes 1327112 | tf_op jit(solution)/shard_map/ppermute | solution.py:862
  302.1 34.5 %collective-permute-start.42 = (bf16[2,384,384]{2,1,0:T(8,128)(2,1)}, bf16[2,384,384]{2,1,0:T(8,128)(2,1)}, u32[]{:S(2)}, u32[]{:S(2)}) collective-permute-start(bf16[2,384,384]{2,1,0:T(8,128)(2,1)} %dynamic-slice_convert_fusion.2), channel_id=1, source_target_pairs={{0,16},{1,17},{2,18},{3,19},{4,20},{5,21},{6,22},{7,23},{8,24},{9,... | collective-permute-start | bytes 1769480 | tf_op jit(solution)/shard_map/ppermute | solution.py:862
  305.5 18.8 %collective-permute-start.36 = (bf16[80,1536]{1,0:T(8,128)(2,1)S(1)}, bf16[80,1536]{1,0:T(8,128)(2,1)S(1)}, u32[]{:S(2)}, u32[]{:S(2)}) collective-permute-start(bf16[80,1536]{1,0:T(8,128)(2,1)S(1)} %pad_maximum_fusion.6), channel_id=1, source_target_pairs={{0,1},{1,0},{2,3},{3,2},{4,5},{5,4},{6,7},{7,6},{8,9},{9,8},{10,11... | collective-permute-start | bytes 737288 | tf_op jit(solution)/shard_map/ppermute | solution.py:862
  320.5 16.0 %copy-start.5 = (f32[2,128,1536]{2,1,0:T(8,128)}, f32[2,128,1536]{2,1,0:T(8,128)S(1)}, u32[]{:S(2)}) copy-start(f32[2,128,1536]{2,1,0:T(8,128)S(1)} %bitcast_add_fusion.1) | copy-start | bytes 4718596
  329.4 60.9 %collective-permute-start.25 = (bf16[64,1536]{1,0:T(8,128)(2,1)}, bf16[64,1536]{1,0:T(8,128)(2,1)}, u32[]{:S(2)}, u32[]{:S(2)}) collective-permute-start(bf16[64,1536]{1,0:T(8,128)(2,1)} %get-tuple-element.215), channel_id=1, source_target_pairs={{0,0},{1,1},{8,2},{9,3},{4,4},{5,5},{12,6},{13,7},{2,8},{3,9},{10,... | collective-permute-start | bytes 589832 | tf_op jit(solution)/shard_map/ppermute | solution.py:862
  331.8 35.5 %collective-permute-start.30 = (bf16[64,1536]{1,0:T(8,128)(2,1)}, bf16[64,1536]{1,0:T(8,128)(2,1)}, u32[]{:S(2)}, u32[]{:S(2)}) collective-permute-start(bf16[64,1536]{1,0:T(8,128)(2,1)} %get-tuple-element.216), channel_id=1, source_target_pairs={{18,0},{19,1},{26,2},{27,3},{22,4},{23,5},{30,6},{31,7},{16,8},{17... | collective-permute-start | bytes 589832 | tf_op jit(solution)/shard_map/ppermute | solution.py:862
  333.3 37.1 %collective-permute-start.29 = (bf16[64,1536]{1,0:T(8,128)(2,1)}, bf16[64,1536]{1,0:T(8,128)(2,1)}, u32[]{:S(2)}, u32[]{:S(2)}) collective-permute-start(bf16[64,1536]{1,0:T(8,128)(2,1)} %get-tuple-element.217), channel_id=1, source_target_pairs={{16,0},{17,1},{24,2},{25,3},{20,4},{21,5},{28,6},{29,7},{18,8},{19... | collective-permute-start | bytes 589832 | tf_op jit(solution)/shard_map/ppermute | solution.py:862
  336.3 19.5 %collective-permute-start.27 = (bf16[128,1536]{1,0:T(8,128)(2,1)S(1)}, bf16[128,1536]{1,0:T(8,128)(2,1)S(1)}, u32[]{:S(2)}, u32[]{:S(2)}) collective-permute-start(bf16[128,1536]{1,0:T(8,128)(2,1)S(1)} %fusion.7), channel_id=1, source_target_pairs={{0,1},{1,0},{2,3},{3,2},{4,5},{5,4},{6,7},{7,6},{8,9},{9,8},{10,11... | collective-permute-start | bytes 1179656 | tf_op jit(solution)/shard_map/ppermute | solution.py:862
  336.6 5.7 %collective-permute-start.37 = (bf16[48,1536]{1,0:T(8,128)(2,1)S(1)}, bf16[48,1536]{1,0:T(8,128)(2,1)S(1)}, u32[]{:S(2)}, u32[]{:S(2)}) collective-permute-start(bf16[48,1536]{1,0:T(8,128)(2,1)S(1)} %pad_maximum_fusion.7), channel_id=1, source_target_pairs={{0,4},{1,5},{2,6},{3,7},{4,0},{5,1},{6,2},{7,3},{8,12},{9,13},{10,... | collective-permute-start | bytes 442376 | tf_op jit(solution)/shard_map/ppermute | solution.py:862
  339.9 18.0 %copy-start.8 = (f32[2,128,1536]{2,1,0:T(8,128)S(1)}, f32[2,128,1536]{2,1,0:T(8,128)}, u32[]{:S(2)}) copy-start(f32[2,128,1536]{2,1,0:T(8,128)} %copy-done.7) | copy-start | bytes 4718596
  342.3 16.7 %collective-permute-start.26 = (bf16[128,1536]{1,0:T(8,128)(2,1)S(1)}, bf16[128,1536]{1,0:T(8,128)(2,1)}, u32[]{:S(2)}, u32[]{:S(2)}) collective-permute-start(bf16[128,1536]{1,0:T(8,128)(2,1)S(1)} %fusion.6), channel_id=1, source_target_pairs={{0,4},{1,5},{2,6},{3,7},{4,0},{5,1},{6,2},{7,3},{8,12},{9,13},{10,... | collective-permute-start | bytes 1179656 | tf_op jit(solution)/shard_map/ppermute | solution.py:862
  343.6 16.4 %copy-start.6 = (f32[2,128,1536]{2,1,0:T(8,128)S(1)}, f32[2,128,1536]{2,1,0:T(8,128)}, u32[]{:S(2)}) copy-start(f32[2,128,1536]{2,1,0:T(8,128)} %copy-done.5) | copy-start | bytes 4718596
  355.8 23.2 %collective-permute-start.43 = (bf16[384,384]{1,0:T(8,128)(2,1)}, bf16[384,384]{1,0:T(8,128)(2,1)S(1)}, u32[]{:S(2)}, u32[]{:S(2)}) collective-permute-start(bf16[384,384]{1,0:T(8,128)(2,1)} %get-tuple-element.227), channel_id=1, source_target_pairs={{0,0},{1,1},{8,2},{9,3},{4,4},{5,5},{12,6},{13,7},{2,8},{3,9},{10,... | collective-permute-start | bytes 884744 | tf_op jit(solution)/shard_map/ppermute | solution.py:862
  359.0 8.2 %collective-permute-start.38 = (bf16[2,80,384]{2,1,0:T(8,128)(2,1)S(1)}, bf16[2,80,384]{2,1,0:T(8,128)(2,1)S(1)}, u32[]{:S(2)}, u32[]{:S(2)}) collective-permute-start(bf16[2,80,384]{2,1,0:T(8,128)(2,1)S(1)} %pad_maximum_fusion.8), channel_id=1, source_target_pairs={{0,16},{1,17},{2,18},{3,19},{4,20},{5,21},{6,22},{7,23},{8,24},{9,... | collective-permute-start | bytes 368648 | tf_op jit(solution)/shard_map/ppermute | solution.py:862
  367.2 11.9 %collective-permute-start.44 = (bf16[384,384]{1,0:T(8,128)(2,1)S(1)}, bf16[384,384]{1,0:T(8,128)(2,1)S(1)}, u32[]{:S(2)}, u32[]{:S(2)}) collective-permute-start(bf16[384,384]{1,0:T(8,128)(2,1)S(1)} %copy-done.19), channel_id=1, source_target_pairs={{2,0},{3,1},{10,2},{11,3},{6,4},{7,5},{14,6},{15,7},{0,8},{1,9},{8... | collective-permute-start | bytes 884744 | tf_op jit(solution)/shard_map/ppermute | solution.py:862
  367.3 16.6 %collective-permute-start.28 = (bf16[64,1536]{1,0:T(8,128)(2,1)S(1)}, bf16[64,1536]{1,0:T(8,128)(2,1)S(1)}, u32[]{:S(2)}, u32[]{:S(2)}) collective-permute-start(bf16[64,1536]{1,0:T(8,128)(2,1)S(1)} %copy-done.20), channel_id=1, source_target_pairs={{2,0},{3,1},{10,2},{11,3},{6,4},{7,5},{14,6},{15,7},{0,8},{1,9},{8... | collective-permute-start | bytes 589832 | tf_op jit(solution)/shard_map/ppermute | solution.py:862
  370.4 34.9 %collective-permute-start.31 = (bf16[64,1536]{1,0:T(8,128)(2,1)S(1)}, bf16[64,1536]{1,0:T(8,128)(2,1)S(1)}, u32[]{:S(2)}, u32[]{:S(2)}) collective-permute-start(bf16[64,1536]{1,0:T(8,128)(2,1)S(1)} %get-tuple-element.211), channel_id=1, source_target_pairs={{0,0},{1,1},{8,2},{9,3},{4,4},{5,5},{12,6},{13,7},{2,8},{3,9},{10,... | collective-permute-start | bytes 589832 | tf_op jit(solution)/shard_map/ppermute | solution.py:862
  379.1 26.3 %collective-permute-start.34 = (bf16[64,1536]{1,0:T(8,128)(2,1)S(1)}, bf16[64,1536]{1,0:T(8,128)(2,1)S(1)}, u32[]{:S(2)}, u32[]{:S(2)}) collective-permute-start(bf16[64,1536]{1,0:T(8,128)(2,1)S(1)} %get-tuple-element.212), channel_id=1, source_target_pairs={{18,0},{19,1},{26,2},{27,3},{22,4},{23,5},{30,6},{31,7},{16,8},{17... | collective-permute-start | bytes 589832 | tf_op jit(solution)/shard_map/ppermute | solution.py:862
  379.1 26.2 %collective-permute-start.33 = (bf16[64,1536]{1,0:T(8,128)(2,1)S(1)}, bf16[64,1536]{1,0:T(8,128)(2,1)S(1)}, u32[]{:S(2)}, u32[]{:S(2)}) collective-permute-start(bf16[64,1536]{1,0:T(8,128)(2,1)S(1)} %get-tuple-element.213), channel_id=1, source_target_pairs={{16,0},{17,1},{24,2},{25,3},{20,4},{21,5},{28,6},{29,7},{18,8},{19... | collective-permute-start | bytes 589832 | tf_op jit(solution)/shard_map/ppermute | solution.py:862
  383.9 12.9 %collective-permute-start.39 = (bf16[80,384]{1,0:T(8,128)(2,1)S(1)}, bf16[80,384]{1,0:T(8,128)(2,1)S(1)}, u32[]{:S(2)}, u32[]{:S(2)}) collective-permute-start(bf16[80,384]{1,0:T(8,128)(2,1)S(1)} %get-tuple-element.251), channel_id=1, source_target_pairs={{0,0},{1,1},{8,2},{9,3},{4,4},{5,5},{12,6},{13,7},{2,8},{3,9},{10,... | collective-permute-start | bytes 184328 | tf_op jit(solution)/shard_map/ppermute | solution.py:862
  390.3 6.6 %collective-permute-start.40 = (bf16[80,384]{1,0:T(8,128)(2,1)S(1)}, bf16[80,384]{1,0:T(8,128)(2,1)S(1)}, u32[]{:S(2)}, u32[]{:S(2)}) collective-permute-start(bf16[80,384]{1,0:T(8,128)(2,1)S(1)} %get-tuple-element.252), channel_id=1, source_target_pairs={{2,0},{3,1},{10,2},{11,3},{6,4},{7,5},{14,6},{15,7},{0,8},{1,9},{8... | collective-permute-start | bytes 184328 | tf_op jit(solution)/shard_map/ppermute | solution.py:862
  396.9 8.4 %collective-permute-start.32 = (bf16[64,1536]{1,0:T(8,128)(2,1)S(1)}, bf16[64,1536]{1,0:T(8,128)(2,1)S(1)}, u32[]{:S(2)}, u32[]{:S(2)}) collective-permute-start(bf16[64,1536]{1,0:T(8,128)(2,1)S(1)} %get-tuple-element.214), channel_id=1, source_target_pairs={{2,0},{3,1},{10,2},{11,3},{6,4},{7,5},{14,6},{15,7},{0,8},{1,9},{8... | collective-permute-start | bytes 589832 | tf_op jit(solution)/shard_map/ppermute | solution.py:862
  400.5 11.8 %collective-permute-start.45 = (bf16[384,384]{1,0:T(8,128)(2,1)}, bf16[384,384]{1,0:T(8,128)(2,1)S(1)}, u32[]{:S(2)}, u32[]{:S(2)}) collective-permute-start(bf16[384,384]{1,0:T(8,128)(2,1)} %reduce-scatter.8.cloned.1.call-done), channel_id=1, source_target_pairs={{0,0},{1,1},{8,2},{9,3},{4,4},{5,5},{12,6},{13,7},{2,8},{3,9},{10,... | collective-permute-start | bytes 884744 | tf_op jit(solution)/shard_map/ppermute | solution.py:862
  405.4 12.5 %collective-permute-start.41 = (bf16[384,384]{1,0:T(8,128)(2,1)}, bf16[384,384]{1,0:T(8,128)(2,1)S(1)}, u32[]{:S(2)}, u32[]{:S(2)}) collective-permute-start(bf16[384,384]{1,0:T(8,128)(2,1)} %reduce-scatter.6.cloned.1.call-done), channel_id=1, source_target_pairs={{0,0},{1,1},{8,2},{9,3},{4,4},{5,5},{12,6},{13,7},{2,8},{3,9},{10,... | collective-permute-start | bytes 884744 | tf_op jit(solution)/shard_map/ppermute | solution.py:862
  (26 other events, 148.3 us)
Sparse Core Ops, SparseCore 0:
  53.9 60.6 all-gather.6
  116.8 37.5 all-gather.4
  183.0 67.6 reduce-scatter.3
  280.8 36.4 reduce-scatter.7
  320.1 50.4 reduce-scatter.5

commit v3 on v2

--- a/solution.py
+++ b/solution.py
@@ -16,7 +16,7 @@
 SUB = 128
 ROWS = 256
 LANES = 128
-VMEM_BYTES = 56 * 1024 * 1024
+MIB = 1024 * 1024
 
 
 def dot_nn(a, b):
@@ -159,8 +159,8 @@
     pair_width = conv_pair_ref.shape[-1]
     pair = small[:, :pair_width]
     step = small[:, pair_width : pair_width + LANES]
-    value_ref[...] = value
-    pair_ref[...] = pair
+    value_ref[...] = value.astype(BF16)
+    pair_ref[...] = pair.astype(BF16)
     step_ref[...] = step
 
     places = base + iota((ROWS, LANES), 0)
@@ -206,8 +206,9 @@
         stepped = mixed[rows] * steps_wide
         stepped_low = stepped.astype(BF16)
         held = state[...]
-        states_ref[sub] = held
-        outside = dot_nn(reads, held.astype(BF16)) * reach_wide
+        held_low = held.astype(BF16)
+        states_ref[sub] = held_low
+        outside = dot_nn(reads, held_low) * reach_wide
         inside = []
         for p in range(pair_count):
             cols = slice(p * LANES, (p + 1) * LANES)
@@ -261,7 +262,7 @@
     grad = dot_nn(back_ref[...].reshape(ROWS, back_ref.shape[-1]), w_out_ref[...])
     live_wide = jnp.concatenate([live] * (grad.shape[1] // LANES), axis=1)
     grad = jnp.where(live_wide, grad, 0.0)
-    grad_normed_ref[...] = grad
+    grad_normed_ref[...] = grad.astype(BF16)
     ones = jnp.ones((8, gated.shape[1]), BF16)
     high, low = split_two(gated * gated)
     square = dot_nt(ones, high) + dot_nt(ones, low)
@@ -296,7 +297,7 @@
     live = segment_of(block * ROWS + iota((ROWS, LANES), 0), bounds) < live_ids
     gate = gate_ref[...]
     scanned = scanned_ref[...]
-    grad_normed = grad_normed_ref[...]
+    grad_normed = grad_normed_ref[...].astype(F32)
     norm_gate = norm_gate_ref[...]
     stats = stats_ref[...].T / inner_full
     spread = lax.rsqrt(stats[:, 0:1] + EPS)
@@ -309,7 +310,7 @@
     normed_out = jnp.where(live_wide, normed_gated * norm_gate, 0.0).astype(BF16)
     normed_out_ref[...] = normed_out.reshape(normed_out_ref.shape)
     grad_gated = spread * (grad_normed * norm_gate - normed_gated * (spread * cross))
-    grad_scanned_ref[...] = grad_gated * act
+    grad_scanned_ref[...] = (grad_gated * act).astype(BF16)
     low_gate_ref[...] = (
         grad_gated * scanned * (sg * (1.0 + gate * (1.0 - sg)))
     ).astype(BF16)
@@ -374,7 +375,8 @@
 
     width = value_ref.shape[1]
     scanned = scanned_ref[...]
-    grad_scanned = grad_scanned_ref[...]
+    grad_low_all = grad_scanned_ref[...]
+    grad_scanned = grad_low_all.astype(F32)
     low_gate = low_gate_ref[...]
 
     conv_value = conv_value_ref[...]
@@ -411,8 +413,8 @@
         stepped = sub_mixed * steps_wide
         stepped_low = stepped.astype(BF16)
         grad_y = grad_scanned[rows]
-        grad_low = grad_y.astype(BF16)
-        held = states_ref[sub]
+        grad_low = grad_low_all[rows]
+        held_low = states_ref[sub]
         later = state[...]
         later_low = later.astype(BF16)
         grad_scores = jnp.zeros((SUB, SUB), F32)
@@ -436,17 +438,17 @@
         grad_stepped = jnp.concatenate(inner, axis=1) + tail_part
         reached = (grad_y * reach_wide).astype(BF16)
         tailed = (stepped * tail_wide).astype(BF16)
-        grad_reads = dot_nn(grad_scores, keys) + dot_nt(reached, held.astype(BF16))
+        grad_reads = dot_nn(grad_scores, keys) + dot_nt(reached, held_low)
         grad_keys = dot_tn(grad_scores, reads) + dot_nt(tailed, later_low)
         stepped_back = stepped_low.astype(F32)
         per_log = reduce_heads(
-            grad_low.astype(F32) * (scanned[rows] - skip * sub_mixed)
+            grad_y * (scanned[rows] - skip * sub_mixed)
             - stepped_back * grad_stepped,
             gather_ref,
         )
         kept_wide = reach_wide[SUB - 1 : SUB, :]
         at_end = jnp.sum(stepped_back * tail_part, axis=0, keepdims=True) + kept_wide * jnp.sum(
-            later * held, axis=0, keepdims=True
+            later * held_low.astype(F32), axis=0, keepdims=True
         )
         at_end = reduce_heads(jnp.broadcast_to(at_end, (8, width)), gather_ref)[0:1, :]
         grad_log = (
@@ -481,10 +483,10 @@
     q_value = grad_mixed * (sig_value * (1.0 + conv_value * (1.0 - sig_value)))
     q_pair = grad_shared * (sig_pair * (1.0 + conv_pair * (1.0 - sig_pair)))
     grad_value, value_sums = convolve_back(
-        q_value, halo_value[...], value_ref[...], taps_value_ref[...]
+        q_value, halo_value[...], value_ref[...].astype(F32), taps_value_ref[...]
     )
     grad_pair, pair_sums = convolve_back(
-        q_pair, halo_pair[...], pair_ref[...], taps_pair_ref[...]
+        q_pair, halo_pair[...], pair_ref[...].astype(F32), taps_pair_ref[...]
     )
     halo_value[...] = q_value[:8, :]
     halo_pair[...] = q_pair[:8, :]
@@ -531,8 +533,8 @@
     return pl.BlockSpec(memory_space=pltpu.SMEM)
 
 
-def kernel_params():
-    return pltpu.CompilerParams(vmem_limit_bytes=VMEM_BYTES)
+def kernel_params(size):
+    return pltpu.CompilerParams(vmem_limit_bytes=size * MIB)
 
 
 def head_constants(head_count, head_width):
@@ -581,6 +583,7 @@
 
     wholes = [norm_in, w_value, w_small, taps_value, taps_pair, heads, skip, spread, lower]
     widths = [width, width, pair_width, pair_width, LANES, width]
+    types = [BF16, F32, BF16, F32, F32, F32]
     return pl.pallas_call(
         partial(forward_kernel, width // LANES),
         grid=(micro_count, blocks),
@@ -591,16 +594,16 @@
             pl.BlockSpec((subs, LANES, width), lambda b, i: (b * blocks + i, 0, 0)),
         ],
         out_shape=[jax.ShapeDtypeStruct((length, full), BF16)]
-        + [jax.ShapeDtypeStruct((length, cols), F32) for cols in widths]
+        + [jax.ShapeDtypeStruct((length, cols), kind) for cols, kind in zip(widths, types)]
         + [
-            jax.ShapeDtypeStruct((length // SUB, LANES, width), F32),
+            jax.ShapeDtypeStruct((length // SUB, LANES, width), BF16),
         ],
         scratch_shapes=[
             pltpu.VMEM((8, width), F32),
             pltpu.VMEM((8, pair_width), F32),
             pltpu.VMEM((LANES, width), F32),
         ],
-        compiler_params=kernel_params(),
+        compiler_params=kernel_params(56),
         cost_estimate=cost(length * full * width * 12, length * width * 8, length * width * 40),
         name="forward",
     )(bounds, rows, *wholes)
@@ -632,10 +635,10 @@
         out_shape=[
             jax.ShapeDtypeStruct((length, width), F32),
             jax.ShapeDtypeStruct(back.shape[:4] + (width,), BF16),
-            jax.ShapeDtypeStruct((length, width), F32),
+            jax.ShapeDtypeStruct((length, width), BF16),
             jax.ShapeDtypeStruct((8, length), F32),
         ],
-        compiler_params=kernel_params(),
+        compiler_params=kernel_params(56),
         cost_estimate=cost(length * full * width * 4, length * width, length * width * 30),
         name="back",
     )(bounds, back, normed, w_gate, w_out, norm_gate, scanned)
@@ -666,10 +669,10 @@
         out_shape=[
             jax.ShapeDtypeStruct((length, width), BF16),
             jax.ShapeDtypeStruct((blocks // 2, 2, 2, micro_count * piece, width), BF16),
-            jax.ShapeDtypeStruct((length, width), F32),
+            jax.ShapeDtypeStruct((length, width), BF16),
             jax.ShapeDtypeStruct((8, width), F32),
         ],
-        compiler_params=kernel_params(),
+        compiler_params=kernel_params(56),
         cost_estimate=cost(length * width * 20, length * width, length * width * 20),
         name="gate",
     )(bounds, stats, grad_normed, gate, scanned, norm_gate)
@@ -733,7 +736,7 @@
             pltpu.VMEM((8, pair_width), F32),
             pltpu.VMEM((LANES, width), F32),
         ],
-        compiler_params=kernel_params(),
+        compiler_params=kernel_params(56),
         cost_estimate=cost(block_len * full * width * 14, block_len * width * 16, block_len * width * 40),
         name="backward",
     )(*ins, *([] if earlier is None else earlier))
@@ -748,10 +751,9 @@
     own_col_ref,
     tokens_ref,
     cotangent_ref,
-    send_tokens_ref,
-    send_cotangent_ref,
     send_map_ref,
     take_map_ref,
+    *piece_refs,
 ):
     start, group, target = place_ref[0], place_ref[1], place_ref[2]
     share = tokens_ref.shape[0]
@@ -778,69 +780,146 @@
     order = jnp.sum(ahead, axis=1, keepdims=True)
     wanted = ((src_col ^ target) * quota).astype(F32) + order
     take_map_ref[...] = (iota((share, share), 1).astype(F32) == wanted).astype(BF16)
-    send_tokens_ref[...] = dot_nn(send_map, tokens_ref[...]).astype(BF16)
-    send_cotangent_ref[...] = dot_nn(send_map, cotangent_ref[...]).astype(BF16)
+    write_pieces(piece_refs[:group_count], dot_nn(send_map, tokens_ref[...]))
+    write_pieces(piece_refs[group_count:], dot_nn(send_map, cotangent_ref[...]))
+
+
+def write_pieces(piece_refs, rows):
+    size = rows.shape[0] // len(piece_refs)
+    for k, piece_ref in enumerate(piece_refs):
+        piece_ref[...] = rows[k * size : (k + 1) * size].astype(BF16)
+
+
+def join_pieces(piece_refs):
+    if piece_refs[0].shape[0] % 16 == 0:
+        return jnp.concatenate([piece_ref[...] for piece_ref in piece_refs], axis=0)
+    wide = [piece_ref[...].astype(F32) for piece_ref in piece_refs]
+    return jnp.concatenate(wide, axis=0).astype(BF16)
 
 
 def run_deal(place, listed, own, tokens, cotangent, group_len):
     share, width = tokens.shape
+    group_count = listed.shape[0]
     vmem = pl.BlockSpec(memory_space=pltpu.VMEM)
-    return pl.pallas_call(
+    piece = jax.ShapeDtypeStruct((share // group_count, width), BF16)
+    outs = pl.pallas_call(
         partial(deal_kernel, group_len.bit_length() - 1),
         in_specs=[smem_spec()] + [vmem] * 6,
-        out_specs=[vmem] * 4,
-        out_shape=[jax.ShapeDtypeStruct((share, width), BF16)] * 2
-        + [jax.ShapeDtypeStruct((share, share), BF16)] * 2,
-        compiler_params=kernel_params(),
+        out_specs=[vmem] * (2 + 2 * group_count),
+        out_shape=[jax.ShapeDtypeStruct((share, share), BF16)] * 2
+        + [piece] * (2 * group_count),
+        compiler_params=kernel_params(16),
         name="deal",
     )(place, listed, listed.T, own[None, :], own[:, None], tokens, cotangent)
-
-
-def pick_kernel(transposed, map_ref, rows_ref, out_ref):
+    return outs[2 : 2 + group_count], outs[2 + group_count :], outs[0], outs[1]
+
+
+def pick_kernel(transposed, extra_rows, map_ref, *refs):
+    out_ref = refs[-1]
+    pieces = refs[:-1]
+    if extra_rows:
+        share = out_ref.shape[0] - extra_rows
+        out_ref[share:, :] = pieces[-1][...]
+        pieces = pieces[:-1]
     dot = dot_tn if transposed else dot_nn
-    out_ref[...] = dot(map_ref[...], rows_ref[...]).astype(BF16)
-
-
-def run_pick(take_map, rows, transposed):
+    rows = dot(map_ref[...], join_pieces(pieces)).astype(BF16)
+    if extra_rows:
+        out_ref[:share, :] = rows
+    else:
+        out_ref[...] = rows
+
+
+def run_pick(take_map, pieces, transposed, extra=None):
     vmem = pl.BlockSpec(memory_space=pltpu.VMEM)
+    extra_rows = 0 if extra is None else extra.shape[0]
+    items = list(pieces) + ([] if extra is None else [extra])
     return pl.pallas_call(
-        partial(pick_kernel, transposed),
-        in_specs=[vmem] * 2,
+        partial(pick_kernel, transposed, extra_rows),
+        in_specs=[vmem] * (1 + len(items)),
         out_specs=vmem,
-        out_shape=jax.ShapeDtypeStruct((take_map.shape[0], rows.shape[1]), BF16),
-        compiler_params=kernel_params(),
+        out_shape=jax.ShapeDtypeStruct(
+            (take_map.shape[0] + extra_rows, pieces[0].shape[1]), BF16
+        ),
+        compiler_params=kernel_params(16),
         name="pick",
-    )(take_map, rows)
-
-
-def close_out_kernel(map_ref, dealt_ref, branch_ref, weight_ref, out_ref):
+    )(take_map, *items)
+
+
+def close_out_kernel(map_ref, dealt_ref, branch_ref, weight_ref, *piece_refs):
     shape = dealt_ref.shape
     out = dealt_ref[...].astype(F32) + weight_ref[...] * branch_ref[...].reshape(shape).astype(F32)
-    out_ref[...] = dot_tn(map_ref[...], out.astype(BF16)).astype(BF16)
-
-
-def close_back_kernel(map_ref, dealt_ref, back_ref, norm_in_ref, *refs):
-    grad_refs, out_ref = refs[:-1], refs[-1]
+    write_pieces(piece_refs, dot_tn(map_ref[...], out.astype(BF16)))
+
+
+def close_back_kernel(
+    grad_count, map_ref, dealt_ref, back_ref, norm_in_ref, *refs
+):
+    grad_refs, piece_refs = refs[: 2 * grad_count], refs[2 * grad_count :]
     x = dealt_ref[...].astype(F32)
     rms = lax.rsqrt(jnp.mean(x * x, axis=1, keepdims=True) + EPS)
     xhat = x * rms
-    grad = jnp.concatenate([item[...].astype(F32) for item in grad_refs], axis=0)
+    grad = jnp.concatenate(
+        [
+            grad_refs[2 * k][...] + grad_refs[2 * k + 1][...].astype(F32)
+            for k in range(grad_count)
+        ],
+        axis=0,
+    )
     win = grad * norm_in_ref[...].astype(F32)
     cross = jnp.mean(win * xhat, axis=1, keepdims=True)
     out = back_ref[...].astype(F32) + rms * (win - xhat * cross)
-    out_ref[...] = dot_tn(map_ref[...], out.astype(BF16)).astype(BF16)
-
-
-def run_close(body, take_map, *items):
-    vmem = pl.BlockSpec(memory_space=pltpu.VMEM)
+    write_pieces(piece_refs, dot_tn(map_ref[...], out.astype(BF16)))
+
+
+def run_close(body, group_count, take_map, dealt, *items):
+    share, width = take_map.shape[0], dealt.shape[1]
+    whole = [whole_spec(item.shape) for item in items]
     return pl.pallas_call(
         body,
-        in_specs=[vmem] * (1 + len(items)),
-        out_specs=vmem,
-        out_shape=jax.ShapeDtypeStruct(items[0].shape, BF16),
-        compiler_params=kernel_params(),
+        grid=(1,),
+        in_specs=[whole_spec(take_map.shape), whole_spec((share, width))] + whole,
+        out_specs=[whole_spec((share // group_count, width))] * group_count,
+        out_shape=[jax.ShapeDtypeStruct((share // group_count, width), BF16)] * group_count,
+        compiler_params=kernel_params(16),
         name="close",
-    )(take_map, *items)
+    )(take_map, dealt, *items)
+
+
+def halves_kernel(axes, bits_ref, *refs):
+    count = len(axes)
+    for k, (axis, bit_index) in enumerate(axes):
+        held_ref, arrived_ref = refs[2 * k], refs[2 * k + 1]
+        keep_ref, send_ref = refs[2 * (count + k)], refs[2 * (count + k) + 1]
+        bit = bits_ref[bit_index]
+
+        def total(where):
+            return held_ref[where].astype(F32) + arrived_ref[where].astype(F32)
+
+        if len(held_ref.shape) == 3:
+            keep_ref[...] = total(bit)
+            send_ref[...] = total(1 - bit).astype(BF16)
+            continue
+        for other in range(2):
+            here = (other, bit) if axis == 1 else (bit, other)
+            there = (other, 1 - bit) if axis == 1 else (1 - bit, other)
+            keep_ref[other] = total(here)
+            send_ref[other] = total(there).astype(BF16)
+
+
+def run_halves(axes, bits, *items):
+    vmem = pl.BlockSpec(memory_space=pltpu.VMEM)
+    outs = []
+    for item in items[::2]:
+        outs.append(jax.ShapeDtypeStruct(item.shape[1:], F32))
+        outs.append(jax.ShapeDtypeStruct(item.shape[1:], BF16))
+    return pl.pallas_call(
+        partial(halves_kernel, axes),
+        in_specs=[smem_spec()] + [vmem] * len(items),
+        out_specs=[vmem] * len(outs),
+        out_shape=outs,
+        compiler_params=kernel_params(56),
+        name="halves",
+    )(bits, *items)
 
 
 ALL = ("pair", "core", "row", "half", "near")
@@ -950,43 +1029,66 @@
             current = choose((my_pair >> k) & 1, current, other, axis)
         return current
 
-    def scatter_groups(current, sums=None, split=None, join=None, waits=(), ends=()):
-        def pack(v):
-            v = v.astype(BF16)
-            if sums is None:
-                return v
-            rows = split(sums)
-            rows = jnp.broadcast_to(rows, v.shape[:-2] + rows.shape)
-            return jnp.concatenate([v, rows], axis=-2)
-
-        length = current.shape[-2]
+    def open_scatter(part):
+        half = part.shape[0] // 2
+        bit = (my_pair >> pair_bits[-1]) & 1
+        kept = lax.dynamic_slice_in_dim(part, bit * half, half, 0)
+        sent = lax.dynamic_slice_in_dim(part, (1 - bit) * half, half, 0)
+        return kept, sent.astype(BF16)
+
+    def scatter_groups(
+        parts, sums=None, split=None, join=None, waits=(), bound=(), opened=None
+    ):
+        def pack(items):
+            items = [item.astype(BF16) for item in items]
+            if sums is not None:
+                rows = split(sums)
+                items.append(jnp.broadcast_to(rows, items[0].shape[:-2] + rows.shape))
+            return jnp.concatenate(items, axis=-2)
+
+        if opened is not None:
+            parts = [opened[0]]
+        marks = np.cumsum([0] + [part.shape[-2] for part in parts])
 
         def unpack(v, total):
+            items = [
+                v[..., int(marks[k]) : int(marks[k + 1]), :].astype(F32)
+                for k in range(len(parts))
+            ]
             if total is None:
-                return v.astype(F32), None
+                return items, None
             first = v if v.ndim == 2 else v[0]
-            return v[..., :length, :].astype(F32), total + join(
-                first[length:], total.shape[0]
-            )
+            return items, total + join(first[int(marks[-1]) :], total.shape[0])
 
         for k in reversed(pair_bits):
-            half = current.shape[0] // 2
+            if opened is not None:
+                arrived = after(swap(opened[1], pair_perms[k]), *waits)
+                parts = [opened[0].astype(F32) + arrived.astype(F32)]
+                opened = None
+                continue
+            half = parts[0].shape[0] // 2
             bit = (my_pair >> k) & 1
-            kept = lax.dynamic_slice_in_dim(current, bit * half, half, 0)
-            sent = lax.dynamic_slice_in_dim(current, (1 - bit) * half, half, 0)
+            kept = [lax.dynamic_slice_in_dim(part, bit * half, half, 0) for part in parts]
+            sent = [lax.dynamic_slice_in_dim(part, (1 - bit) * half, half, 0) for part in parts]
             arrived = after(swap(pack(sent), pair_perms[k]), *waits)
             arrived, sums = unpack(arrived, sums)
-            current = kept + arrived
-        first = lax.dynamic_index_in_dim(current, my_half, 0, keepdims=False)
-        second = lax.dynamic_index_in_dim(current, 1 - my_half, 0, keepdims=False)
-        first = after(swap(pack(first), turned(cross_perms[0])), *ends)
-        second = after(swap(pack(second), turned(cross_perms[1])), *ends)
-        if sums is None:
-            return first.astype(F32) + second.astype(F32)
-        zero = jnp.zeros_like(sums)
-        first, sums_first = unpack(first, zero)
-        second, sums_second = unpack(second, zero)
-        return first + second, sums_first + sums_second
+            parts = [mine.astype(F32) + other for mine, other in zip(kept, arrived)]
+        first = [lax.dynamic_index_in_dim(part, my_half, 0, keepdims=False) for part in parts]
+        second = [
+            lax.dynamic_index_in_dim(part, 1 - my_half, 0, keepdims=False) for part in parts
+        ]
+        first, second, *bound = lax.optimization_barrier((pack(first), pack(second), *bound))
+        first = swap(first, turned(cross_perms[0]))
+        second = swap(second, turned(cross_perms[1]))
+
+        def finish(first, second):
+            zero = None if sums is None else jnp.zeros_like(sums)
+            first, sums_first = unpack(first, zero)
+            second, sums_second = unpack(second, zero)
+            total = [mine + other for mine, other in zip(first, second)]
+            return total, None if sums is None else sums_first + sums_second
+
+        return (first, second), finish, bound
 
     listed = lax.dynamic_index_in_dim(
         token_order.reshape(group_count, micro_count, team_size, piece_len),
@@ -1000,7 +1102,7 @@
         (1, micro_count, 1, piece_len),
     ).reshape(share_len)
     start = (group * team_size + member) * share_len
-    send_tokens, send_cotangent, send_map, take_map = run_deal(
+    token_pieces, back_pieces, send_map, take_map = run_deal(
         jnp.stack([start, group, target]).astype(jnp.int32),
         listed,
         seat_listed,
@@ -1009,19 +1111,15 @@
         group_len,
     )
 
-    def deal_pieces(rows):
-        return [
-            swap(rows[e * quota_len : (e + 1) * quota_len], deal_perms[e])
-            for e in range(group_count)
+    def deal_pieces(pieces):
+        return [swap(piece, perm) for piece, perm in zip(pieces, deal_perms)]
+
+    def undeal(pieces, *waits):
+        pieces = [
+            after(swap(piece, turned(perm)), *waits)
+            for piece, perm in zip(pieces, deal_perms)
         ]
-
-    def undeal(rows, *waits):
-        pieces = [
-            swap(rows[e * quota_len : (e + 1) * quota_len], turned(deal_perms[e]))
-            for e in range(group_count)
-        ]
-        pieces = [after(piece, *waits) for piece in pieces]
-        return run_pick(send_map, jnp.concatenate(pieces, axis=0), True)
+        return run_pick(send_map, pieces, True)
 
     def exchange(v, axis_name):
         return swap(v, team_perms[axis_name])
@@ -1051,7 +1149,7 @@
         ],
         axis=0,
     )
-    local_params = swap(after(local_params, send_tokens), cross_perms[0])
+    local_params = swap(after(local_params, *token_pieces), cross_perms[0])
     taps_value = local_params[:8]
     norm_gate_row = local_params[8:9]
     heads_got = local_params[16:24, :head_count]
@@ -1075,28 +1173,23 @@
     small_own = jnp.concatenate(
         [w_pair.T, w_step.T, jnp.zeros((small_pad, w_pair.shape[0]), BF16)], axis=0
     )
-    small_w = gather_groups(cross_groups(after(small_own, send_tokens)), 1)
-
-    pieces = deal_pieces(send_tokens)
-    dealt_tokens = run_pick(take_map, jnp.concatenate(pieces, axis=0), False)
-    full_rows = seat_view(
-        lax.all_gather(
-            jnp.concatenate(
-                [
-                    dealt_tokens,
-                    small_w[:pair_part],
-                    jnp.pad(tap_row, ((0, 15), (0, width_full - tap_count))),
-                ],
-                axis=0,
-            ),
-            TEAM,
-            axis=0,
-        )
-    )
+    small_w = gather_groups(cross_groups(after(small_own, *token_pieces)), 1)
+
+    pieces = deal_pieces(token_pieces)
+    extra = jnp.concatenate(
+        [
+            small_w[:pair_part],
+            jnp.pad(tap_row, ((0, 15), (0, width_full - tap_count))),
+        ],
+        axis=0,
+    )
+    dealt_tokens = run_pick(take_map, pieces, False, extra)
+    full_rows = seat_view(lax.all_gather(dealt_tokens, TEAM, axis=0))
     value_w = cross_groups(after(w_value, *pieces))
-    pieces = deal_pieces(after(send_cotangent, *value_w))
+    back_pieces = lax.optimization_barrier((*back_pieces, *value_w))[:group_count]
+    pieces = deal_pieces(back_pieces)
     value_w = gather_groups(value_w, 0)
-    dealt_back = run_pick(take_map, jnp.concatenate(pieces, axis=0), False)
+    dealt_back = run_pick(take_map, pieces, False)
     full_back = seat_view(lax.all_gather(dealt_back, TEAM, axis=0))
     later_w = cross_groups(after(jnp.stack([w_gate, w_out.T]), *pieces))
     full_rows, *later_w = lax.optimization_barrier((full_rows, *later_w))
@@ -1132,7 +1225,6 @@
         bounds, full_back, normed, gate_w, out_w, norm_gate_row, scanned, live_ids, micro_count, piece_len
     )
     partial_out = dot_nt(scaled.reshape(flat, width), out_w).astype(BF16)
-    partial_out, stats = lax.optimization_barrier((partial_out, stats))
     branch = lax.psum_scatter(partial_out, TEAM, scatter_dimension=0, tiled=True)
     stats = sum_over(stats, ("core", "near", "row"))
     low_gate, normed_out, grad_scanned, gate_sums = run_gate(
@@ -1147,45 +1239,59 @@
     flagged = jnp.concatenate(
         [bounds, jnp.full((1, bounds.shape[1]), my_core, jnp.int32)], axis=0
     )
-    totals = []
+    live_start = seat * piece_len
+    local_stats = lax.dynamic_slice_in_dim(
+        stats[0].reshape(micro_count, block_len), live_start, piece_len, 1
+    )
+    local_places = live_start + jnp.arange(piece_len, dtype=jnp.int32)
+    local_seg = jnp.sum(
+        (local_places[None, :, None] >= bounds[:, None, :]).astype(jnp.int32), axis=2
+    )
+    weight = jnp.where(
+        local_seg < live_ids, lax.rsqrt(local_stats / inner_full + EPS), 0.0
+    ).reshape(share_len, 1)
+    bits = jnp.stack([my_near, my_row]).astype(jnp.int32)
+    held = []
     all_sums = []
     earlier = None
+    crossed = ()
+    early = [item.reshape(group_count, -1, width) for item in (g_out, g_gate)]
     for micro in range(micro_count):
+        if micro == micro_count - 1 and micro:
+            crossed, finish_early, (low_value, low_small, bits, weight, *all_sums[0]) = scatter_groups(
+                early, waits=earlier, bound=(*earlier, bits, weight, *all_sums[0])
+            )
+            earlier = (low_value, low_small)
         low_value, low_small, keep, send, sums, sums_in = run_backward(
             flagged, grad_scanned, low_gate, kept, weights, consts, micro, piece_len, earlier, True
         )
         earlier = (low_value, low_small)
-        totals.append(keep.astype(F32) + exchange(send, "core").astype(F32))
-        all_sums.append((sums, sums_in))
-    low_value, low_small, branch, g_out, g_gate, *totals = lax.optimization_barrier(
-        (low_value, low_small, branch, g_out, g_gate, *totals)
-    )
-    early = [
-        lax.psum_scatter(item, ("pair", "half"), scatter_dimension=0, tiled=True)
-        for item in (g_out, g_gate)
-    ]
-    sides = {"near": (my_near, 1), "row": (my_row, 0)}
-
-    def halve(total, name, other):
-        bit, axis = sides[name]
-        axis = min(axis, total.ndim - 3)
-        keep = lax.dynamic_index_in_dim(total, bit, axis, keepdims=False)
-        send = lax.dynamic_index_in_dim(total, 1 - bit, axis, keepdims=False)
-        return keep + exchange(send.astype(BF16), name).astype(F32)
-
-    orders = [("near", "row") if micro % 2 == 0 else ("row", "near") for micro in range(micro_count)]
-    totals = [halve(total, order[0], order[1]) for total, order in zip(totals, orders)]
-    branch, *totals = lax.optimization_barrier((branch, *totals))
-    middle = totals
-    totals = [halve(total, order[1], order[0]) for total, order in zip(totals, orders)]
-    grad_ins = totals
-
-    g_out, g_gate = [
-        swap(after(item, *grad_ins), turned(cross_perms[0])).astype(F32) for item in early
-    ]
-    g_out = g_out.T
-    g_value = dot_tn(normed, low_value)
+        if crossed:
+            send, *crossed = lax.optimization_barrier((send, *crossed))
+        held += [keep, exchange(send, "core")]
+        all_sums.append([sums, sums_in])
+    first_axes = tuple((1 - micro % 2, micro % 2) for micro in range(micro_count))
+    next_axes = tuple((0, 1 - micro % 2) for micro in range(micro_count))
+
+    def cross_sides(held, axes):
+        names = ("near", "row")
+        return [
+            item if k % 2 == 0 else exchange(item, names[axes[k // 2][1]])
+            for k, item in enumerate(held)
+        ]
+
+    held = run_halves(first_axes, bits, *held)
+    low_value, low_small, all_sums, *held = lax.optimization_barrier(
+        (low_value, low_small, all_sums, *held)
+    )
+    held = cross_sides(held, first_axes)
+    g_value = dot_tn(normed, low_value).astype(BF16)
+    opened = open_scatter(g_value.reshape(group_count, -1, width))
     g_small = dot_tn(low_small, normed)
+    opened, g_small, held = lax.optimization_barrier((opened, g_small, held))
+    held = run_halves(next_axes, bits, *held)
+    branch, held = lax.optimization_barrier((branch, held))
+    grad_ins = cross_sides(held, next_axes)
     sums = reduce(jnp.add, [item[0] for item in all_sums])
     sums_in = reduce(jnp.add, [item[1] for item in all_sums])[0:1]
     pair_sums = sums[8:13, :pair_width].reshape(1, -1)
@@ -1203,18 +1309,43 @@
         return v[:count].astype(F32) + v[count : 2 * count].astype(F32)
 
     g_pair = g_small[:pair_width].reshape(sizes[2], sizes[4], 2, pair_part, width_full)
-    for name, bit, axis in (("core", my_core, 2), ("near", my_near, 1), ("row", my_row, 0)):
+
+    def pair_stage(g_pair, team_rows, name, bit, axis, *waits):
         keep = lax.dynamic_index_in_dim(g_pair, bit, axis, keepdims=False)
         send = lax.dynamic_index_in_dim(g_pair, 1 - bit, axis, keepdims=False)
         count = send.size // width_full
         packed = jnp.concatenate(
             [send.astype(BF16).reshape(count, width_full), split_rows(team_rows)], axis=0
         )
-        packed = exchange(packed, name)
-        if name != "core":
-            packed = after(packed, *middle)
-        g_pair = keep + packed[:count].reshape(keep.shape).astype(F32)
-        team_rows = team_rows + join_rows(packed[count:], team_rows.shape[0])
+        packed = after(exchange(packed, name), *waits)
+        return (
+            keep + packed[:count].reshape(keep.shape).astype(F32),
+            team_rows + join_rows(packed[count:], team_rows.shape[0]),
+        )
+
+    g_pair, team_rows = pair_stage(g_pair, team_rows, "core", my_core, 2, *held)
+    g_pair, team_rows = pair_stage(g_pair, team_rows, "near", my_near, 1)
+    g_pair, team_rows, grad_ins, crossed = lax.optimization_barrier(
+        (g_pair, team_rows, grad_ins, crossed)
+    )
+    send_back = run_close(
+        partial(close_back_kernel, micro_count),
+        group_count,
+        take_map,
+        dealt_tokens,
+        dealt_back,
+        norm_in[None, :],
+        *grad_ins,
+    )
+    crossed = lax.optimization_barrier((crossed, send_back))[0]
+    (g_out, g_gate), _ = finish_early(*crossed)
+    g_out = g_out.T
+    branch, send_back = lax.optimization_barrier((branch, send_back))
+    send_out = run_close(
+        close_out_kernel, group_count, take_map, dealt_tokens, branch, weight
+    )
+    out_pieces = [swap(piece, turned(perm)) for piece, perm in zip(send_out, deal_perms)]
+    g_pair, team_rows = pair_stage(g_pair, team_rows, "row", my_row, 0, *send_back)
     g_small = jnp.concatenate(
         [
             g_pair,
@@ -1231,14 +1362,10 @@
     late = jnp.swapaxes(g_small.reshape(small_rows, group_count, -1), 0, 1)
     if value_rows != width:
         late = jnp.pad(late, ((0, 0), (0, 0), (0, width - value_rows)))
-    send_back = run_close(
-        close_back_kernel, take_map, dealt_tokens, dealt_back, norm_in[None, :], *grad_ins
-    )
-    late, sums = scatter_groups(
-        late, sums, split_rows, join_rows, grad_ins, [send_back]
-    )
-    g_value = g_value.reshape(group_count, -1, width)
-    g_value = scatter_groups(g_value, waits=middle, ends=[send_back])
+    crossed, finish, _ = scatter_groups([late], sums, split_rows, join_rows, waits=send_back)
+    (late,), sums = finish(*crossed)
+    crossed, finish, _ = scatter_groups([g_value], waits=send_back, opened=opened)
+    (g_value,), _ = finish(*crossed)
     g_small = late[:, :value_rows]
     g_pair = g_small[:pair_part].T
     g_step = g_small[pair_part : pair_part + head_count].T
@@ -1250,18 +1377,7 @@
     g_norm_in = in_sums.reshape(-1) / norm_in.astype(F32)
     g_skip = jnp.sum(sums[6].reshape(head_count, head_width), axis=1)
 
-    live_start = seat * piece_len
-    local_stats = lax.dynamic_slice_in_dim(
-        stats[0].reshape(micro_count, block_len), live_start, piece_len, 1
-    )
-    local_places = live_start + jnp.arange(piece_len, dtype=jnp.int32)
-    local_seg = jnp.sum(
-        (local_places[None, :, None] >= bounds[:, None, :]).astype(jnp.int32), axis=2
-    )
-    weight = jnp.where(
-        local_seg < live_ids, lax.rsqrt(local_stats / inner_full + EPS), 0.0
-    ).reshape(share_len, 1)
-    block_out = undeal(run_close(close_out_kernel, take_map, dealt_tokens, branch, weight), send_back)
+    block_out = run_pick(send_map, out_pieces, True)
     grad_tokens = undeal(send_back)
     return (
         block_out,

time: 431 us -> 403 us (0.935)
  waiting for transfers between devices: 113 us -> 88.8 us
  other arithmetic: 37.5 us -> 21.3 us
  starting transfers between devices: 72.6 us -> 86.2 us
    ppermute x46 -> x47, waiting for transfers between devices: 113 us -> 87.8 us  [swap(): return lax.ppermute(v, ALL, perm)]
    ppermute x46 -> x47, starting transfers between devices: 72.2 us -> 86 us  [swap(): return lax.ppermute(v, ALL, perm)]
    add x15 -> x11, other arithmetic: 16.2 us -> 4.02 us  [the longest x3 1.83 us: pair_stage(): keep + packed[:count].reshape(keep.shape).astype(F32)]
    concatenate x10 -> x9, other arithmetic: 7.98 us -> 1.32 us  [the longest x5 1.25 us: pack(): return jnp.concatenate(items, axis=-2)]
    unnamed x79 -> x107, local copies, waits for them, and re-layouts: 5.03 us -> 11.4 us
    convert_element_type x10 -> x7, local copies, waits for them, and re-layouts: 6.33 us -> 1.13 us  [the longest x4 1.04 us: pack(): items = [item.astype(BF16) for item in items]]
    pallas_call x6 -> x8, Pallas kernels: 16.6 us -> 19 us  [the longest x2 9.68 us: run_halves(): pl.pallas_call(partial(halves_kernel, axes), in_specs=[smem_spec()] + [vm...]
  transfers between devices with their start and end apart: 51 -> 50, of which waited for: 23 -> 22; matrix products, arithmetic and copies ran while one was open for 20% -> 16% of each run, Pallas kernels for 23% -> 26%
where the time goes in v3:
time: 403 us; the launch traced here: 396 us
  Pallas kernels  119 us (30%)
  waiting for transfers between devices  88.8 us (22%)
  starting transfers between devices  86.2 us (21%)
  local copies, waits for them, and re-layouts  37.9 us (9%)
  matrix products  27.2 us (7%)
  other arithmetic  21.3 us (5%)
  between operations  15.3 us (4%)
    ppermute x47, waiting for transfers between devices, swap(): return lax.ppermute(v, ALL, perm)  87.8 us
    ppermute x47, starting transfers between devices, swap(): return lax.ppermute(v, ALL, perm)  86 us
    pallas_call x2, Pallas kernels, run_backward(): pl.pallas_call(partial(backward_kernel, width // LANES, micro, earlier is...  47.5 us
    pallas_call x1, Pallas kernels, run_forward(): pl.pallas_call(partial(forward_kernel, width // LANES), grid=(micro_count...  26.4 us
    dot_general x4, matrix products, dot_tn(): lax.dot_general(a, b, (((0,), (0,)), ((), ())), preferred_element_type=F32)  20.4 us
    pallas_call x1, Pallas kernels, run_back(): pl.pallas_call(partial(back_kernel, live_ids), grid=(micro_count, blocks)...  14.4 us
    unnamed x107, local copies, waits for them, and re-layouts  11.4 us
    pallas_call x1, Pallas kernels, run_gate(): pl.pallas_call(partial(gate_kernel, live_ids, inner_full), grid=(micro_co...  10.1 us
  transfers between devices with their start and end apart: 50, of which 22 were waited for; matrix products, arithmetic and copies ran while one was open for 16% of the time, Pallas kernels for 26%

profile of v3, /device:TPU:1, one launch (start us, length us, event | category | flops | bytes accessed | tf_op | source)
XLA Modules:
  0.0 395.7 jit_solution(11485589686167836798)
XLA Ops:
  12.5 1.5 deal.1
  14.1 5.6 %collective-permute-start.4 = (bf16[48,384]{1,0:T(8,128)(2,1)S(1)}, bf16[48,384]{1,0:T(8,128)(2,1)S(1)}, u32[]{:S(2)}, u32[]{:S(2)}) collective-permute-start(bf16[48,384]{1,0:T(8,128)(2,1)S(1)} %maximum_maximum_fusion.1), channel_id=1, source_target_pairs={{0,0},{1,1},{2,8},{3,9},{4,4},{5,5},{6,12},{7,13},{8,2},{9,3},{10,... | collective-permute-start | bytes 110600 | tf_op jit(solution)/shard_map/ppermute | solution.py:941
  19.7 1.9 collective-permute-start
  21.7 3.7 collective-permute-start.2
  26.8 1.9 collective-permute-start.7
  28.7 14.5 %collective-permute-done.7 = f32[40,384]{1,0:T(8,128)S(1)} collective-permute-done((f32[40,384]{1,0:T(8,128)S(1)}, f32[40,384]{1,0:T(8,128)S(1)}, u32[]{:S(2)}, u32[]{:S(2)}) %collective-permute-start.7) | collective-permute-done | bytes 61472 | tf_op jit(solution)/shard_map/ppermute | solution.py:941
  43.2 1.7 collective-permute-start.6
  44.9 1.6 collective-permute-done.6
  46.7 1.4 pick.4.dealt_ref
  48.2 2.7 collective-permute-start.8
  50.9 10.2 %collective-permute-done.9 = bf16[384,384]{1,0:T(8,128)(2,1)S(1)} collective-permute-done((bf16[384,384]{1,0:T(8,128)(2,1)S(1)}, bf16[384,384]{1,0:T(8,128)(2,1)S(1)}, u32[]{:S(2)}, u32[]{:S(2)}) %collective-permute-start.9) | collective-permute-done | bytes 294944 | tf_op jit(solution)/shard_map/ppermute | solution.py:941
  62.3 1.9 collective-permute-start.10
  64.3 3.9 collective-permute-start.12
  68.9 4.6 %collective-permute-done.10.refs_0_ = bf16[64,1536]{1,0:T(8,128)(2,1)S(1)} collective-permute-done((bf16[64,1536]{1,0:T(8,128)(2,1)S(1)}, bf16[64,1536]{1,0:T(8,128)(2,1)S(1)}, u32[]{:S(2)}, u32[]{:S(2)}) %collective-permute-start.10) | collective-permute-done | bytes 196640 | tf_op jit(solution)/shard_map/ppermute | solution.py:941
  73.6 8.6 %collective-permute-done.12.refs_2_ = bf16[64,1536]{1,0:T(8,128)(2,1)S(1)} collective-permute-done((bf16[64,1536]{1,0:T(8,128)(2,1)S(1)}, bf16[64,1536]{1,0:T(8,128)(2,1)S(1)}, u32[]{:S(2)}, u32[]{:S(2)}) %collective-permute-start.12) | collective-permute-done | bytes 196640 | tf_op jit(solution)/shard_map/ppermute | solution.py:941
  84.4 1.3 broadcast_in_dim.49.norm_in_ref
  87.1 3.3 collective-permute-start.15
  90.4 4.9 %collective-permute-start.14 = (bf16[2,384,384]{2,1,0:T(8,128)(2,1)S(1)}, bf16[2,384,384]{2,1,0:T(8,128)(2,1)S(1)}, u32[]{:S(2)}, u32[]{:S(2)}) collective-permute-start(bf16[2,384,384]{2,1,0:T(8,128)(2,1)S(1)} %pad_maximum_fusion.1), channel_id=1, source_target_pairs={{0,0},{1,1},{2,8},{3,9},{4,4},{5,5},{6,12},{7,13},{8,2},{9,3},{10,... | collective-permute-start | bytes 1769480 | tf_op jit(solution)/shard_map/ppermute | solution.py:941
  96.8 1.3 slice.294.norm_gate_ref
  98.1 1.3 slice.285.taps_value_ref
  100.0 1.5 maximum_select_fusion.1.w_value_ref
  101.5 14.3 %collective-permute-done.14 = bf16[2,384,384]{2,1,0:T(8,128)(2,1)S(1)} collective-permute-done((bf16[2,384,384]{2,1,0:T(8,128)(2,1)S(1)}, bf16[2,384,384]{2,1,0:T(8,128)(2,1)S(1)}, u32[]{:S(2)}, u32[]{:S(2)}) %collective-permute-start.14) | collective-permute-done | bytes 589856 | tf_op jit(solution)/shard_map/ppermute | solution.py:941
  121.4 26.4 %forward.1 = (bf16[2048,1536]{1,0:T(8,128)(2,1)}, bf16[2048,384]{1,0:T(8,128)(2,1)}, f32[2048,384]{1,0:T(8,128)}, bf16[2048,256]{1,0:T(8,128)(2,1)}, f32[2048,25...) custom-call(s32[2,4]{1,0:T(2,128)} %reduce_window_sum.11.bounds_ref, ...), custom_call_target="tpu_custom_call" | custom-call | flops 14495514624 | bytes 31457280 | tf_op jit(solution)/shard_map/forward/pallas_call | solution.py:587
  148.5 1.7 slice_bitcast_fusion
  151.1 14.4 %back.1 = (f32[2048,384]{1,0:T(8,128)}, bf16[2,2,2,256,384]{4,3,2,1,0:T(8,128)(2,1)}, bf16[2048,384]{1,0:T(8,128)(2,1)}, f32[8,2048]{1,0:T(8,128)}) custom-call(s32[2,4]{1,0:T(2,128)} %reduce_window_sum.11.bounds_ref, bf16[2,2,2,256,1536]{4,3,2,1,0:T(8,128)(2,1)} %bitcast.127, bf16[2048,1536]{1,0:T(8,128)(2,1)} %get-tuple-element.160.normed_ref, ...), custom_call_target="tpu_custom_call" | custom-call | flops 4831838208 | bytes 23592960 | tf_op jit(solution)/shard_map/back/pallas_call | solution.py:622
  165.6 6.8 %convolution_convert_fusion = bf16[2048,1536]{1,0:T(8,128)(2,1)} fusion(bf16[2048,384]{1,0:T(8,128)(2,1)} %bitcast.157, bf16[2,1536,384]{2,1,0:T(8,128)(2,1)S(1)} %maximum_select_fusion), kind=kOutput, calls=%fused_computation | convolution fusion | flops 2419064832 | bytes 9043968 | tf_op jit(solution)/shard_map/dot_general | solution.py:27
  174.5 4.4 %collective-permute-start.19 = (f32[8,2048]{1,0:T(8,128)S(1)}, f32[8,2048]{1,0:T(8,128)S(1)}, u32[]{:S(2)}, u32[]{:S(2)}) collective-permute-start(f32[8,2048]{1,0:T(8,128)S(1)} %add.243), channel_id=1, source_target_pairs={{0,1},{1,0},{2,3},{3,2},{4,5},{5,4},{6,7},{7,6},{8,9},{9,8},{10,11... | collective-permute-start | bytes 196616 | tf_op jit(solution)/shard_map/ppermute | solution.py:941
  178.9 2.2 collective-permute-done.19
  181.1 1.4 collective-permute-start.20
  185.0 10.1 %gate.1 = (bf16[2048,384]{1,0:T(8,128)(2,1)}, bf16[2,2,2,256,384]{4,3,2,1,0:T(8,128)(2,1)}, bf16[2048,384]{1,0:T(8,128)(2,1)}, f32[8,384]{1,0:T(8,128)}) custom-call(s32[2,4]{1,0:T(2,128)} %reduce_window_sum.11.bounds_ref, f32[8,2048]{1,0:T(8,128)} %add.245.stats_ref, bf16[2048,384]{1,0:T(8,128)(2,1)} %get-tuple-element.166.grad_normed_ref, ...), custom_call_target="tpu_custom_call" | custom-call | flops 15728640 | bytes 15728640 | tf_op jit(solution)/shard_map/gate/pallas_call | solution.py:652
  195.1 5.0 %convolution_convert_fusion.2 = bf16[1536,384]{1,0:T(8,128)(2,1)S(1)} fusion(bf16[2048,1536]{1,0:T(8,128)(2,1)S(1)} %bitcast.124, bf16[2048,384]{1,0:T(8,128)(2,1)} %get-tuple-element.169.low_gate_ref), kind=kOutput, calls=%fused_computation.2 | convolution fusion | flops 2416508928 | bytes 9043968 | tf_op jit(solution)/shard_map/dot_general | solution.py:31
  200.1 6.3 %convolution_convert_fusion.3 = bf16[1536,384]{1,0:T(8,128)(2,1)S(1)} fusion(bf16[2048,1536]{1,0:T(8,128)(2,1)} %all-gather.5.cloned.1.call-done, bf16[2048,384]{1,0:T(8,128)(2,1)S(1)} %bitcast.156), kind=kOutput, calls=%fused_computation.3 | convolution fusion | flops 2416508928 | bytes 9043968 | tf_op jit(solution)/shard_map/dot_general | solution.py:31
  211.3 23.8 %backward.2 = (bf16[2048,384]{1,0:T(8,128)(2,1)}, bf16[2048,384]{1,0:T(8,128)(2,1)}, bf16[2,2,128,1536]{3,2,1,0:T(8,128)(2,1)}, bf16[2,2,128,1536]{3,2,1,0:T(8,1...) custom-call(s32[3,4]{1,0:T(4,128)} %concatenate.133.bounds_ref, bf16[2048,384]{1,0:T(8,128)(2,1)} %get-tuple-element.173.grad_scanned_ref, ...), custom_call_target="tpu_custom_call" | custom-call | flops 8455716864 | bytes 15728640 | tf_op jit(solution)/shard_map/backward/pallas_call | solution.py:721
  235.1 2.4 collective-permute-start.22
  238.1 4.7 %collective-permute-start.23 = (bf16[768,384]{0,1:T(8,128)(2,1)S(1)}, bf16[768,384]{0,1:T(8,128)(2,1)S(1)}, u32[]{:S(2)}, u32[]{:S(2)}) collective-permute-start(bf16[768,384]{0,1:T(8,128)(2,1)S(1)} %pad_maximum_fusion.2), channel_id=1, source_target_pairs={{0,0},{1,1},{8,2},{9,3},{4,4},{5,5},{12,6},{13,7},{2,8},{3,9},{10,... | collective-permute-start | bytes 1769480 | tf_op jit(solution)/shard_map/ppermute | solution.py:941
  242.9 23.7 %backward.3 = (bf16[2048,384]{1,0:T(8,128)(2,1)}, bf16[2048,384]{1,0:T(8,128)(2,1)}, bf16[2,2,128,1536]{3,2,1,0:T(8,128)(2,1)}, bf16[2,2,128,1536]{3,2,1,0:T(8,1...) custom-call(s32[3,4]{1,0:T(4,128)} %concatenate.133.bounds_ref, ...), custom_call_target="tpu_custom_call", output_to_operand_aliasing={{0}: (22, {}), {1}: (23, {})} | custom-call | flops 8455716864 | bytes 15728640 | tf_op jit(solution)/shard_map/backward/pallas_call | solution.py:721
  268.2 2.6 collective-permute-start.25
  270.8 3.2 collective-permute-done.25.refs_3_
  275.3 5.7 %halves.2 = (f32[2,128,1536]{2,1,0:T(8,128)}, bf16[2,128,1536]{2,1,0:T(8,128)(2,1)}, f32[2,128,1536]{2,1,0:T(8,128)}, bf16[2,128,1536]{2,1,0:T(8,128)(2,1)}) custom-call(s32[2]{0:T(128)} %pad_add_fusion.1.bits_ref, bf16[2,2,128,1536]{3,2,1,0:T(8,128)(2,1)} %get-tuple-element.194.refs_0_, bf16[2,2,128,1536]{3,2,1,0:T(8,128)(2,1)} %collective-permute-done.22.refs_1_, ...), custom_call_target="tpu_custom_call" | custom-call | tf_op jit(solution)/shard_map/halves/pallas_call | solution.py:915
  281.2 2.4 collective-permute-start.27
  284.5 6.4 %convolution_convert_fusion.1 = bf16[1536,384]{1,0:T(8,128)(2,1)S(1)} fusion(bf16[2048,1536]{1,0:T(8,128)(2,1)} %get-tuple-element.160.normed_ref, bf16[2048,384]{1,0:T(8,128)(2,1)S(1)} %copy-done.44), kind=kOutput, calls=%fused_computation.1 | convolution fusion | flops 2416508928 | bytes 9043968 | tf_op jit(solution)/shard_map/dot_general | solution.py:31
  292.8 2.6 fusion.44
  295.4 4.6 %collective-permute-done.26.refs_1_ = bf16[2,128,1536]{2,1,0:T(8,128)(2,1)S(1)} collective-permute-done((bf16[2,128,1536]{2,1,0:T(8,128)(2,1)}, bf16[2,128,1536]{2,1,0:T(8,128)(2,1)S(1)}, u32[]{:S(2)}, u32[]{:S(2)}) %collective-permute-start.26) | collective-permute-done | bytes 786464 | tf_op jit(solution)/shard_map/ppermute | solution.py:941
  300.0 1.4 collective-permute-done.27.refs_3_
  302.6 4.0 %halves.3 = (f32[128,1536]{1,0:T(8,128)}, bf16[128,1536]{1,0:T(8,128)(2,1)}, f32[128,1536]{1,0:T(8,128)}, bf16[128,1536]{1,0:T(8,128)(2,1)}) custom-call(s32[2]{0:T(128)} %pad_add_fusion.1.bits_ref, f32[2,128,1536]{2,1,0:T(8,128)} %get-tuple-element.211.refs_0_, bf16[2,128,1536]{2,1,0:T(8,128)(2,1)} %copy-done.11, ...), custom_call_target="tpu_custom_call" | custom-call | tf_op jit(solution)/shard_map/halves/pallas_call | solution.py:915
  309.5 1.5 collective-permute-start.29
  314.0 1.5 collective-permute-start.30
  319.4 4.2 %collective-permute-done.30.refs_1_ = bf16[128,1536]{1,0:T(8,128)(2,1)S(1)} collective-permute-done((bf16[128,1536]{1,0:T(8,128)(2,1)}, bf16[128,1536]{1,0:T(8,128)(2,1)S(1)}, u32[]{:S(2)}, u32[]{:S(2)}) %collective-permute-start.30) | collective-permute-done | bytes 393248 | tf_op jit(solution)/shard_map/ppermute | solution.py:941
  324.9 2.5 close.2
  327.5 2.6 collective-permute-start.40
  330.1 5.2 %collective-permute-start.36 = (bf16[64,1536]{1,0:T(8,128)(2,1)S(1)}, bf16[64,1536]{1,0:T(8,128)(2,1)S(1)}, u32[]{:S(2)}, u32[]{:S(2)}) collective-permute-start(bf16[64,1536]{1,0:T(8,128)(2,1)S(1)} %get-tuple-element.246), channel_id=1, source_target_pairs={{0,0},{1,1},{8,2},{9,3},{4,4},{5,5},{12,6},{13,7},{2,8},{3,9},{10,... | collective-permute-start | bytes 589832 | tf_op jit(solution)/shard_map/ppermute | solution.py:941
  337.8 1.7 close.3
  339.7 5.1 %collective-permute-start.32 = (bf16[64,1536]{1,0:T(8,128)(2,1)S(1)}, bf16[64,1536]{1,0:T(8,128)(2,1)S(1)}, u32[]{:S(2)}, u32[]{:S(2)}) collective-permute-start(bf16[64,1536]{1,0:T(8,128)(2,1)S(1)} %get-tuple-element.242), channel_id=1, source_target_pairs={{0,0},{1,1},{8,2},{9,3},{4,4},{5,5},{12,6},{13,7},{2,8},{3,9},{10,... | collective-permute-start | bytes 589832 | tf_op jit(solution)/shard_map/ppermute | solution.py:941
  345.6 1.7 maximum_maximum_fusion
  347.3 1.8 reshape.159
  350.3 1.6 collective-permute-start.34
  351.9 2.3 collective-permute-done.38.refs_2_
  355.5 2.2 copy.91
  358.7 1.3 pick.7
  360.0 1.9 collective-permute-done.32.refs_0_
  361.9 6.3 %collective-permute-start.45 = (bf16[384,384]{1,0:T(8,128)(2,1)S(1)}, bf16[384,384]{1,0:T(8,128)(2,1)S(1)}, u32[]{:S(2)}, u32[]{:S(2)}) collective-permute-start(bf16[384,384]{1,0:T(8,128)(2,1)S(1)} %copy-done.22), channel_id=1, source_target_pairs={{0,0},{1,1},{8,2},{9,3},{4,4},{5,5},{12,6},{13,7},{2,8},{3,9},{10,... | collective-permute-start | bytes 884744 | tf_op jit(solution)/shard_map/ppermute | solution.py:941
  368.9 1.3 pick.6
  370.3 3.6 collective-permute-start.42
  375.9 7.6 %collective-permute-done.42 = bf16[80,384]{1,0:T(8,128)(2,1)S(1)} collective-permute-done((bf16[80,384]{1,0:T(8,128)(2,1)S(1)}, bf16[80,384]{1,0:T(8,128)(2,1)S(1)}, u32[]{:S(2)}, u32[]{:S(2)}) %collective-permute-start.42) | collective-permute-done | bytes 61472 | tf_op jit(solution)/shard_map/ppermute | solution.py:941
  (300 shorter events, 64.7 us)
Async XLA Ops:
  7.2 18.3 %copy-start.38 = (f32[32]{0:T(128)S(1)}, f32[32]{0:T(128)}, u32[]{:S(2)}) copy-start(f32[32]{0:T(128)} %param.34) | copy-start | bytes 388
  7.2 18.2 %copy-start.33 = (f32[4,32]{1,0:T(4,128)S(1)}, f32[4,32]{1,0:T(4,128)}, u32[]{:S(2)}) copy-start(f32[4,32]{1,0:T(4,128)} %param.33) | copy-start | bytes 1540
  7.2 18.3 %copy-start.39 = (f32[6]{0:T(128)S(1)}, f32[6]{0:T(128)}, u32[]{:S(2)}) copy-start(f32[6]{0:T(128)} %param.37) | copy-start | bytes 76
  7.2 18.3 %copy-start.40 = (f32[6]{0:T(128)S(1)}, f32[6]{0:T(128)}, u32[]{:S(2)}) copy-start(f32[6]{0:T(128)} %param.36) | copy-start | bytes 76
  7.2 18.3 %copy-start.41 = (f32[6]{0:T(128)S(1)}, f32[6]{0:T(128)}, u32[]{:S(2)}) copy-start(f32[6]{0:T(128)} %param.35) | copy-start | bytes 76
  7.2 18.3 %copy-start.36 = (s32[2,4]{1,0:T(2,128)S(1)}, s32[2,4]{1,0:T(2,128)}, u32[]{:S(2)}) copy-start(s32[2,4]{1,0:T(2,128)} %param.24) | copy-start | bytes 100
  7.2 18.3 %copy-start.35 = (f32[384]{0:T(512)S(1)}, f32[384]{0:T(512)}, u32[]{:S(2)}) copy-start(f32[384]{0:T(512)} %param.32) | copy-start | bytes 4612
  7.3 18.4 %copy-start.32 = (f32[4,384]{1,0:T(4,128)S(1)}, f32[4,384]{1,0:T(4,128)}, u32[]{:S(2)}) copy-start(f32[4,384]{1,0:T(4,128)} %param.31) | copy-start | bytes 18436
  7.3 18.4 %copy-start.34 = (f32[384]{0:T(512)S(1)}, f32[384]{0:T(512)}, u32[]{:S(2)}) copy-start(f32[384]{0:T(512)} %param.38) | copy-start | bytes 4612
  7.3 108.5 %all-gather.7.cloned.1.call-start = ((), (), s32[]{:S(2)}) async-start(), calls=%async_computation.3 | async-start | bytes 8404992 | tf_op jit(solution)/shard_map/all_gather | solution.py:1187
  14.0 11.7 %collective-permute-start.5 = (bf16[48,384]{1,0:T(8,128)(2,1)S(1)}, bf16[48,384]{1,0:T(8,128)(2,1)S(1)}, u32[]{:S(2)}, u32[]{:S(2)}) collective-permute-start(bf16[48,384]{1,0:T(8,128)(2,1)S(1)} %maximum_maximum_fusion.1), channel_id=1, source_target_pairs={{0,2},{1,3},{2,10},{3,11},{4,6},{5,7},{6,14},{7,15},{8,0},{9,1},{1... | collective-permute-start | bytes 110600 | tf_op jit(solution)/shard_map/ppermute | solution.py:941
  14.1 12.6 %collective-permute-start.4 = (bf16[48,384]{1,0:T(8,128)(2,1)S(1)}, bf16[48,384]{1,0:T(8,128)(2,1)S(1)}, u32[]{:S(2)}, u32[]{:S(2)}) collective-permute-start(bf16[48,384]{1,0:T(8,128)(2,1)S(1)} %maximum_maximum_fusion.1), channel_id=1, source_target_pairs={{0,0},{1,1},{2,8},{3,9},{4,4},{5,5},{6,12},{7,13},{8,2},{9,3},{10,... | collective-permute-start | bytes 110600 | tf_op jit(solution)/shard_map/ppermute | solution.py:941
  19.7 27.0 %collective-permute-start = (bf16[64,1536]{1,0:T(8,128)(2,1)S(1)}, bf16[64,1536]{1,0:T(8,128)(2,1)S(1)}, u32[]{:S(2)}, u32[]{:S(2)}) collective-permute-start(bf16[64,1536]{1,0:T(8,128)(2,1)S(1)} %get-tuple-element.143), channel_id=1, source_target_pairs={{0,0},{1,1},{2,8},{3,9},{4,4},{5,5},{6,12},{7,13},{8,2},{9,3},{10,... | collective-permute-start | bytes 589832 | tf_op jit(solution)/shard_map/ppermute | solution.py:941
  21.6 25.1 %collective-permute-start.1 = (bf16[64,1536]{1,0:T(8,128)(2,1)S(1)}, bf16[64,1536]{1,0:T(8,128)(2,1)S(1)}, u32[]{:S(2)}, u32[]{:S(2)}) collective-permute-start(bf16[64,1536]{1,0:T(8,128)(2,1)S(1)} %get-tuple-element.144), channel_id=1, source_target_pairs={{0,2},{1,3},{2,10},{3,11},{4,6},{5,7},{6,14},{7,15},{8,0},{9,1},{1... | collective-permute-start | bytes 589832 | tf_op jit(solution)/shard_map/ppermute | solution.py:941
  21.7 25.0 %collective-permute-start.2 = (bf16[64,1536]{1,0:T(8,128)(2,1)S(1)}, bf16[64,1536]{1,0:T(8,128)(2,1)S(1)}, u32[]{:S(2)}, u32[]{:S(2)}) collective-permute-start(bf16[64,1536]{1,0:T(8,128)(2,1)S(1)} %get-tuple-element.145), channel_id=1, source_target_pairs={{0,16},{1,17},{2,24},{3,25},{4,20},{5,21},{6,28},{7,29},{8,18},{9,... | collective-permute-start | bytes 589832 | tf_op jit(solution)/shard_map/ppermute | solution.py:941
  25.7 21.0 %collective-permute-start.3 = (bf16[64,1536]{1,0:T(8,128)(2,1)S(1)}, bf16[64,1536]{1,0:T(8,128)(2,1)S(1)}, u32[]{:S(2)}, u32[]{:S(2)}) collective-permute-start(bf16[64,1536]{1,0:T(8,128)(2,1)S(1)} %get-tuple-element.146), channel_id=1, source_target_pairs={{0,18},{1,19},{2,26},{3,27},{4,22},{5,23},{6,30},{7,31},{8,16},{9,... | collective-permute-start | bytes 589832 | tf_op jit(solution)/shard_map/ppermute | solution.py:941
  26.8 16.4 %collective-permute-start.7 = (f32[40,384]{1,0:T(8,128)S(1)}, f32[40,384]{1,0:T(8,128)S(1)}, u32[]{:S(2)}, u32[]{:S(2)}) collective-permute-start(f32[40,384]{1,0:T(8,128)S(1)} %concatenate.120), channel_id=1, source_target_pairs={{0,0},{1,1},{2,8},{3,9},{4,4},{5,5},{6,12},{7,13},{8,2},{9,3},{10,... | collective-permute-start | bytes 184328 | tf_op jit(solution)/shard_map/ppermute | solution.py:941
  43.2 3.4 collective-permute-start.6
  46.6 53.4 %copy-start.18 = (bf16[48,1536]{1,0:T(8,128)(2,1)}, bf16[48,1536]{1,0:T(8,128)(2,1)S(1)}, u32[]{:S(2)}) copy-start(bf16[48,1536]{1,0:T(8,128)(2,1)S(1)} %maximum_select_fusion.4) | copy-start | bytes 442372
  48.1 35.4 %copy-start.19 = (bf16[384,384]{1,0:T(8,128)(2,1)S(1)}, bf16[384,384]{1,0:T(8,128)(2,1)}, u32[]{:S(2)}) copy-start(bf16[384,384]{1,0:T(8,128)(2,1)} %param.39) | copy-start | bytes 884740
  48.1 103.0 %all-gather.5.cloned.1.call-start = ((), (), s32[]{:S(2)}) async-start(), calls=%async_computation.2 | async-start | bytes 7077888 | tf_op jit(solution)/shard_map/all_gather | solution.py:1193
  48.1 13.0 %collective-permute-start.9 = (bf16[384,384]{1,0:T(8,128)(2,1)S(1)}, bf16[384,384]{1,0:T(8,128)(2,1)S(1)}, u32[]{:S(2)}, u32[]{:S(2)}) collective-permute-start(bf16[384,384]{1,0:T(8,128)(2,1)S(1)} %copy-done.43), channel_id=1, source_target_pairs={{0,2},{1,3},{2,10},{3,11},{4,6},{5,7},{6,14},{7,15},{8,0},{9,1},{1... | collective-permute-start | bytes 884744 | tf_op jit(solution)/shard_map/ppermute | solution.py:941
  48.2 14.1 %collective-permute-start.8 = (bf16[384,384]{1,0:T(8,128)(2,1)S(1)}, bf16[384,384]{1,0:T(8,128)(2,1)S(1)}, u32[]{:S(2)}, u32[]{:S(2)}) collective-permute-start(bf16[384,384]{1,0:T(8,128)(2,1)S(1)} %copy-done.43), channel_id=1, source_target_pairs={{0,0},{1,1},{2,8},{3,9},{4,4},{5,5},{6,12},{7,13},{8,2},{9,3},{10,... | collective-permute-start | bytes 884744 | tf_op jit(solution)/shard_map/ppermute | solution.py:941
  62.3 11.3 %collective-permute-start.10 = (bf16[64,1536]{1,0:T(8,128)(2,1)S(1)}, bf16[64,1536]{1,0:T(8,128)(2,1)S(1)}, u32[]{:S(2)}, u32[]{:S(2)}) collective-permute-start(bf16[64,1536]{1,0:T(8,128)(2,1)S(1)} %get-tuple-element.154), channel_id=1, source_target_pairs={{0,0},{1,1},{2,8},{3,9},{4,4},{5,5},{6,12},{7,13},{8,2},{9,3},{10,... | collective-permute-start | bytes 589832 | tf_op jit(solution)/shard_map/ppermute | solution.py:941
  64.2 9.4 %collective-permute-start.11 = (bf16[64,1536]{1,0:T(8,128)(2,1)S(1)}, bf16[64,1536]{1,0:T(8,128)(2,1)S(1)}, u32[]{:S(2)}, u32[]{:S(2)}) collective-permute-start(bf16[64,1536]{1,0:T(8,128)(2,1)S(1)} %get-tuple-element.155), channel_id=1, source_target_pairs={{0,2},{1,3},{2,10},{3,11},{4,6},{5,7},{6,14},{7,15},{8,0},{9,1},{1... | collective-permute-start | bytes 589832 | tf_op jit(solution)/shard_map/ppermute | solution.py:941
  64.3 17.9 %collective-permute-start.12 = (bf16[64,1536]{1,0:T(8,128)(2,1)S(1)}, bf16[64,1536]{1,0:T(8,128)(2,1)S(1)}, u32[]{:S(2)}, u32[]{:S(2)}) collective-permute-start(bf16[64,1536]{1,0:T(8,128)(2,1)S(1)} %get-tuple-element.156), channel_id=1, source_target_pairs={{0,16},{1,17},{2,24},{3,25},{4,20},{5,21},{6,28},{7,29},{8,18},{9,... | collective-permute-start | bytes 589832 | tf_op jit(solution)/shard_map/ppermute | solution.py:941
  68.1 14.0 %collective-permute-start.13 = (bf16[64,1536]{1,0:T(8,128)(2,1)S(1)}, bf16[64,1536]{1,0:T(8,128)(2,1)S(1)}, u32[]{:S(2)}, u32[]{:S(2)}) collective-permute-start(bf16[64,1536]{1,0:T(8,128)(2,1)S(1)} %get-tuple-element.157), channel_id=1, source_target_pairs={{0,18},{1,19},{2,26},{3,27},{4,22},{5,23},{6,30},{7,31},{8,16},{9,... | collective-permute-start | bytes 589832 | tf_op jit(solution)/shard_map/ppermute | solution.py:941
  83.4 223.2 %reduce-scatter.2.cloned.1.call-start = ((), (), s32[]{:S(2)}) async-start(), calls=%async_computation.1 | async-start | bytes 7077888 | tf_op jit(solution)/shard_map/reduce_scatter | solution.py:1228
  83.9 16.1 %collective-permute-start.16 = (bf16[768,384]{1,0:T(8,128)(2,1)S(1)}, bf16[768,384]{1,0:T(8,128)(2,1)S(1)}, u32[]{:S(2)}, u32[]{:S(2)}) collective-permute-start(bf16[768,384]{1,0:T(8,128)(2,1)S(1)} %maximum_select_fusion.3), channel_id=1, source_target_pairs={{0,16},{1,17},{2,18},{3,19},{4,20},{5,21},{6,22},{7,23},{8,24},{9,... | collective-permute-start | bytes 1769480 | tf_op jit(solution)/shard_map/ppermute | solution.py:941
  87.1 14.4 %collective-permute-start.15 = (bf16[2,384,384]{2,1,0:T(8,128)(2,1)S(1)}, bf16[2,384,384]{2,1,0:T(8,128)(2,1)S(1)}, u32[]{:S(2)}, u32[]{:S(2)}) collective-permute-start(bf16[2,384,384]{2,1,0:T(8,128)(2,1)S(1)} %pad_maximum_fusion.1), channel_id=1, source_target_pairs={{0,2},{1,3},{2,10},{3,11},{4,6},{5,7},{6,14},{7,15},{8,0},{9,1},{1... | collective-permute-start | bytes 1769480 | tf_op jit(solution)/shard_map/ppermute | solution.py:941
  90.4 25.3 %collective-permute-start.14 = (bf16[2,384,384]{2,1,0:T(8,128)(2,1)S(1)}, bf16[2,384,384]{2,1,0:T(8,128)(2,1)S(1)}, u32[]{:S(2)}, u32[]{:S(2)}) collective-permute-start(bf16[2,384,384]{2,1,0:T(8,128)(2,1)S(1)} %pad_maximum_fusion.1), channel_id=1, source_target_pairs={{0,0},{1,1},{2,8},{3,9},{4,4},{5,5},{6,12},{7,13},{8,2},{9,3},{10,... | collective-permute-start | bytes 1769480 | tf_op jit(solution)/shard_map/ppermute | solution.py:941
  119.2 28.7 %collective-permute-start.17 = (bf16[2,768,384]{2,1,0:T(8,128)(2,1)S(1)}, bf16[2,768,384]{2,1,0:T(8,128)(2,1)S(1)}, u32[]{:S(2)}, u32[]{:S(2)}) collective-permute-start(bf16[2,768,384]{2,1,0:T(8,128)(2,1)S(1)} %maximum_select_fusion.2), channel_id=1, source_target_pairs={{0,16},{1,17},{2,18},{3,19},{4,20},{5,21},{6,22},{7,23},{8,24},{9,... | collective-permute-start | bytes 3538952 | tf_op jit(solution)/shard_map/ppermute | solution.py:941
  172.4 22.7 %slice-start = ((s8[6291456]{0:T(1024)(128)(4,1)}), s8[2097152]{0:T(1024)(128)(4,1)S(1)}, s32[]{:S(2)}) async-start(s8[6291456]{0:T(1024)(128)(4,1)} %bitcast.123), calls=%async_computation.4 | async-start | bytes 4194304
  173.2 1.3 collective-permute-start.18
  174.5 6.6 %collective-permute-start.19 = (f32[8,2048]{1,0:T(8,128)S(1)}, f32[8,2048]{1,0:T(8,128)S(1)}, u32[]{:S(2)}, u32[]{:S(2)}) collective-permute-start(f32[8,2048]{1,0:T(8,128)S(1)} %add.243), channel_id=1, source_target_pairs={{0,1},{1,0},{2,3},{3,2},{4,5},{5,4},{6,7},{7,6},{8,9},{9,8},{10,11... | collective-permute-start | bytes 196616 | tf_op jit(solution)/shard_map/ppermute | solution.py:941
  181.1 3.2 collective-permute-start.20
  208.5 29.0 %collective-permute-start.21 = (bf16[2,768,384]{1,2,0:T(8,128)(2,1)}, bf16[2,768,384]{1,2,0:T(8,128)(2,1)S(1)}, u32[]{:S(2)}, u32[]{:S(2)}) collective-permute-start(bf16[2,768,384]{1,2,0:T(8,128)(2,1)} %pad_maximum_fusion), channel_id=1, source_target_pairs={{0,16},{1,17},{2,18},{3,19},{4,20},{5,21},{6,22},{7,23},{8,24},{9,... | collective-permute-start | bytes 3538952 | tf_op jit(solution)/shard_map/ppermute | solution.py:941
  235.1 35.7 %collective-permute-start.22 = (bf16[2,2,128,1536]{3,2,1,0:T(8,128)(2,1)}, bf16[2,2,128,1536]{3,2,1,0:T(8,128)(2,1)}, u32[]{:S(2)}, u32[]{:S(2)}) collective-permute-start(bf16[2,2,128,1536]{3,2,1,0:T(8,128)(2,1)} %get-tuple-element.195), channel_id=1, source_target_pairs={{0,8},{1,9},{2,10},{3,11},{4,12},{5,13},{6,14},{7,15},{8,0},{9,1},... | collective-permute-start | bytes 4718600 | tf_op jit(solution)/shard_map/ppermute | solution.py:941
  238.1 28.5 %collective-permute-start.23 = (bf16[768,384]{0,1:T(8,128)(2,1)S(1)}, bf16[768,384]{0,1:T(8,128)(2,1)S(1)}, u32[]{:S(2)}, u32[]{:S(2)}) collective-permute-start(bf16[768,384]{0,1:T(8,128)(2,1)S(1)} %pad_maximum_fusion.2), channel_id=1, source_target_pairs={{0,0},{1,1},{8,2},{9,3},{4,4},{5,5},{12,6},{13,7},{2,8},{3,9},{10,... | collective-permute-start | bytes 1769480 | tf_op jit(solution)/shard_map/ppermute | solution.py:941
  242.8 23.8 %collective-permute-start.24 = (bf16[768,384]{0,1:T(8,128)(2,1)S(1)}, bf16[768,384]{0,1:T(8,128)(2,1)S(1)}, u32[]{:S(2)}, u32[]{:S(2)}) collective-permute-start(bf16[768,384]{0,1:T(8,128)(2,1)S(1)} %pad_maximum_fusion.3), channel_id=1, source_target_pairs={{2,0},{3,1},{10,2},{11,3},{6,4},{7,5},{14,6},{15,7},{0,8},{1,9},{8... | collective-permute-start | bytes 1769480 | tf_op jit(solution)/shard_map/ppermute | solution.py:941
  268.2 5.9 %collective-permute-start.25 = (bf16[2,2,128,1536]{3,2,1,0:T(8,128)(2,1)}, bf16[2,2,128,1536]{3,2,1,0:T(8,128)(2,1)S(1)}, u32[]{:S(2)}, u32[]{:S(2)}) collective-permute-start(bf16[2,2,128,1536]{3,2,1,0:T(8,128)(2,1)} %get-tuple-element.200), channel_id=1, source_target_pairs={{0,8},{1,9},{2,10},{3,11},{4,12},{5,13},{6,14},{7,15},{8,0},{9,1},... | collective-permute-start | bytes 4718600 | tf_op jit(solution)/shard_map/ppermute | solution.py:941
  281.0 19.0 %collective-permute-start.26 = (bf16[2,128,1536]{2,1,0:T(8,128)(2,1)}, bf16[2,128,1536]{2,1,0:T(8,128)(2,1)S(1)}, u32[]{:S(2)}, u32[]{:S(2)}) collective-permute-start(bf16[2,128,1536]{2,1,0:T(8,128)(2,1)} %get-tuple-element.208), channel_id=1, source_target_pairs={{0,1},{1,0},{2,3},{3,2},{4,5},{5,4},{6,7},{7,6},{8,9},{9,8},{10,11... | collective-permute-start | bytes 2359304 | tf_op jit(solution)/shard_map/ppermute | solution.py:941
  281.2 20.2 %collective-permute-start.27 = (bf16[2,128,1536]{2,1,0:T(8,128)(2,1)}, bf16[2,128,1536]{2,1,0:T(8,128)(2,1)S(1)}, u32[]{:S(2)}, u32[]{:S(2)}) collective-permute-start(bf16[2,128,1536]{2,1,0:T(8,128)(2,1)} %get-tuple-element.210), channel_id=1, source_target_pairs={{0,4},{1,5},{2,6},{3,7},{4,0},{5,1},{6,2},{7,3},{8,12},{9,13},{10,... | collective-permute-start | bytes 2359304 | tf_op jit(solution)/shard_map/ppermute | solution.py:941
  301.7 4.9 %collective-permute-start.28 = (bf16[144,1536]{1,0:T(8,128)(2,1)S(1)}, bf16[144,1536]{1,0:T(8,128)(2,1)}, u32[]{:S(2)}, u32[]{:S(2)}) collective-permute-start(bf16[144,1536]{1,0:T(8,128)(2,1)S(1)} %pad_maximum_fusion.4), channel_id=1, source_target_pairs={{0,8},{1,9},{2,10},{3,11},{4,12},{5,13},{6,14},{7,15},{8,0},{9,1},... | collective-permute-start | bytes 1327112 | tf_op jit(solution)/shard_map/ppermute | solution.py:941
  309.5 7.1 %collective-permute-start.29 = (bf16[80,1536]{1,0:T(8,128)(2,1)S(1)}, bf16[80,1536]{1,0:T(8,128)(2,1)}, u32[]{:S(2)}, u32[]{:S(2)}) collective-permute-start(bf16[80,1536]{1,0:T(8,128)(2,1)S(1)} %pad_maximum_fusion.5), channel_id=1, source_target_pairs={{0,1},{1,0},{2,3},{3,2},{4,5},{5,4},{6,7},{7,6},{8,9},{9,8},{10,11... | collective-permute-start | bytes 737288 | tf_op jit(solution)/shard_map/ppermute | solution.py:941
  313.0 23.2 %collective-permute-start.44 = (bf16[2,384,384]{2,1,0:T(8,128)(2,1)S(1)}, bf16[2,384,384]{2,1,0:T(8,128)(2,1)S(1)}, u32[]{:S(2)}, u32[]{:S(2)}) collective-permute-start(bf16[2,384,384]{2,1,0:T(8,128)(2,1)S(1)} %copy-done.17), channel_id=1, source_target_pairs={{0,16},{1,17},{2,18},{3,19},{4,20},{5,21},{6,22},{7,23},{8,24},{9,... | collective-permute-start | bytes 1769480 | tf_op jit(solution)/shard_map/ppermute | solution.py:941
  314.0 9.7 %collective-permute-start.30 = (bf16[128,1536]{1,0:T(8,128)(2,1)}, bf16[128,1536]{1,0:T(8,128)(2,1)S(1)}, u32[]{:S(2)}, u32[]{:S(2)}) collective-permute-start(bf16[128,1536]{1,0:T(8,128)(2,1)} %get-tuple-element.226), channel_id=1, source_target_pairs={{0,4},{1,5},{2,6},{3,7},{4,0},{5,1},{6,2},{7,3},{8,12},{9,13},{10,... | collective-permute-start | bytes 1179656 | tf_op jit(solution)/shard_map/ppermute | solution.py:941
  315.5 9.4 %collective-permute-start.31 = (bf16[128,1536]{1,0:T(8,128)(2,1)}, bf16[128,1536]{1,0:T(8,128)(2,1)S(1)}, u32[]{:S(2)}, u32[]{:S(2)}) collective-permute-start(bf16[128,1536]{1,0:T(8,128)(2,1)} %get-tuple-element.228), channel_id=1, source_target_pairs={{0,1},{1,0},{2,3},{3,2},{4,5},{5,4},{6,7},{7,6},{8,9},{9,8},{10,11... | collective-permute-start | bytes 1179656 | tf_op jit(solution)/shard_map/ppermute | solution.py:941
  319.4 17.3 %copy-start.14 = (bf16[768,384]{0,1:T(8,128)(2,1)S(1)}, bf16[768,384]{0,1:T(8,128)(2,1)}, u32[]{:S(2)}) copy-start(bf16[768,384]{0,1:T(8,128)(2,1)} %copy-done.13) | copy-start | bytes 1769476
  327.5 12.2 %collective-permute-start.40 = (bf16[48,1536]{1,0:T(8,128)(2,1)S(1)}, bf16[48,1536]{1,0:T(8,128)(2,1)S(1)}, u32[]{:S(2)}, u32[]{:S(2)}) collective-permute-start(bf16[48,1536]{1,0:T(8,128)(2,1)S(1)} %pad_maximum_fusion.6), channel_id=1, source_target_pairs={{0,4},{1,5},{2,6},{3,7},{4,0},{5,1},{6,2},{7,3},{8,12},{9,13},{10,... | collective-permute-start | bytes 442376 | tf_op jit(solution)/shard_map/ppermute | solution.py:941
  330.1 20.1 %collective-permute-start.36 = (bf16[64,1536]{1,0:T(8,128)(2,1)S(1)}, bf16[64,1536]{1,0:T(8,128)(2,1)S(1)}, u32[]{:S(2)}, u32[]{:S(2)}) collective-permute-start(bf16[64,1536]{1,0:T(8,128)(2,1)S(1)} %get-tuple-element.246), channel_id=1, source_target_pairs={{0,0},{1,1},{8,2},{9,3},{4,4},{5,5},{12,6},{13,7},{2,8},{3,9},{10,... | collective-permute-start | bytes 589832 | tf_op jit(solution)/shard_map/ppermute | solution.py:941
  335.3 15.0 %collective-permute-start.37 = (bf16[64,1536]{1,0:T(8,128)(2,1)S(1)}, bf16[64,1536]{1,0:T(8,128)(2,1)S(1)}, u32[]{:S(2)}, u32[]{:S(2)}) collective-permute-start(bf16[64,1536]{1,0:T(8,128)(2,1)S(1)} %get-tuple-element.247), channel_id=1, source_target_pairs={{2,0},{3,1},{10,2},{11,3},{6,4},{7,5},{14,6},{15,7},{0,8},{1,9},{8... | collective-permute-start | bytes 589832 | tf_op jit(solution)/shard_map/ppermute | solution.py:941
  335.4 18.8 %collective-permute-start.38 = (bf16[64,1536]{1,0:T(8,128)(2,1)S(1)}, bf16[64,1536]{1,0:T(8,128)(2,1)S(1)}, u32[]{:S(2)}, u32[]{:S(2)}) collective-permute-start(bf16[64,1536]{1,0:T(8,128)(2,1)S(1)} %get-tuple-element.248), channel_id=1, source_target_pairs={{16,0},{17,1},{24,2},{25,3},{20,4},{21,5},{28,6},{29,7},{18,8},{19... | collective-permute-start | bytes 589832 | tf_op jit(solution)/shard_map/ppermute | solution.py:941
  336.3 17.9 %collective-permute-start.39 = (bf16[64,1536]{1,0:T(8,128)(2,1)S(1)}, bf16[64,1536]{1,0:T(8,128)(2,1)S(1)}, u32[]{:S(2)}, u32[]{:S(2)}) collective-permute-start(bf16[64,1536]{1,0:T(8,128)(2,1)S(1)} %get-tuple-element.249), channel_id=1, source_target_pairs={{18,0},{19,1},{26,2},{27,3},{22,4},{23,5},{30,6},{31,7},{16,8},{17... | collective-permute-start | bytes 589832 | tf_op jit(solution)/shard_map/ppermute | solution.py:941
  339.7 22.1 %collective-permute-start.32 = (bf16[64,1536]{1,0:T(8,128)(2,1)S(1)}, bf16[64,1536]{1,0:T(8,128)(2,1)S(1)}, u32[]{:S(2)}, u32[]{:S(2)}) collective-permute-start(bf16[64,1536]{1,0:T(8,128)(2,1)S(1)} %get-tuple-element.242), channel_id=1, source_target_pairs={{0,0},{1,1},{8,2},{9,3},{4,4},{5,5},{12,6},{13,7},{2,8},{3,9},{10,... | collective-permute-start | bytes 589832 | tf_op jit(solution)/shard_map/ppermute | solution.py:941
  350.2 17.9 %collective-permute-start.33 = (bf16[64,1536]{1,0:T(8,128)(2,1)S(1)}, bf16[64,1536]{1,0:T(8,128)(2,1)S(1)}, u32[]{:S(2)}, u32[]{:S(2)}) collective-permute-start(bf16[64,1536]{1,0:T(8,128)(2,1)S(1)} %get-tuple-element.243), channel_id=1, source_target_pairs={{2,0},{3,1},{10,2},{11,3},{6,4},{7,5},{14,6},{15,7},{0,8},{1,9},{8... | collective-permute-start | bytes 589832 | tf_op jit(solution)/shard_map/ppermute | solution.py:941
  350.3 18.6 %collective-permute-start.34 = (bf16[64,1536]{1,0:T(8,128)(2,1)S(1)}, bf16[64,1536]{1,0:T(8,128)(2,1)S(1)}, u32[]{:S(2)}, u32[]{:S(2)}) collective-permute-start(bf16[64,1536]{1,0:T(8,128)(2,1)S(1)} %get-tuple-element.244), channel_id=1, source_target_pairs={{16,0},{17,1},{24,2},{25,3},{20,4},{21,5},{28,6},{29,7},{18,8},{19... | collective-permute-start | bytes 589832 | tf_op jit(solution)/shard_map/ppermute | solution.py:941
  354.2 14.7 %collective-permute-start.35 = (bf16[64,1536]{1,0:T(8,128)(2,1)S(1)}, bf16[64,1536]{1,0:T(8,128)(2,1)S(1)}, u32[]{:S(2)}, u32[]{:S(2)}) collective-permute-start(bf16[64,1536]{1,0:T(8,128)(2,1)S(1)} %get-tuple-element.245), channel_id=1, source_target_pairs={{18,0},{19,1},{26,2},{27,3},{22,4},{23,5},{30,6},{31,7},{16,8},{17... | collective-permute-start | bytes 589832 | tf_op jit(solution)/shard_map/ppermute | solution.py:941
  354.2 16.0 %collective-permute-start.41 = (bf16[2,80,384]{2,1,0:T(8,128)(2,1)S(1)}, bf16[2,80,384]{2,1,0:T(8,128)(2,1)S(1)}, u32[]{:S(2)}, u32[]{:S(2)}) collective-permute-start(bf16[2,80,384]{2,1,0:T(8,128)(2,1)S(1)} %pad_maximum_fusion.7), channel_id=1, source_target_pairs={{0,16},{1,17},{2,18},{3,19},{4,20},{5,21},{6,22},{7,23},{8,24},{9,... | collective-permute-start | bytes 368648 | tf_op jit(solution)/shard_map/ppermute | solution.py:941
  361.9 12.1 %collective-permute-start.45 = (bf16[384,384]{1,0:T(8,128)(2,1)S(1)}, bf16[384,384]{1,0:T(8,128)(2,1)S(1)}, u32[]{:S(2)}, u32[]{:S(2)}) collective-permute-start(bf16[384,384]{1,0:T(8,128)(2,1)S(1)} %copy-done.22), channel_id=1, source_target_pairs={{0,0},{1,1},{8,2},{9,3},{4,4},{5,5},{12,6},{13,7},{2,8},{3,9},{10,... | collective-permute-start | bytes 884744 | tf_op jit(solution)/shard_map/ppermute | solution.py:941
  368.2 6.8 %collective-permute-start.46 = (bf16[384,384]{1,0:T(8,128)(2,1)S(1)}, bf16[384,384]{1,0:T(8,128)(2,1)S(1)}, u32[]{:S(2)}, u32[]{:S(2)}) collective-permute-start(bf16[384,384]{1,0:T(8,128)(2,1)S(1)} %copy-done.21), channel_id=1, source_target_pairs={{2,0},{3,1},{10,2},{11,3},{6,4},{7,5},{14,6},{15,7},{0,8},{1,9},{8... | collective-permute-start | bytes 884744 | tf_op jit(solution)/shard_map/ppermute | solution.py:941
  370.2 18.2 %copy-start.29 = (bf16[1536]{0:T(1024)(128)(2,1)S(1)}, bf16[1536]{0:T(1024)(128)(2,1)}, u32[]{:S(2)}) copy-start(bf16[1536]{0:T(1024)(128)(2,1)} %param.26) | copy-start | bytes 9220
  370.3 13.2 %collective-permute-start.42 = (bf16[80,384]{1,0:T(8,128)(2,1)S(1)}, bf16[80,384]{1,0:T(8,128)(2,1)S(1)}, u32[]{:S(2)}, u32[]{:S(2)}) collective-permute-start(bf16[80,384]{1,0:T(8,128)(2,1)S(1)} %get-tuple-element.255), channel_id=1, source_target_pairs={{0,0},{1,1},{8,2},{9,3},{4,4},{5,5},{12,6},{13,7},{2,8},{3,9},{10,... | collective-permute-start | bytes 184328 | tf_op jit(solution)/shard_map/ppermute | solution.py:941
  373.9 9.6 %collective-permute-start.43 = (bf16[80,384]{1,0:T(8,128)(2,1)S(1)}, bf16[80,384]{1,0:T(8,128)(2,1)S(1)}, u32[]{:S(2)}, u32[]{:S(2)}) collective-permute-start(bf16[80,384]{1,0:T(8,128)(2,1)S(1)} %get-tuple-element.256), channel_id=1, source_target_pairs={{2,0},{3,1},{10,2},{11,3},{6,4},{7,5},{14,6},{15,7},{0,8},{1,9},{8... | collective-permute-start | bytes 184328 | tf_op jit(solution)/shard_map/ppermute | solution.py:941
  (37 other events, 219.7 us)
Sparse Core Ops, SparseCore 0:
  48.2 63.6 all-gather.6
  114.1 36.9 all-gather.4
  172.5 72.7 reduce-scatter.1

commit v4 on v3

--- a/solution.py
+++ b/solution.py
@@ -672,7 +672,7 @@
             jax.ShapeDtypeStruct((length, width), BF16),
             jax.ShapeDtypeStruct((8, width), F32),
         ],
-        compiler_params=kernel_params(56),
+        compiler_params=kernel_params(32),
         cost_estimate=cost(length * width * 20, length * width, length * width * 20),
         name="gate",
     )(bounds, stats, grad_normed, gate, scanned, norm_gate)

time: 403 us -> 401 us (level)
  waiting for transfers between devices: 88.8 us -> 98 us
  starting transfers between devices: 86.2 us -> 81.1 us
    ppermute x47, waiting for transfers between devices: 87.8 us -> 97 us  [swap(): return lax.ppermute(v, ALL, perm)]
    ppermute x47, starting transfers between devices: 86 us -> 81 us  [swap(): return lax.ppermute(v, ALL, perm)]
    pallas_call x1, Pallas kernels: 10.1 us -> 6.06 us  [run_gate(): pl.pallas_call(partial(gate_kernel, live_ids, inner_full), grid=(micro_co...]
    unnamed x107 -> x109, local copies, waits for them, and re-layouts: 11.4 us -> 14.5 us
  transfers between devices with their start and end apart: 50 -> 50, of which waited for: 22 -> 23; matrix products, arithmetic and copies ran while one was open for 16% -> 14% of each run, Pallas kernels for 26% -> 25%
where the time goes in v4:
time: 401 us; the launch traced here: 395 us
  Pallas kernels  116 us (29%)
  waiting for transfers between devices  98 us (24%)
  starting transfers between devices  81.1 us (20%)
  local copies, waits for them, and re-layouts  37.6 us (9%)
  matrix products  27.2 us (7%)
  other arithmetic  19.8 us (5%)
  between operations  15.3 us (4%)
    ppermute x47, waiting for transfers between devices, swap(): return lax.ppermute(v, ALL, perm)  97 us
    ppermute x47, starting transfers between devices, swap(): return lax.ppermute(v, ALL, perm)  81 us
    pallas_call x2, Pallas kernels, run_backward(): pl.pallas_call(partial(backward_kernel, width // LANES, micro, earlier is...  47.5 us
    pallas_call x1, Pallas kernels, run_forward(): pl.pallas_call(partial(forward_kernel, width // LANES), grid=(micro_count...  26.4 us
    dot_general x4, matrix products, dot_tn(): lax.dot_general(a, b, (((0,), (0,)), ((), ())), preferred_element_type=F32)  20.4 us
    unnamed x109, local copies, waits for them, and re-layouts  14.5 us
    pallas_call x1, Pallas kernels, run_back(): pl.pallas_call(partial(back_kernel, live_ids), grid=(micro_count, blocks)...  14.5 us
    pallas_call x2, Pallas kernels, run_halves(): pl.pallas_call(partial(halves_kernel, axes), in_specs=[smem_spec()] + [vm...  9.67 us
  transfers between devices with their start and end apart: 50, of which 23 were waited for; matrix products, arithmetic and copies ran while one was open for 14% of the time, Pallas kernels for 25%

profile of v4, /device:TPU:1, one launch (start us, length us, event | category | flops | bytes accessed | tf_op | source)
XLA Modules:
  0.0 394.7 jit_solution(6840893163218383037)
XLA Ops:
  12.5 1.5 deal.1
  14.1 5.6 %collective-permute-start.4 = (bf16[48,384]{1,0:T(8,128)(2,1)S(1)}, bf16[48,384]{1,0:T(8,128)(2,1)S(1)}, u32[]{:S(2)}, u32[]{:S(2)}) collective-permute-start(bf16[48,384]{1,0:T(8,128)(2,1)S(1)} %maximum_maximum_fusion.1), channel_id=1, source_target_pairs={{0,0},{1,1},{2,8},{3,9},{4,4},{5,5},{6,12},{7,13},{8,2},{9,3},{10,... | collective-permute-start | bytes 110600 | tf_op jit(solution)/shard_map/ppermute | solution.py:941
  19.7 1.9 collective-permute-start
  21.7 3.7 collective-permute-start.2
  26.8 1.9 collective-permute-start.7
  28.7 14.5 %collective-permute-done.7 = f32[40,384]{1,0:T(8,128)S(1)} collective-permute-done((f32[40,384]{1,0:T(8,128)S(1)}, f32[40,384]{1,0:T(8,128)S(1)}, u32[]{:S(2)}, u32[]{:S(2)}) %collective-permute-start.7) | collective-permute-done | bytes 61472 | tf_op jit(solution)/shard_map/ppermute | solution.py:941
  43.2 1.7 collective-permute-start.6
  44.9 1.6 collective-permute-done.6
  46.7 1.3 pick.4.dealt_ref
  48.2 2.7 collective-permute-start.8
  50.9 10.2 %collective-permute-done.9 = bf16[384,384]{1,0:T(8,128)(2,1)S(1)} collective-permute-done((bf16[384,384]{1,0:T(8,128)(2,1)S(1)}, bf16[384,384]{1,0:T(8,128)(2,1)S(1)}, u32[]{:S(2)}, u32[]{:S(2)}) %collective-permute-start.9) | collective-permute-done | bytes 294944 | tf_op jit(solution)/shard_map/ppermute | solution.py:941
  62.3 1.9 collective-permute-start.10
  64.3 3.9 collective-permute-start.12
  68.9 4.6 %collective-permute-done.10.refs_0_ = bf16[64,1536]{1,0:T(8,128)(2,1)S(1)} collective-permute-done((bf16[64,1536]{1,0:T(8,128)(2,1)S(1)}, bf16[64,1536]{1,0:T(8,128)(2,1)S(1)}, u32[]{:S(2)}, u32[]{:S(2)}) %collective-permute-start.10) | collective-permute-done | bytes 196640 | tf_op jit(solution)/shard_map/ppermute | solution.py:941
  73.5 8.6 %collective-permute-done.12.refs_2_ = bf16[64,1536]{1,0:T(8,128)(2,1)S(1)} collective-permute-done((bf16[64,1536]{1,0:T(8,128)(2,1)S(1)}, bf16[64,1536]{1,0:T(8,128)(2,1)S(1)}, u32[]{:S(2)}, u32[]{:S(2)}) %collective-permute-start.12) | collective-permute-done | bytes 196640 | tf_op jit(solution)/shard_map/ppermute | solution.py:941
  84.4 1.3 broadcast_in_dim.49.norm_in_ref
  87.1 3.3 collective-permute-start.15
  90.4 4.9 %collective-permute-start.14 = (bf16[2,384,384]{2,1,0:T(8,128)(2,1)S(1)}, bf16[2,384,384]{2,1,0:T(8,128)(2,1)S(1)}, u32[]{:S(2)}, u32[]{:S(2)}) collective-permute-start(bf16[2,384,384]{2,1,0:T(8,128)(2,1)S(1)} %pad_maximum_fusion.1), channel_id=1, source_target_pairs={{0,0},{1,1},{2,8},{3,9},{4,4},{5,5},{6,12},{7,13},{8,2},{9,3},{10,... | collective-permute-start | bytes 1769480 | tf_op jit(solution)/shard_map/ppermute | solution.py:941
  98.1 1.3 slice.285.taps_value_ref
  100.0 1.5 maximum_select_fusion.1.w_value_ref
  101.5 14.3 %collective-permute-done.14 = bf16[2,384,384]{2,1,0:T(8,128)(2,1)S(1)} collective-permute-done((bf16[2,384,384]{2,1,0:T(8,128)(2,1)S(1)}, bf16[2,384,384]{2,1,0:T(8,128)(2,1)S(1)}, u32[]{:S(2)}, u32[]{:S(2)}) %collective-permute-start.14) | collective-permute-done | bytes 589856 | tf_op jit(solution)/shard_map/ppermute | solution.py:941
  121.4 26.4 %forward.1 = (bf16[2048,1536]{1,0:T(8,128)(2,1)}, bf16[2048,384]{1,0:T(8,128)(2,1)}, f32[2048,384]{1,0:T(8,128)}, bf16[2048,256]{1,0:T(8,128)(2,1)}, f32[2048,25...) custom-call(s32[2,4]{1,0:T(2,128)} %reduce_window_sum.11.bounds_ref, ...), custom_call_target="tpu_custom_call" | custom-call | flops 14495514624 | bytes 31457280 | tf_op jit(solution)/shard_map/forward/pallas_call | solution.py:587
  148.4 1.7 slice_bitcast_fusion
  151.1 14.5 %back.1 = (f32[2048,384]{1,0:T(8,128)}, bf16[2,2,2,256,384]{4,3,2,1,0:T(8,128)(2,1)}, bf16[2048,384]{1,0:T(8,128)(2,1)}, f32[8,2048]{1,0:T(8,128)}) custom-call(s32[2,4]{1,0:T(2,128)} %reduce_window_sum.11.bounds_ref, bf16[2,2,2,256,1536]{4,3,2,1,0:T(8,128)(2,1)} %bitcast.126, bf16[2048,1536]{1,0:T(8,128)(2,1)} %get-tuple-element.160.normed_ref, ...), custom_call_target="tpu_custom_call" | custom-call | flops 4831838208 | bytes 23592960 | tf_op jit(solution)/shard_map/back/pallas_call | solution.py:622
  165.5 6.8 %convolution_convert_fusion = bf16[2048,1536]{1,0:T(8,128)(2,1)} fusion(bf16[2048,384]{1,0:T(8,128)(2,1)} %bitcast.157, bf16[2,1536,384]{2,1,0:T(8,128)(2,1)S(1)} %maximum_select_fusion), kind=kOutput, calls=%fused_computation | convolution fusion | flops 2419064832 | bytes 9043968 | tf_op jit(solution)/shard_map/dot_general | solution.py:27
  175.4 4.4 %collective-permute-start.19 = (f32[8,2048]{1,0:T(8,128)S(1)}, f32[8,2048]{1,0:T(8,128)S(1)}, u32[]{:S(2)}, u32[]{:S(2)}) collective-permute-start(f32[8,2048]{1,0:T(8,128)S(1)} %add.243), channel_id=1, source_target_pairs={{0,1},{1,0},{2,3},{3,2},{4,5},{5,4},{6,7},{7,6},{8,9},{9,8},{10,11... | collective-permute-start | bytes 196616 | tf_op jit(solution)/shard_map/ppermute | solution.py:941
  179.8 2.2 collective-permute-done.19
  182.0 1.4 collective-permute-start.20
  184.0 1.4 collective-permute-done.20
  185.5 1.9 copy-done.1
  187.3 1.4 copy-done.2
  188.8 6.1 %gate.1 = (bf16[2048,384]{1,0:T(8,128)(2,1)S(1)}, bf16[2,2,2,256,384]{4,3,2,1,0:T(8,128)(2,1)S(1)}, bf16[2048,384]{1,0:T(8,128)(2,1)S(1)}, f32[8,384]{1,0:T(8,128)S(1)}) custom-call(s32[2,4]{1,0:T(2,128)S(1)} %copy-done.8, f32[8,2048]{1,0:T(8,128)S(1)} %add.245.stats_ref, bf16[2048,384]{1,0:T(8,128)(2,1)S(1)} %copy-done.2, f32[2048,384]{1,0:T(8,128)S(1)} %copy-done.1, ...), custom_call_target="tpu_custom_call" | custom-call | flops 15728640 | bytes 15728640 | tf_op jit(solution)/shard_map/gate/pallas_call | solution.py:652
  194.8 7.5 %convolution_convert_fusion.2 = bf16[1536,384]{1,0:T(8,128)(2,1)S(1)} fusion(bf16[2048,1536]{1,0:T(8,128)(2,1)} %get-tuple-element.160.normed_ref, bf16[2048,384]{1,0:T(8,128)(2,1)S(1)} %get-tuple-element.169.low_gate_ref), kind=kOutput, calls=%fused_computation.2 | convolution fusion | flops 2416508928 | bytes 9043968 | tf_op jit(solution)/shard_map/dot_general | solution.py:31
  202.4 3.5 convolution_convert_fusion.3
  209.7 23.8 %backward.2 = (bf16[2048,384]{1,0:T(8,128)(2,1)}, bf16[2048,384]{1,0:T(8,128)(2,1)}, bf16[2,2,128,1536]{3,2,1,0:T(8,128)(2,1)}, bf16[2,2,128,1536]{3,2,1,0:T(8,1...) custom-call(s32[3,4]{1,0:T(4,128)} %concatenate.133.bounds_ref, bf16[2048,384]{1,0:T(8,128)(2,1)} %copy-done.12, ...), custom_call_target="tpu_custom_call" | custom-call | flops 8455716864 | bytes 15728640 | tf_op jit(solution)/shard_map/backward/pallas_call | solution.py:721
  233.5 3.0 collective-permute-start.22
  237.1 6.6 %collective-permute-start.23 = (bf16[768,384]{0,1:T(8,128)(2,1)S(1)}, bf16[768,384]{0,1:T(8,128)(2,1)S(1)}, u32[]{:S(2)}, u32[]{:S(2)}) collective-permute-start(bf16[768,384]{0,1:T(8,128)(2,1)S(1)} %pad_maximum_fusion.2), channel_id=1, source_target_pairs={{0,0},{1,1},{8,2},{9,3},{4,4},{5,5},{12,6},{13,7},{2,8},{3,9},{10,... | collective-permute-start | bytes 1769480 | tf_op jit(solution)/shard_map/ppermute | solution.py:941
  243.7 23.7 %backward.3 = (bf16[2048,384]{1,0:T(8,128)(2,1)}, bf16[2048,384]{1,0:T(8,128)(2,1)}, bf16[2,2,128,1536]{3,2,1,0:T(8,128)(2,1)}, bf16[2,2,128,1536]{3,2,1,0:T(8,1...) custom-call(s32[3,4]{1,0:T(4,128)} %concatenate.133.bounds_ref, ...), custom_call_target="tpu_custom_call", output_to_operand_aliasing={{0}: (22, {}), {1}: (23, {})} | custom-call | flops 8455716864 | bytes 15728640 | tf_op jit(solution)/shard_map/backward/pallas_call | solution.py:721
  269.0 2.6 collective-permute-start.25
  271.7 3.2 collective-permute-done.25.refs_3_
  276.1 5.7 %halves.2 = (f32[2,128,1536]{2,1,0:T(8,128)}, bf16[2,128,1536]{2,1,0:T(8,128)(2,1)}, f32[2,128,1536]{2,1,0:T(8,128)}, bf16[2,128,1536]{2,1,0:T(8,128)(2,1)}) custom-call(s32[2]{0:T(128)} %pad_add_fusion.1.bits_ref, bf16[2,2,128,1536]{3,2,1,0:T(8,128)(2,1)} %get-tuple-element.194.refs_0_, bf16[2,2,128,1536]{3,2,1,0:T(8,128)(2,1)} %collective-permute-done.22.refs_1_, ...), custom_call_target="tpu_custom_call" | custom-call | tf_op jit(solution)/shard_map/halves/pallas_call | solution.py:915
  283.8 6.8 %convolution_convert_fusion.1 = bf16[1536,384]{1,0:T(8,128)(2,1)S(1)} fusion(bf16[2048,1536]{1,0:T(8,128)(2,1)} %get-tuple-element.160.normed_ref, bf16[2048,384]{1,0:T(8,128)(2,1)} %get-tuple-element.205), kind=kOutput, calls=%fused_computation.1 | convolution fusion | flops 2416508928 | bytes 9043968 | tf_op jit(solution)/shard_map/dot_general | solution.py:31
  292.4 2.6 fusion.44
  295.1 5.8 %collective-permute-done.26.refs_1_ = bf16[2,128,1536]{2,1,0:T(8,128)(2,1)S(1)} collective-permute-done((bf16[2,128,1536]{2,1,0:T(8,128)(2,1)}, bf16[2,128,1536]{2,1,0:T(8,128)(2,1)S(1)}, u32[]{:S(2)}, u32[]{:S(2)}) %collective-permute-start.26) | collective-permute-done | bytes 786464 | tf_op jit(solution)/shard_map/ppermute | solution.py:941
  303.1 4.0 %halves.3 = (f32[128,1536]{1,0:T(8,128)}, bf16[128,1536]{1,0:T(8,128)(2,1)}, f32[128,1536]{1,0:T(8,128)}, bf16[128,1536]{1,0:T(8,128)(2,1)}) custom-call(s32[2]{0:T(128)} %pad_add_fusion.1.bits_ref, f32[2,128,1536]{2,1,0:T(8,128)} %get-tuple-element.211.refs_0_, bf16[2,128,1536]{2,1,0:T(8,128)(2,1)} %copy-done.18, ...), custom_call_target="tpu_custom_call" | custom-call | tf_op jit(solution)/shard_map/halves/pallas_call | solution.py:915
  313.3 3.4 collective-permute-done.29
  318.6 2.6 collective-permute-done.30.refs_1_
  321.1 3.9 collective-permute-done.31.refs_3_
  325.1 3.2 close.2
  329.4 4.9 %collective-permute-start.36 = (bf16[64,1536]{1,0:T(8,128)(2,1)S(1)}, bf16[64,1536]{1,0:T(8,128)(2,1)S(1)}, u32[]{:S(2)}, u32[]{:S(2)}) collective-permute-start(bf16[64,1536]{1,0:T(8,128)(2,1)S(1)} %get-tuple-element.246), channel_id=1, source_target_pairs={{0,0},{1,1},{8,2},{9,3},{4,4},{5,5},{12,6},{13,7},{2,8},{3,9},{10,... | collective-permute-start | bytes 589832 | tf_op jit(solution)/shard_map/ppermute | solution.py:941
  336.8 1.7 close.3
  338.7 5.1 %collective-permute-start.32 = (bf16[64,1536]{1,0:T(8,128)(2,1)S(1)}, bf16[64,1536]{1,0:T(8,128)(2,1)S(1)}, u32[]{:S(2)}, u32[]{:S(2)}) collective-permute-start(bf16[64,1536]{1,0:T(8,128)(2,1)S(1)} %get-tuple-element.242), channel_id=1, source_target_pairs={{0,0},{1,1},{8,2},{9,3},{4,4},{5,5},{12,6},{13,7},{2,8},{3,9},{10,... | collective-permute-start | bytes 589832 | tf_op jit(solution)/shard_map/ppermute | solution.py:941
  346.0 2.1 collective-permute-done.36.refs_0_
  348.1 2.3 collective-permute-start.34
  350.5 2.3 collective-permute-done.38.refs_2_
  354.4 2.2 copy.91
  356.7 1.3 pick.7
  357.9 2.8 collective-permute-done.32.refs_0_
  360.8 3.1 collective-permute-start.45
  363.9 3.6 collective-permute-done.34.refs_2_
  367.5 1.3 pick.6
  370.5 3.4 collective-permute-start.42
  374.0 4.7 %collective-permute-done.45 = bf16[384,384]{1,0:T(8,128)(2,1)S(1)} collective-permute-done((bf16[384,384]{1,0:T(8,128)(2,1)S(1)}, bf16[384,384]{1,0:T(8,128)(2,1)S(1)}, u32[]{:S(2)}, u32[]{:S(2)}) %collective-permute-start.45) | collective-permute-done | bytes 294944 | tf_op jit(solution)/shard_map/ppermute | solution.py:941
  379.5 2.9 collective-permute-done.42
  (302 shorter events, 63.7 us)
Async XLA Ops:
  7.2 18.3 %copy-start.41 = (f32[32]{0:T(128)S(1)}, f32[32]{0:T(128)}, u32[]{:S(2)}) copy-start(f32[32]{0:T(128)} %param.34) | copy-start | bytes 388
  7.2 18.2 %copy-start.36 = (f32[4,32]{1,0:T(4,128)S(1)}, f32[4,32]{1,0:T(4,128)}, u32[]{:S(2)}) copy-start(f32[4,32]{1,0:T(4,128)} %param.33) | copy-start | bytes 1540
  7.2 18.3 %copy-start.42 = (f32[6]{0:T(128)S(1)}, f32[6]{0:T(128)}, u32[]{:S(2)}) copy-start(f32[6]{0:T(128)} %param.37) | copy-start | bytes 76
  7.2 18.3 %copy-start.43 = (f32[6]{0:T(128)S(1)}, f32[6]{0:T(128)}, u32[]{:S(2)}) copy-start(f32[6]{0:T(128)} %param.36) | copy-start | bytes 76
  7.2 18.3 %copy-start.44 = (f32[6]{0:T(128)S(1)}, f32[6]{0:T(128)}, u32[]{:S(2)}) copy-start(f32[6]{0:T(128)} %param.35) | copy-start | bytes 76
  7.2 18.3 %copy-start.39 = (s32[2,4]{1,0:T(2,128)S(1)}, s32[2,4]{1,0:T(2,128)}, u32[]{:S(2)}) copy-start(s32[2,4]{1,0:T(2,128)} %param.24) | copy-start | bytes 100
  7.2 18.3 %copy-start.38 = (f32[384]{0:T(512)S(1)}, f32[384]{0:T(512)}, u32[]{:S(2)}) copy-start(f32[384]{0:T(512)} %param.32) | copy-start | bytes 4612
  7.3 18.4 %copy-start.35 = (f32[4,384]{1,0:T(4,128)S(1)}, f32[4,384]{1,0:T(4,128)}, u32[]{:S(2)}) copy-start(f32[4,384]{1,0:T(4,128)} %param.31) | copy-start | bytes 18436
  7.3 18.4 %copy-start.37 = (f32[384]{0:T(512)S(1)}, f32[384]{0:T(512)}, u32[]{:S(2)}) copy-start(f32[384]{0:T(512)} %param.38) | copy-start | bytes 4612
  7.3 108.5 %all-gather.7.cloned.1.call-start = ((), (), s32[]{:S(2)}) async-start(), calls=%async_computation.3 | async-start | bytes 8404992 | tf_op jit(solution)/shard_map/all_gather | solution.py:1187
  14.0 11.7 %collective-permute-start.5 = (bf16[48,384]{1,0:T(8,128)(2,1)S(1)}, bf16[48,384]{1,0:T(8,128)(2,1)S(1)}, u32[]{:S(2)}, u32[]{:S(2)}) collective-permute-start(bf16[48,384]{1,0:T(8,128)(2,1)S(1)} %maximum_maximum_fusion.1), channel_id=1, source_target_pairs={{0,2},{1,3},{2,10},{3,11},{4,6},{5,7},{6,14},{7,15},{8,0},{9,1},{1... | collective-permute-start | bytes 110600 | tf_op jit(solution)/shard_map/ppermute | solution.py:941
  14.1 12.6 %collective-permute-start.4 = (bf16[48,384]{1,0:T(8,128)(2,1)S(1)}, bf16[48,384]{1,0:T(8,128)(2,1)S(1)}, u32[]{:S(2)}, u32[]{:S(2)}) collective-permute-start(bf16[48,384]{1,0:T(8,128)(2,1)S(1)} %maximum_maximum_fusion.1), channel_id=1, source_target_pairs={{0,0},{1,1},{2,8},{3,9},{4,4},{5,5},{6,12},{7,13},{8,2},{9,3},{10,... | collective-permute-start | bytes 110600 | tf_op jit(solution)/shard_map/ppermute | solution.py:941
  19.7 27.0 %collective-permute-start = (bf16[64,1536]{1,0:T(8,128)(2,1)S(1)}, bf16[64,1536]{1,0:T(8,128)(2,1)S(1)}, u32[]{:S(2)}, u32[]{:S(2)}) collective-permute-start(bf16[64,1536]{1,0:T(8,128)(2,1)S(1)} %get-tuple-element.143), channel_id=1, source_target_pairs={{0,0},{1,1},{2,8},{3,9},{4,4},{5,5},{6,12},{7,13},{8,2},{9,3},{10,... | collective-permute-start | bytes 589832 | tf_op jit(solution)/shard_map/ppermute | solution.py:941
  21.6 25.1 %collective-permute-start.1 = (bf16[64,1536]{1,0:T(8,128)(2,1)S(1)}, bf16[64,1536]{1,0:T(8,128)(2,1)S(1)}, u32[]{:S(2)}, u32[]{:S(2)}) collective-permute-start(bf16[64,1536]{1,0:T(8,128)(2,1)S(1)} %get-tuple-element.144), channel_id=1, source_target_pairs={{0,2},{1,3},{2,10},{3,11},{4,6},{5,7},{6,14},{7,15},{8,0},{9,1},{1... | collective-permute-start | bytes 589832 | tf_op jit(solution)/shard_map/ppermute | solution.py:941
  21.7 25.0 %collective-permute-start.2 = (bf16[64,1536]{1,0:T(8,128)(2,1)S(1)}, bf16[64,1536]{1,0:T(8,128)(2,1)S(1)}, u32[]{:S(2)}, u32[]{:S(2)}) collective-permute-start(bf16[64,1536]{1,0:T(8,128)(2,1)S(1)} %get-tuple-element.145), channel_id=1, source_target_pairs={{0,16},{1,17},{2,24},{3,25},{4,20},{5,21},{6,28},{7,29},{8,18},{9,... | collective-permute-start | bytes 589832 | tf_op jit(solution)/shard_map/ppermute | solution.py:941
  25.7 21.0 %collective-permute-start.3 = (bf16[64,1536]{1,0:T(8,128)(2,1)S(1)}, bf16[64,1536]{1,0:T(8,128)(2,1)S(1)}, u32[]{:S(2)}, u32[]{:S(2)}) collective-permute-start(bf16[64,1536]{1,0:T(8,128)(2,1)S(1)} %get-tuple-element.146), channel_id=1, source_target_pairs={{0,18},{1,19},{2,26},{3,27},{4,22},{5,23},{6,30},{7,31},{8,16},{9,... | collective-permute-start | bytes 589832 | tf_op jit(solution)/shard_map/ppermute | solution.py:941
  26.8 16.4 %collective-permute-start.7 = (f32[40,384]{1,0:T(8,128)S(1)}, f32[40,384]{1,0:T(8,128)S(1)}, u32[]{:S(2)}, u32[]{:S(2)}) collective-permute-start(f32[40,384]{1,0:T(8,128)S(1)} %concatenate.120), channel_id=1, source_target_pairs={{0,0},{1,1},{2,8},{3,9},{4,4},{5,5},{6,12},{7,13},{8,2},{9,3},{10,... | collective-permute-start | bytes 184328 | tf_op jit(solution)/shard_map/ppermute | solution.py:941
  43.2 3.4 collective-permute-start.6
  46.6 53.4 %copy-start.24 = (bf16[48,1536]{1,0:T(8,128)(2,1)}, bf16[48,1536]{1,0:T(8,128)(2,1)S(1)}, u32[]{:S(2)}) copy-start(bf16[48,1536]{1,0:T(8,128)(2,1)S(1)} %maximum_select_fusion.4) | copy-start | bytes 442372
  48.0 35.4 %copy-start.25 = (bf16[384,384]{1,0:T(8,128)(2,1)S(1)}, bf16[384,384]{1,0:T(8,128)(2,1)}, u32[]{:S(2)}) copy-start(bf16[384,384]{1,0:T(8,128)(2,1)} %param.39) | copy-start | bytes 884740
  48.1 103.0 %all-gather.5.cloned.1.call-start = ((), (), s32[]{:S(2)}) async-start(), calls=%async_computation.2 | async-start | bytes 7077888 | tf_op jit(solution)/shard_map/all_gather | solution.py:1193
  48.1 13.0 %collective-permute-start.9 = (bf16[384,384]{1,0:T(8,128)(2,1)S(1)}, bf16[384,384]{1,0:T(8,128)(2,1)S(1)}, u32[]{:S(2)}, u32[]{:S(2)}) collective-permute-start(bf16[384,384]{1,0:T(8,128)(2,1)S(1)} %copy-done.45), channel_id=1, source_target_pairs={{0,2},{1,3},{2,10},{3,11},{4,6},{5,7},{6,14},{7,15},{8,0},{9,1},{1... | collective-permute-start | bytes 884744 | tf_op jit(solution)/shard_map/ppermute | solution.py:941
  48.2 14.1 %collective-permute-start.8 = (bf16[384,384]{1,0:T(8,128)(2,1)S(1)}, bf16[384,384]{1,0:T(8,128)(2,1)S(1)}, u32[]{:S(2)}, u32[]{:S(2)}) collective-permute-start(bf16[384,384]{1,0:T(8,128)(2,1)S(1)} %copy-done.45), channel_id=1, source_target_pairs={{0,0},{1,1},{2,8},{3,9},{4,4},{5,5},{6,12},{7,13},{8,2},{9,3},{10,... | collective-permute-start | bytes 884744 | tf_op jit(solution)/shard_map/ppermute | solution.py:941
  62.3 11.3 %collective-permute-start.10 = (bf16[64,1536]{1,0:T(8,128)(2,1)S(1)}, bf16[64,1536]{1,0:T(8,128)(2,1)S(1)}, u32[]{:S(2)}, u32[]{:S(2)}) collective-permute-start(bf16[64,1536]{1,0:T(8,128)(2,1)S(1)} %get-tuple-element.154), channel_id=1, source_target_pairs={{0,0},{1,1},{2,8},{3,9},{4,4},{5,5},{6,12},{7,13},{8,2},{9,3},{10,... | collective-permute-start | bytes 589832 | tf_op jit(solution)/shard_map/ppermute | solution.py:941
  64.2 9.4 %collective-permute-start.11 = (bf16[64,1536]{1,0:T(8,128)(2,1)S(1)}, bf16[64,1536]{1,0:T(8,128)(2,1)S(1)}, u32[]{:S(2)}, u32[]{:S(2)}) collective-permute-start(bf16[64,1536]{1,0:T(8,128)(2,1)S(1)} %get-tuple-element.155), channel_id=1, source_target_pairs={{0,2},{1,3},{2,10},{3,11},{4,6},{5,7},{6,14},{7,15},{8,0},{9,1},{1... | collective-permute-start | bytes 589832 | tf_op jit(solution)/shard_map/ppermute | solution.py:941
  64.3 17.9 %collective-permute-start.12 = (bf16[64,1536]{1,0:T(8,128)(2,1)S(1)}, bf16[64,1536]{1,0:T(8,128)(2,1)S(1)}, u32[]{:S(2)}, u32[]{:S(2)}) collective-permute-start(bf16[64,1536]{1,0:T(8,128)(2,1)S(1)} %get-tuple-element.156), channel_id=1, source_target_pairs={{0,16},{1,17},{2,24},{3,25},{4,20},{5,21},{6,28},{7,29},{8,18},{9,... | collective-permute-start | bytes 589832 | tf_op jit(solution)/shard_map/ppermute | solution.py:941
  68.1 14.0 %collective-permute-start.13 = (bf16[64,1536]{1,0:T(8,128)(2,1)S(1)}, bf16[64,1536]{1,0:T(8,128)(2,1)S(1)}, u32[]{:S(2)}, u32[]{:S(2)}) collective-permute-start(bf16[64,1536]{1,0:T(8,128)(2,1)S(1)} %get-tuple-element.157), channel_id=1, source_target_pairs={{0,18},{1,19},{2,26},{3,27},{4,22},{5,23},{6,30},{7,31},{8,16},{9,... | collective-permute-start | bytes 589832 | tf_op jit(solution)/shard_map/ppermute | solution.py:941
  83.4 223.7 %reduce-scatter.2.cloned.1.call-start = ((), (), s32[]{:S(2)}) async-start(), calls=%async_computation.1 | async-start | bytes 7077888 | tf_op jit(solution)/shard_map/reduce_scatter | solution.py:1228
  83.9 16.1 %collective-permute-start.16 = (bf16[768,384]{1,0:T(8,128)(2,1)S(1)}, bf16[768,384]{1,0:T(8,128)(2,1)S(1)}, u32[]{:S(2)}, u32[]{:S(2)}) collective-permute-start(bf16[768,384]{1,0:T(8,128)(2,1)S(1)} %maximum_select_fusion.3), channel_id=1, source_target_pairs={{0,16},{1,17},{2,18},{3,19},{4,20},{5,21},{6,22},{7,23},{8,24},{9,... | collective-permute-start | bytes 1769480 | tf_op jit(solution)/shard_map/ppermute | solution.py:941
  87.1 14.4 %collective-permute-start.15 = (bf16[2,384,384]{2,1,0:T(8,128)(2,1)S(1)}, bf16[2,384,384]{2,1,0:T(8,128)(2,1)S(1)}, u32[]{:S(2)}, u32[]{:S(2)}) collective-permute-start(bf16[2,384,384]{2,1,0:T(8,128)(2,1)S(1)} %pad_maximum_fusion.1), channel_id=1, source_target_pairs={{0,2},{1,3},{2,10},{3,11},{4,6},{5,7},{6,14},{7,15},{8,0},{9,1},{1... | collective-permute-start | bytes 1769480 | tf_op jit(solution)/shard_map/ppermute | solution.py:941
  90.4 25.3 %collective-permute-start.14 = (bf16[2,384,384]{2,1,0:T(8,128)(2,1)S(1)}, bf16[2,384,384]{2,1,0:T(8,128)(2,1)S(1)}, u32[]{:S(2)}, u32[]{:S(2)}) collective-permute-start(bf16[2,384,384]{2,1,0:T(8,128)(2,1)S(1)} %pad_maximum_fusion.1), channel_id=1, source_target_pairs={{0,0},{1,1},{2,8},{3,9},{4,4},{5,5},{6,12},{7,13},{8,2},{9,3},{10,... | collective-permute-start | bytes 1769480 | tf_op jit(solution)/shard_map/ppermute | solution.py:941
  119.1 28.7 %collective-permute-start.17 = (bf16[2,768,384]{2,1,0:T(8,128)(2,1)S(1)}, bf16[2,768,384]{2,1,0:T(8,128)(2,1)S(1)}, u32[]{:S(2)}, u32[]{:S(2)}) collective-permute-start(bf16[2,768,384]{2,1,0:T(8,128)(2,1)S(1)} %maximum_select_fusion.2), channel_id=1, source_target_pairs={{0,16},{1,17},{2,18},{3,19},{4,20},{5,21},{6,22},{7,23},{8,24},{9,... | collective-permute-start | bytes 3538952 | tf_op jit(solution)/shard_map/ppermute | solution.py:941
  173.2 1.4 collective-permute-start.18
  175.4 6.6 %collective-permute-start.19 = (f32[8,2048]{1,0:T(8,128)S(1)}, f32[8,2048]{1,0:T(8,128)S(1)}, u32[]{:S(2)}, u32[]{:S(2)}) collective-permute-start(f32[8,2048]{1,0:T(8,128)S(1)} %add.243), channel_id=1, source_target_pairs={{0,1},{1,0},{2,3},{3,2},{4,5},{5,4},{6,7},{7,6},{8,9},{9,8},{10,11... | collective-permute-start | bytes 196616 | tf_op jit(solution)/shard_map/ppermute | solution.py:941
  182.0 3.4 collective-permute-start.20
  207.9 28.6 %collective-permute-start.21 = (bf16[2,768,384]{1,2,0:T(8,128)(2,1)}, bf16[2,768,384]{1,2,0:T(8,128)(2,1)S(1)}, u32[]{:S(2)}, u32[]{:S(2)}) collective-permute-start(bf16[2,768,384]{1,2,0:T(8,128)(2,1)} %pad_maximum_fusion), channel_id=1, source_target_pairs={{0,16},{1,17},{2,18},{3,19},{4,20},{5,21},{6,22},{7,23},{8,24},{9,... | collective-permute-start | bytes 3538952 | tf_op jit(solution)/shard_map/ppermute | solution.py:941
  233.5 38.2 %collective-permute-start.22 = (bf16[2,2,128,1536]{3,2,1,0:T(8,128)(2,1)}, bf16[2,2,128,1536]{3,2,1,0:T(8,128)(2,1)}, u32[]{:S(2)}, u32[]{:S(2)}) collective-permute-start(bf16[2,2,128,1536]{3,2,1,0:T(8,128)(2,1)} %get-tuple-element.195), channel_id=1, source_target_pairs={{0,8},{1,9},{2,10},{3,11},{4,12},{5,13},{6,14},{7,15},{8,0},{9,1},... | collective-permute-start | bytes 4718600 | tf_op jit(solution)/shard_map/ppermute | solution.py:941
  237.1 30.3 %collective-permute-start.23 = (bf16[768,384]{0,1:T(8,128)(2,1)S(1)}, bf16[768,384]{0,1:T(8,128)(2,1)S(1)}, u32[]{:S(2)}, u32[]{:S(2)}) collective-permute-start(bf16[768,384]{0,1:T(8,128)(2,1)S(1)} %pad_maximum_fusion.2), channel_id=1, source_target_pairs={{0,0},{1,1},{8,2},{9,3},{4,4},{5,5},{12,6},{13,7},{2,8},{3,9},{10,... | collective-permute-start | bytes 1769480 | tf_op jit(solution)/shard_map/ppermute | solution.py:941
  243.6 23.8 %collective-permute-start.24 = (bf16[768,384]{0,1:T(8,128)(2,1)S(1)}, bf16[768,384]{0,1:T(8,128)(2,1)S(1)}, u32[]{:S(2)}, u32[]{:S(2)}) collective-permute-start(bf16[768,384]{0,1:T(8,128)(2,1)S(1)} %pad_maximum_fusion.3), channel_id=1, source_target_pairs={{2,0},{3,1},{10,2},{11,3},{6,4},{7,5},{14,6},{15,7},{0,8},{1,9},{8... | collective-permute-start | bytes 1769480 | tf_op jit(solution)/shard_map/ppermute | solution.py:941
  269.0 5.9 %collective-permute-start.25 = (bf16[2,2,128,1536]{3,2,1,0:T(8,128)(2,1)}, bf16[2,2,128,1536]{3,2,1,0:T(8,128)(2,1)S(1)}, u32[]{:S(2)}, u32[]{:S(2)}) collective-permute-start(bf16[2,2,128,1536]{3,2,1,0:T(8,128)(2,1)} %get-tuple-element.200), channel_id=1, source_target_pairs={{0,8},{1,9},{2,10},{3,11},{4,12},{5,13},{6,14},{7,15},{8,0},{9,1},... | collective-permute-start | bytes 4718600 | tf_op jit(solution)/shard_map/ppermute | solution.py:941
  281.8 19.0 %collective-permute-start.26 = (bf16[2,128,1536]{2,1,0:T(8,128)(2,1)}, bf16[2,128,1536]{2,1,0:T(8,128)(2,1)S(1)}, u32[]{:S(2)}, u32[]{:S(2)}) collective-permute-start(bf16[2,128,1536]{2,1,0:T(8,128)(2,1)} %get-tuple-element.208), channel_id=1, source_target_pairs={{0,1},{1,0},{2,3},{3,2},{4,5},{5,4},{6,7},{7,6},{8,9},{9,8},{10,11... | collective-permute-start | bytes 2359304 | tf_op jit(solution)/shard_map/ppermute | solution.py:941
  281.9 19.0 %collective-permute-start.27 = (bf16[2,128,1536]{2,1,0:T(8,128)(2,1)}, bf16[2,128,1536]{2,1,0:T(8,128)(2,1)S(1)}, u32[]{:S(2)}, u32[]{:S(2)}) collective-permute-start(bf16[2,128,1536]{2,1,0:T(8,128)(2,1)} %get-tuple-element.210), channel_id=1, source_target_pairs={{0,4},{1,5},{2,6},{3,7},{4,0},{5,1},{6,2},{7,3},{8,12},{9,13},{10,... | collective-permute-start | bytes 2359304 | tf_op jit(solution)/shard_map/ppermute | solution.py:941
  301.8 5.2 %collective-permute-start.28 = (bf16[144,1536]{1,0:T(8,128)(2,1)S(1)}, bf16[144,1536]{1,0:T(8,128)(2,1)}, u32[]{:S(2)}, u32[]{:S(2)}) collective-permute-start(bf16[144,1536]{1,0:T(8,128)(2,1)S(1)} %pad_maximum_fusion.4), channel_id=1, source_target_pairs={{0,8},{1,9},{2,10},{3,11},{4,12},{5,13},{6,14},{7,15},{8,0},{9,1},... | collective-permute-start | bytes 1327112 | tf_op jit(solution)/shard_map/ppermute | solution.py:941
  309.2 7.6 %collective-permute-start.29 = (bf16[80,1536]{1,0:T(8,128)(2,1)S(1)}, bf16[80,1536]{1,0:T(8,128)(2,1)}, u32[]{:S(2)}, u32[]{:S(2)}) collective-permute-start(bf16[80,1536]{1,0:T(8,128)(2,1)S(1)} %pad_maximum_fusion.5), channel_id=1, source_target_pairs={{0,1},{1,0},{2,3},{3,2},{4,5},{5,4},{6,7},{7,6},{8,9},{9,8},{10,11... | collective-permute-start | bytes 737288 | tf_op jit(solution)/shard_map/ppermute | solution.py:941
  311.3 23.5 %collective-permute-start.44 = (bf16[2,384,384]{2,1,0:T(8,128)(2,1)}, bf16[2,384,384]{2,1,0:T(8,128)(2,1)S(1)}, u32[]{:S(2)}, u32[]{:S(2)}) collective-permute-start(bf16[2,384,384]{2,1,0:T(8,128)(2,1)} %get-tuple-element.262), channel_id=1, source_target_pairs={{0,16},{1,17},{2,18},{3,19},{4,20},{5,21},{6,22},{7,23},{8,24},{9,... | collective-permute-start | bytes 1769480 | tf_op jit(solution)/shard_map/ppermute | solution.py:941
  311.4 9.8 %collective-permute-start.30 = (bf16[128,1536]{1,0:T(8,128)(2,1)}, bf16[128,1536]{1,0:T(8,128)(2,1)S(1)}, u32[]{:S(2)}, u32[]{:S(2)}) collective-permute-start(bf16[128,1536]{1,0:T(8,128)(2,1)} %get-tuple-element.226), channel_id=1, source_target_pairs={{0,4},{1,5},{2,6},{3,7},{4,0},{5,1},{6,2},{7,3},{8,12},{9,13},{10,... | collective-permute-start | bytes 1179656 | tf_op jit(solution)/shard_map/ppermute | solution.py:941
  312.6 12.5 %collective-permute-start.31 = (bf16[128,1536]{1,0:T(8,128)(2,1)}, bf16[128,1536]{1,0:T(8,128)(2,1)S(1)}, u32[]{:S(2)}, u32[]{:S(2)}) collective-permute-start(bf16[128,1536]{1,0:T(8,128)(2,1)} %get-tuple-element.228), channel_id=1, source_target_pairs={{0,1},{1,0},{2,3},{3,2},{4,5},{5,4},{6,7},{7,6},{8,9},{9,8},{10,11... | collective-permute-start | bytes 1179656 | tf_op jit(solution)/shard_map/ppermute | solution.py:941
  318.6 17.1 %copy-start.21 = (bf16[768,384]{0,1:T(8,128)(2,1)S(1)}, bf16[768,384]{0,1:T(8,128)(2,1)}, u32[]{:S(2)}) copy-start(bf16[768,384]{0,1:T(8,128)(2,1)} %copy-done.20) | copy-start | bytes 1769476
  318.6 17.0 %copy-start.23 = (bf16[768,384]{0,1:T(8,128)(2,1)S(1)}, bf16[768,384]{0,1:T(8,128)(2,1)}, u32[]{:S(2)}) copy-start(bf16[768,384]{0,1:T(8,128)(2,1)} %copy-done.22) | copy-start | bytes 1769476
  328.4 10.2 %collective-permute-start.40 = (bf16[48,1536]{1,0:T(8,128)(2,1)S(1)}, bf16[48,1536]{1,0:T(8,128)(2,1)S(1)}, u32[]{:S(2)}, u32[]{:S(2)}) collective-permute-start(bf16[48,1536]{1,0:T(8,128)(2,1)S(1)} %pad_maximum_fusion.6), channel_id=1, source_target_pairs={{0,4},{1,5},{2,6},{3,7},{4,0},{5,1},{6,2},{7,3},{8,12},{9,13},{10,... | collective-permute-start | bytes 442376 | tf_op jit(solution)/shard_map/ppermute | solution.py:941
  329.4 18.7 %collective-permute-start.36 = (bf16[64,1536]{1,0:T(8,128)(2,1)S(1)}, bf16[64,1536]{1,0:T(8,128)(2,1)S(1)}, u32[]{:S(2)}, u32[]{:S(2)}) collective-permute-start(bf16[64,1536]{1,0:T(8,128)(2,1)S(1)} %get-tuple-element.246), channel_id=1, source_target_pairs={{0,0},{1,1},{8,2},{9,3},{4,4},{5,5},{12,6},{13,7},{2,8},{3,9},{10,... | collective-permute-start | bytes 589832 | tf_op jit(solution)/shard_map/ppermute | solution.py:941
  334.2 13.9 %collective-permute-start.37 = (bf16[64,1536]{1,0:T(8,128)(2,1)S(1)}, bf16[64,1536]{1,0:T(8,128)(2,1)S(1)}, u32[]{:S(2)}, u32[]{:S(2)}) collective-permute-start(bf16[64,1536]{1,0:T(8,128)(2,1)S(1)} %get-tuple-element.247), channel_id=1, source_target_pairs={{2,0},{3,1},{10,2},{11,3},{6,4},{7,5},{14,6},{15,7},{0,8},{1,9},{8... | collective-permute-start | bytes 589832 | tf_op jit(solution)/shard_map/ppermute | solution.py:941
  334.3 18.4 %collective-permute-start.38 = (bf16[64,1536]{1,0:T(8,128)(2,1)}, bf16[64,1536]{1,0:T(8,128)(2,1)S(1)}, u32[]{:S(2)}, u32[]{:S(2)}) collective-permute-start(bf16[64,1536]{1,0:T(8,128)(2,1)} %get-tuple-element.248), channel_id=1, source_target_pairs={{16,0},{17,1},{24,2},{25,3},{20,4},{21,5},{28,6},{29,7},{18,8},{19... | collective-permute-start | bytes 589832 | tf_op jit(solution)/shard_map/ppermute | solution.py:941
  334.8 17.9 %collective-permute-start.39 = (bf16[64,1536]{1,0:T(8,128)(2,1)}, bf16[64,1536]{1,0:T(8,128)(2,1)S(1)}, u32[]{:S(2)}, u32[]{:S(2)}) collective-permute-start(bf16[64,1536]{1,0:T(8,128)(2,1)} %get-tuple-element.249), channel_id=1, source_target_pairs={{18,0},{19,1},{26,2},{27,3},{22,4},{23,5},{30,6},{31,7},{16,8},{17... | collective-permute-start | bytes 589832 | tf_op jit(solution)/shard_map/ppermute | solution.py:941
  338.7 22.1 %collective-permute-start.32 = (bf16[64,1536]{1,0:T(8,128)(2,1)S(1)}, bf16[64,1536]{1,0:T(8,128)(2,1)S(1)}, u32[]{:S(2)}, u32[]{:S(2)}) collective-permute-start(bf16[64,1536]{1,0:T(8,128)(2,1)S(1)} %get-tuple-element.242), channel_id=1, source_target_pairs={{0,0},{1,1},{8,2},{9,3},{4,4},{5,5},{12,6},{13,7},{2,8},{3,9},{10,... | collective-permute-start | bytes 589832 | tf_op jit(solution)/shard_map/ppermute | solution.py:941
  348.1 15.7 %collective-permute-start.33 = (bf16[64,1536]{1,0:T(8,128)(2,1)S(1)}, bf16[64,1536]{1,0:T(8,128)(2,1)S(1)}, u32[]{:S(2)}, u32[]{:S(2)}) collective-permute-start(bf16[64,1536]{1,0:T(8,128)(2,1)S(1)} %get-tuple-element.243), channel_id=1, source_target_pairs={{2,0},{3,1},{10,2},{11,3},{6,4},{7,5},{14,6},{15,7},{0,8},{1,9},{8... | collective-permute-start | bytes 589832 | tf_op jit(solution)/shard_map/ppermute | solution.py:941
  348.1 19.4 %collective-permute-start.34 = (bf16[64,1536]{1,0:T(8,128)(2,1)S(1)}, bf16[64,1536]{1,0:T(8,128)(2,1)S(1)}, u32[]{:S(2)}, u32[]{:S(2)}) collective-permute-start(bf16[64,1536]{1,0:T(8,128)(2,1)S(1)} %get-tuple-element.244), channel_id=1, source_target_pairs={{16,0},{17,1},{24,2},{25,3},{20,4},{21,5},{28,6},{29,7},{18,8},{19... | collective-permute-start | bytes 589832 | tf_op jit(solution)/shard_map/ppermute | solution.py:941
  352.7 14.7 %collective-permute-start.35 = (bf16[64,1536]{1,0:T(8,128)(2,1)S(1)}, bf16[64,1536]{1,0:T(8,128)(2,1)S(1)}, u32[]{:S(2)}, u32[]{:S(2)}) collective-permute-start(bf16[64,1536]{1,0:T(8,128)(2,1)S(1)} %get-tuple-element.245), channel_id=1, source_target_pairs={{18,0},{19,1},{26,2},{27,3},{22,4},{23,5},{30,6},{31,7},{16,8},{17... | collective-permute-start | bytes 589832 | tf_op jit(solution)/shard_map/ppermute | solution.py:941
  352.8 16.0 %collective-permute-start.41 = (bf16[2,80,384]{2,1,0:T(8,128)(2,1)S(1)}, bf16[2,80,384]{2,1,0:T(8,128)(2,1)}, u32[]{:S(2)}, u32[]{:S(2)}) collective-permute-start(bf16[2,80,384]{2,1,0:T(8,128)(2,1)S(1)} %pad_maximum_fusion.7), channel_id=1, source_target_pairs={{0,16},{1,17},{2,18},{3,19},{4,20},{5,21},{6,22},{7,23},{8,24},{9,... | collective-permute-start | bytes 368648 | tf_op jit(solution)/shard_map/ppermute | solution.py:941
  360.8 17.9 %collective-permute-start.45 = (bf16[384,384]{1,0:T(8,128)(2,1)S(1)}, bf16[384,384]{1,0:T(8,128)(2,1)S(1)}, u32[]{:S(2)}, u32[]{:S(2)}) collective-permute-start(bf16[384,384]{1,0:T(8,128)(2,1)S(1)} %copy-done.28), channel_id=1, source_target_pairs={{0,0},{1,1},{8,2},{9,3},{4,4},{5,5},{12,6},{13,7},{2,8},{3,9},{10,... | collective-permute-start | bytes 884744 | tf_op jit(solution)/shard_map/ppermute | solution.py:941
  363.9 14.8 %collective-permute-start.46 = (bf16[384,384]{1,0:T(8,128)(2,1)S(1)}, bf16[384,384]{1,0:T(8,128)(2,1)S(1)}, u32[]{:S(2)}, u32[]{:S(2)}) collective-permute-start(bf16[384,384]{1,0:T(8,128)(2,1)S(1)} %copy-done.27), channel_id=1, source_target_pairs={{2,0},{3,1},{10,2},{11,3},{6,4},{7,5},{14,6},{15,7},{0,8},{1,9},{8... | collective-permute-start | bytes 884744 | tf_op jit(solution)/shard_map/ppermute | solution.py:941
  368.8 18.6 %copy-start.32 = (bf16[1536]{0:T(1024)(128)(2,1)S(1)}, bf16[1536]{0:T(1024)(128)(2,1)}, u32[]{:S(2)}) copy-start(bf16[1536]{0:T(1024)(128)(2,1)} %param.26) | copy-start | bytes 9220
  370.5 12.0 %collective-permute-start.42 = (bf16[80,384]{1,0:T(8,128)(2,1)S(1)}, bf16[80,384]{1,0:T(8,128)(2,1)S(1)}, u32[]{:S(2)}, u32[]{:S(2)}) collective-permute-start(bf16[80,384]{1,0:T(8,128)(2,1)S(1)} %get-tuple-element.255), channel_id=1, source_target_pairs={{0,0},{1,1},{8,2},{9,3},{4,4},{5,5},{12,6},{13,7},{2,8},{3,9},{10,... | collective-permute-start | bytes 184328 | tf_op jit(solution)/shard_map/ppermute | solution.py:941
  373.9 8.6 %collective-permute-start.43 = (bf16[80,384]{1,0:T(8,128)(2,1)S(1)}, bf16[80,384]{1,0:T(8,128)(2,1)S(1)}, u32[]{:S(2)}, u32[]{:S(2)}) collective-permute-start(bf16[80,384]{1,0:T(8,128)(2,1)S(1)} %get-tuple-element.256), channel_id=1, source_target_pairs={{2,0},{3,1},{10,2},{11,3},{6,4},{7,5},{14,6},{15,7},{0,8},{1,9},{8... | collective-permute-start | bytes 184328 | tf_op jit(solution)/shard_map/ppermute | solution.py:941
  (38 other events, 239.9 us)
Sparse Core Ops, SparseCore 0:
  48.2 63.6 all-gather.6
  114.1 36.9 all-gather.4
  172.5 72.7 reduce-scatter.1
